TPU v7x, 32 devices: a whole 2x2x4 slice. The times are simulated.
32 devices in a mesh: pipe: 2 (over core), seq: 4 (over y, x), dp: 4 (over z).
Axes of the slice: x: 2, y: 2, z: 4, core: 2. Of those that a mesh axis runs over, the one named last changes fastest.
Arguments:
- encoded: bfloat16 [4, 256, 4096], P('dp', 'seq'), may hold values from -6 to 6
- sent_forward: bfloat16 [2, 4, 256, 4096], P('pipe', 'dp', 'seq'), may hold values from -6 to 6
- head_cotangent: bfloat16 [4, 256, 4096], P('dp', 'seq'), may hold values from -6 to 6
- grad_sent: bfloat16 [2, 4, 256, 4096], P('pipe', 'dp', 'seq'), may hold values from -6 to 6
- x_saved: bfloat16 [2, 4, 256, 4096], P('pipe', 'dp', 'seq'), may hold values from -6 to 6
- q_saved: bfloat16 [2, 4, 256, 2048], P('pipe', 'dp', None, 'seq'), may hold values from -6 to 6
- k_saved: bfloat16 [2, 4, 256, 2048], P('pipe', 'dp', None, 'seq'), may hold values from -6 to 6
- v_saved: bfloat16 [2, 4, 256, 2048], P('pipe', 'dp', None, 'seq'), may hold values from -6 to 6
- norm_gain: float32 [2, 4096], P('pipe'), may hold values from 0.25 to 1.75
- logit_scale: float32 [2, 16], P('pipe', 'seq'), may hold values from 0.25 to 48
- w_query: bfloat16 [2, 4096, 2048], P('pipe', None, 'seq'), may hold values from -0.09375 to 0.09375
- w_key: bfloat16 [2, 4096, 2048], P('pipe', None, 'seq'), may hold values from -0.09375 to 0.09375
- w_value: bfloat16 [2, 4096, 2048], P('pipe', None, 'seq'), may hold values from -0.09375 to 0.09375
- w_out: bfloat16 [2, 2048, 4096], P('pipe', 'seq'), may hold values from -0.5 to 0.5
- key_blocks: int32 [4, 2, 2], P('dp'), may hold values from 0 to 1, as said below
- key_counts: int32 [4, 2], P('dp'), may hold values from 1 to 2, as said below
Outputs:
- forward_out: bfloat16 [2, 4, 256, 4096], P('pipe', 'dp', 'seq')
- back_out: bfloat16 [2, 4, 256, 4096], P('pipe', 'dp', 'seq')
- grad_query: bfloat16 [2, 4096, 2048], P('pipe', 'dp', 'seq')
- grad_key: bfloat16 [2, 4096, 2048], P('pipe', 'dp', 'seq')
- grad_value: bfloat16 [2, 4096, 2048], P('pipe', 'dp', 'seq')
- grad_out_proj: bfloat16 [2, 2048, 4096], P('pipe', 'seq', 'dp')
- grad_gain: float32 [2, 4096], P('pipe')
Inputs may be any that keep to these rules, and one draw needn't show every extreme that they name: `key_blocks`: for each sample and query block i, the first key_counts entries of its list are different block numbers and the first is i itself; entries after them are block numbers that are not used. `key_counts`: in every sample some query block uses all 2 slots.
All inputs are finite; a program needn't handle non-finite values.
Results may differ from a plain program's by a relative error of at most 0.025.
The roundings to bfloat16 on the way count: a program that leaves them out, or rounds other values in their place, can miss the bound.
Values may be sent and summed in bfloat16 or wider, within the bound.
No kernel may reach another device: no remote copies, remote signals or barrier semaphores. Data moves between devices by JAX's collectives and lax.ppermute only.
A program may use at most 128 MiB of HBM per device.

v0:
```python
import math

import jax
import jax.numpy as jnp
from jax import lax
from jax.sharding import PartitionSpec as P

HD = 128
BLOCK = 128


epsilon = 1e-05


def passed_along(value, axis, by):
    devices = lax.axis_size(axis)
    pairs = [(i, i + by) for i in range(devices) if 0 <= i + by < devices]
    return lax.ppermute(value, axis, pairs)


def normalize(rows_in, gain_row):
    widened = rows_in.astype(jnp.float32)
    inverse_rms = lax.rsqrt(jnp.mean(widened * widened, axis=-1, keepdims=True) + epsilon)
    unit_rows = widened * inverse_rms
    return ((unit_rows * gain_row).astype(jnp.bfloat16), inverse_rms, unit_rows)


def gather_sets(tensor, block_ids):
    block_count, slot_count = block_ids.shape
    blocks = tensor.reshape(block_count, BLOCK, tensor.shape[1], tensor.shape[2])
    return blocks[block_ids].reshape(
        block_count, slot_count * BLOCK, tensor.shape[1], tensor.shape[2]
    )


def attention_parts(queries, key_rows, value_rows, factor, block_ids, counts):
    block_count, slot_count = block_ids.shape
    head_count, head_width = (queries.shape[1], queries.shape[2])
    query_blocks = queries.reshape(block_count, BLOCK, head_count, head_width)
    live_slots = jnp.arange(slot_count, dtype=jnp.int32)[None, :] < counts[:, None]
    choose = (
        block_ids[:, :, None] == jnp.arange(block_count, dtype=jnp.int32)[None, None, :]
    ) & live_slots[:, :, None]
    key_sets = gather_sets(key_rows, block_ids)
    value_sets = gather_sets(value_rows, block_ids)
    allowed = jnp.repeat(live_slots, BLOCK, axis=1)
    scores = jnp.einsum(
        "qihd,qjhd->qhij", query_blocks, key_sets, preferred_element_type=jnp.float32
    )
    scores = scores * factor[None, :, None, None]
    scores = jnp.where(allowed[:, None, None, :], scores, -1e30)
    row_max = jnp.max(scores, axis=-1, keepdims=True)
    lifted = jnp.exp(scores - row_max)
    soft = lifted / jnp.sum(lifted, axis=-1, keepdims=True)
    rounded = soft.astype(jnp.bfloat16)
    attended = jnp.einsum(
        "qhij,qjhd->qihd", rounded, value_sets, preferred_element_type=jnp.float32
    )
    return (
        soft,
        rounded,
        attended.astype(jnp.bfloat16),
        query_blocks,
        key_sets,
        value_sets,
        choose,
    )


def attention_grads(parts, grad_attended, factor):
    soft, rounded, attended, query_blocks, key_sets, value_sets, choose = parts
    block_count, _, head_count, head_width = query_blocks.shape
    seq_len = block_count * BLOCK
    flat_width = head_count * head_width
    cot_blocks = grad_attended.reshape(block_count, BLOCK, head_count, head_width)
    grad_probs = jnp.einsum(
        "qihd,qjhd->qhij", cot_blocks, value_sets, preferred_element_type=jnp.float32
    )
    row_dots = jnp.sum(cot_blocks.astype(jnp.float32) * attended.astype(jnp.float32), axis=-1)
    row_dots = jnp.transpose(row_dots, (0, 2, 1))[..., None]
    grad_scores = (soft * (grad_probs - row_dots) * factor[None, :, None, None]).astype(
        jnp.bfloat16
    )
    slot_count = choose.shape[1]
    query_grads = jnp.einsum(
        "qhij,qjhd->qihd", grad_scores, key_sets, preferred_element_type=jnp.float32
    )
    key_terms = jnp.einsum(
        "qhij,qihd->qjhd", grad_scores, query_blocks, preferred_element_type=jnp.float32
    )
    value_terms = jnp.einsum(
        "qhij,qihd->qjhd", rounded, cot_blocks, preferred_element_type=jnp.float32
    )
    picked = choose.astype(jnp.float32)
    split_shape = (block_count, slot_count, BLOCK, head_count, head_width)
    key_grads = jnp.einsum("qkn,qkjhd->njhd", picked, key_terms.reshape(split_shape))
    value_grads = jnp.einsum("qkn,qkjhd->njhd", picked, value_terms.reshape(split_shape))
    return (
        query_grads.reshape(seq_len, flat_width).astype(jnp.bfloat16),
        key_grads.reshape(seq_len, flat_width).astype(jnp.bfloat16),
        value_grads.reshape(seq_len, flat_width).astype(jnp.bfloat16),
    )


def local(
    encoded,
    sent_forward,
    head_cotangent,
    grad_sent,
    x_saved,
    q_saved,
    k_saved,
    v_saved,
    norm_gain,
    logit_scale,
    w_query,
    w_key,
    w_value,
    w_out,
    key_blocks,
    key_counts,
):
    section_id = lax.axis_index("pipe")
    final_section = lax.axis_size("pipe") - 1
    arrived = passed_along(sent_forward, "pipe", 1)[0, 0]
    section_in = jnp.where(section_id == 0, encoded[0], arrived)
    returned = passed_along(grad_sent, "pipe", -1)[0, 0]
    cot_in = jnp.where(section_id == final_section, head_cotangent[0], returned)
    gain_row = norm_gain[0]
    factor = logit_scale[0] / math.sqrt(HD)
    query_weight, key_weight, value_weight, out_weight = (
        w_query[0],
        w_key[0],
        w_value[0],
        w_out[0],
    )
    block_ids = key_blocks[0]
    counts = key_counts[0]
    model_width = section_in.shape[1]
    slice_width = query_weight.shape[1]
    head_count = slice_width // HD
    normed, _, _ = normalize(section_in, gain_row)
    saved_normed, inverse_rms, unit_rows = normalize(x_saved[0, 0], gain_row)
    segment = lax.all_gather(normed, "seq", axis=0, tiled=True)
    projected = jnp.concatenate(
        [
            jnp.dot(segment, query_weight, preferred_element_type=jnp.float32),
            jnp.dot(segment, key_weight, preferred_element_type=jnp.float32),
            jnp.dot(segment, value_weight, preferred_element_type=jnp.float32),
        ],
        axis=1,
    ).astype(jnp.bfloat16)
    seq_len = projected.shape[0]
    shaped = (seq_len, head_count, HD)
    queries = projected[:, :slice_width].reshape(shaped)
    key_rows = projected[:, slice_width : 2 * slice_width].reshape(shaped)
    value_rows = projected[:, 2 * slice_width :].reshape(shaped)
    attended = attention_parts(queries, key_rows, value_rows, factor, block_ids, counts)[2]
    attended = attended.reshape(seq_len, slice_width)
    row_block = attended
    mixed = lax.psum_scatter(
        jnp.dot(row_block, out_weight, preferred_element_type=jnp.float32).astype(jnp.bfloat16),
        "seq",
        scatter_dimension=0,
        tiled=True,
    ).astype(jnp.float32)
    forward_out = (section_in.astype(jnp.float32) + mixed).astype(jnp.bfloat16)
    saved_parts = attention_parts(
        q_saved[0, 0].reshape(shaped),
        k_saved[0, 0].reshape(shaped),
        v_saved[0, 0].reshape(shaped),
        factor,
        block_ids,
        counts,
    )
    saved_attended = saved_parts[2].reshape(seq_len, slice_width)
    segment = lax.all_gather(cot_in, "seq", axis=0, tiled=True)
    row_block = saved_attended
    weight_total = jnp.einsum("tc,td->cd", row_block, segment, preferred_element_type=jnp.float32)
    fresh = jnp.einsum("td,cd->tc", segment, out_weight, preferred_element_type=jnp.float32).astype(
        jnp.bfloat16
    )
    query_grads, key_grads, value_grads = attention_grads(
        saved_parts, fresh.reshape(shaped), factor
    )
    empty_total = jnp.zeros((model_width, slice_width), jnp.float32)
    totals = (empty_total, empty_total, empty_total)
    segment = lax.all_gather(saved_normed, "seq", axis=0, tiled=True)
    sums_out = []
    for grads, running in zip((query_grads, key_grads, value_grads), totals):
        row_block = grads
        sums_out.append(
            jnp.einsum("td,tc->dc", segment, row_block, preferred_element_type=jnp.float32)
        )
    query_total = sums_out[0]
    key_total = sums_out[1]
    value_total = sums_out[2]
    result = jnp.einsum("tc,dc->td", query_grads, query_weight, preferred_element_type=jnp.float32)
    result = result + jnp.einsum(
        "tc,dc->td", key_grads, key_weight, preferred_element_type=jnp.float32
    )
    grad_normed = lax.psum_scatter(
        (
            result
            + jnp.einsum("tc,dc->td", value_grads, value_weight, preferred_element_type=jnp.float32)
        ).astype(jnp.bfloat16),
        "seq",
        scatter_dimension=0,
        tiled=True,
    ).astype(jnp.float32)
    scaled = gain_row * grad_normed
    back_out = (
        cot_in.astype(jnp.float32)
        + inverse_rms * (scaled - unit_rows * jnp.mean(scaled * unit_rows, axis=-1, keepdims=True))
    ).astype(jnp.bfloat16)
    gain_part = jnp.sum(grad_normed * unit_rows, axis=0)
    grad_gain = lax.psum(gain_part, ("seq", "dp"))
    summed = (
        lax.psum_scatter(
            query_total.astype(jnp.bfloat16), "dp", scatter_dimension=0, tiled=True
        ).astype(jnp.float32),
        lax.psum_scatter(
            key_total.astype(jnp.bfloat16), "dp", scatter_dimension=0, tiled=True
        ).astype(jnp.float32),
        lax.psum_scatter(
            value_total.astype(jnp.bfloat16), "dp", scatter_dimension=0, tiled=True
        ).astype(jnp.float32),
        lax.psum_scatter(
            weight_total.astype(jnp.bfloat16), "dp", scatter_dimension=1, tiled=True
        ).astype(jnp.float32),
    )
    return (
        forward_out[None, None],
        back_out[None, None],
        summed[0].astype(jnp.bfloat16)[None],
        summed[1].astype(jnp.bfloat16)[None],
        summed[2].astype(jnp.bfloat16)[None],
        summed[3].astype(jnp.bfloat16)[None],
        grad_gain[None],
    )


def solution(mesh):
    in_specs = (
        P("dp", "seq", None),
        P("pipe", "dp", "seq", None),
        P("dp", "seq", None),
        P("pipe", "dp", "seq", None),
        P("pipe", "dp", "seq", None),
        P("pipe", "dp", None, "seq"),
        P("pipe", "dp", None, "seq"),
        P("pipe", "dp", None, "seq"),
        P("pipe", None),
        P("pipe", "seq"),
        P("pipe", None, "seq"),
        P("pipe", None, "seq"),
        P("pipe", None, "seq"),
        P("pipe", "seq", None),
        P("dp", None, None),
        P("dp", None),
    )
    out_specs = (
        P("pipe", "dp", "seq", None),
        P("pipe", "dp", "seq", None),
        P("pipe", "dp", "seq"),
        P("pipe", "dp", "seq"),
        P("pipe", "dp", "seq"),
        P("pipe", "seq", "dp"),
        P("pipe", None),
    )
    return jax.shard_map(local, mesh=mesh, in_specs=in_specs, out_specs=out_specs, check_vma=False)
```

profile of v0, /device:TPU:0, one launch (start us, length us, event | category | flops | bytes accessed | tf_op | source)
XLA Modules:
  0.0 552.8 jit_solution(2297217561296470739)
XLA Ops:
  7.2 1.4 collective-permute-start.1
  8.7 2.7 collective-permute-done.1
  11.4 1.9 bitcast_select_fusion
  13.3 0.7 iota_compare_fusion
  14.0 0.1 copy.91
  14.2 0.8 copy.111
  15.0 0.7 compare_select_fusion
  15.6 0.1 reshape.146
  15.7 1.0 reshape_reshape_squeeze.10
  16.7 1.0 reshape_reshape_squeeze.9
  17.8 0.6 gather_fusion.2
  18.7 0.6 gather_fusion.3
  19.4 1.5 fusion.114
  20.8 30.6 %all-gather.6.cloned.1.call-done = bf16[256,4096]{1,0:T(8,128)(2,1)} async-done(((bf16[64,4096]{1,0:T(8,128)(2,1)}), bf16[256,4096]{1,0:T(8,128)(2,1)}) %all-gather.6.cloned.1.call-update) | async-done | bytes 2097168 | tf_op jit(solution)/shard_map/all_gather | solution.py:177
  51.5 4.1 fusion.42
  55.6 0.2 copy.107
  55.8 1.7 convolution_bitcast_fusion
  57.6 2.4 multiply_reduce_fusion
  60.0 0.5 fusion.29
  60.5 0.4 fusion.47
  60.8 0.4 fusion.87
  61.2 1.0 fusion.31
  62.3 0.2 copy.110
  62.5 0.1 reshape.141
  62.6 0.7 copy.117
  63.4 0.9 fusion.32
  64.4 3.6 fusion.9
  68.1 1.3 convolution_add_fusion.1
  69.4 0.9 copy-done.4
  70.2 2.7 fusion.2
  73.0 2.7 collective-permute-start
  75.7 0.2 fusion.54
  75.9 0.6 collective-permute-done
  76.5 1.3 fusion.55
  77.9 30.4 %reduce-scatter.9.cloned.1.call-done = bf16[64,4096]{1,0:T(8,128)(2,1)} async-done(((bf16[256,4096]{1,0:T(8,128)(2,1)}), bf16[64,4096]{1,0:T(8,128)(2,1)}) %reduce-scatter.9.cloned.1.call-update) | async-done | bytes 524304 | tf_op jit(solution)/shard_map/reduce_scatter | solution.py:202
  108.3 2.3 fusion.53
  110.6 2.5 fusion.61
  113.2 0.5 all-gather.8.cloned.1.call-update
  113.7 0.2 reduce-scatter.7.cloned.1.call-start
  114.0 34.7 %all-gather.4.cloned.1.call-done = bf16[256,4096]{1,0:T(8,128)(2,1)} async-done(((bf16[64,4096]{1,0:T(8,128)(2,1)}), bf16[256,4096]{1,0:T(8,128)(2,1)}) %all-gather.4.cloned.1.call-update) | async-done | bytes 2097168 | tf_op jit(solution)/shard_map/all_gather | solution.py:144
  148.6 4.1 fusion.39
  152.8 0.6 gather_fusion.1
  153.5 4.1 fusion.36
  157.7 4.4 fusion.33
  162.2 0.6 gather_fusion
  162.8 0.8 copy.90
  163.7 0.6 fusion.119
  164.2 0.3 fusion.24
  164.6 3.1 fusion.45
  167.7 0.2 copy.97
  167.9 4.8 convolution_convert_fusion.4
  172.9 0.2 copy.119
  173.1 4.8 convolution_convert_fusion
  177.9 8.4 %all-gather.8.cloned.1.call-done = bf16[256,4096]{1,0:T(8,128)(2,1)} async-done(((bf16[64,4096]{1,0:T(8,128)(2,1)}), bf16[256,4096]{1,0:T(8,128)(2,1)}) %all-gather.8.cloned.1.call-update) | async-done | bytes 2097168 | tf_op jit(solution)/shard_map/all_gather | solution.py:188
  186.4 4.8 convolution_convert_fusion.1
  191.3 1.5 copy-done
  192.8 3.2 convolution_convert_fusion.2
  196.1 3.3 convolution_convert_fusion.3
  199.4 78.6 %psum.7 = f32[1,4096]{1,0:T(1,128)} all-reduce(f32[1,4096]{1,0:T(1,128)S(1)} %bitcast.182), channel_id=1, replica_groups=mesh['pipe'=2,'seq'=4,'dp'=4] {'seq','dp'}, use_global_device_ids=true, to_apply=%region_15.16 | all-reduce | flops 4096 | bytes 32768 | tf_op jit(solution)/shard_map/psum | solution.py:217
  278.1 2.0 fusion.60
  280.0 25.6 %reduce-scatter.17.cloned.1.call-done = bf16[512,1024]{1,0:T(8,128)(2,1)} async-done(((bf16[512,4096]{1,0:T(8,128)(2,1)}), bf16[512,1024]{1,0:T(8,128)(2,1)}) %reduce-scatter.17.cloned.1.call-update) | async-done | bytes 1048592 | tf_op jit(solution)/shard_map/reduce_scatter | solution.py:228
  305.7 80.2 %reduce-scatter.15.cloned.1.call-done = bf16[1024,512]{1,0:T(8,128)(2,1)} async-done(((bf16[4096,512]{1,0:T(8,128)(2,1)}), bf16[1024,512]{1,0:T(8,128)(2,1)}) %reduce-scatter.15.cloned.1.call-update) | async-done | bytes 1048592 | tf_op jit(solution)/shard_map/reduce_scatter | solution.py:225
  385.8 80.2 %reduce-scatter.13.cloned.1.call-done = bf16[1024,512]{1,0:T(8,128)(2,1)} async-done(((bf16[4096,512]{1,0:T(8,128)(2,1)}), bf16[1024,512]{1,0:T(8,128)(2,1)}) %reduce-scatter.13.cloned.1.call-update) | async-done | bytes 1048592 | tf_op jit(solution)/shard_map/reduce_scatter | solution.py:222
  466.0 80.3 %reduce-scatter.11.cloned.1.call-done = bf16[1024,512]{1,0:T(8,128)(2,1)} async-done(((bf16[4096,512]{1,0:T(8,128)(2,1)}), bf16[1024,512]{1,0:T(8,128)(2,1)}) %reduce-scatter.11.cloned.1.call-update) | async-done | bytes 1048592 | tf_op jit(solution)/shard_map/reduce_scatter | solution.py:219
  (60 shorter events, 1.4 us)
Async XLA Ops:
  7.2 11.4 %copy-start.6 = (bf16[1,1,256,512]{3,2,1,0:T(8,128)(2,1)S(1)}, bf16[1,1,256,512]{3,2,1,0:T(8,128)(2,1)}, u32[]{:S(2)}) copy-start(bf16[1,1,256,512]{3,2,1,0:T(8,128)(2,1)} %param.23) | copy-start | bytes 786436
  7.2 44.3 %all-gather.6.cloned.1.call-start = ((), (), s32[]{:S(2)}) async-start(), calls=%async_computation.8 | async-start | bytes 2621440 | tf_op jit(solution)/shard_map/all_gather | solution.py:177
  7.2 4.1 collective-permute-start.1
  8.7 10.7 %copy-start.10 = (f32[1,4]{1,0:T(1,128)S(1)}, f32[1,4]{1,0:T(1,128)}, u32[]{:S(2)}) copy-start(f32[1,4]{1,0:T(1,128)} %param.25) | copy-start | bytes 52
  13.3 95.0 %reduce-scatter.9.cloned.1.call-start = ((), (), s32[]{:S(2)}) async-start(), calls=%async_computation.9 | async-start | bytes 2621440 | tf_op jit(solution)/shard_map/reduce_scatter | solution.py:202
  55.8 4.2 copy-start.11
  64.4 3.6 copy-start.3
  68.0 2.2 copy-start.4
  70.2 2.7 copy-start.9
  70.2 5.4 copy-start.2
  70.2 6.3 %copy-start.5 = (bf16[1,64,4096]{2,1,0:T(8,128)(2,1)S(1)}, bf16[1,64,4096]{2,1,0:T(8,128)(2,1)}, u32[]{:S(2)}) copy-start(bf16[1,64,4096]{2,1,0:T(8,128)(2,1)} %param.16) | copy-start | bytes 1572868
  72.9 35.4 %copy-start.8 = (f32[1,4096]{1,0:T(1,128)S(1)}, f32[1,4096]{1,0:T(1,128)}, u32[]{:S(2)}) copy-start(f32[1,4096]{1,0:T(1,128)} %param.24) | copy-start | bytes 49156
  72.9 37.7 %copy-start.1 = (bf16[64,4096]{1,0:T(8,128)(2,1)S(1)}, bf16[64,4096]{1,0:T(8,128)(2,1)}, u32[]{:S(2)}) copy-start(bf16[64,4096]{1,0:T(8,128)(2,1)} %bitcast_select_fusion) | copy-start | bytes 1572868
  72.9 75.7 %all-gather.4.cloned.1.call-start = ((), (), s32[]{:S(2)}) async-start(), calls=%async_computation.6 | async-start | bytes 2621440 | tf_op jit(solution)/shard_map/all_gather | solution.py:144
  73.0 3.5 collective-permute-start
  113.1 73.2 %all-gather.8.cloned.1.call-start = ((), (), s32[]{:S(2)}) async-start(), calls=%async_computation.10 | async-start | bytes 2621440 | tf_op jit(solution)/shard_map/all_gather | solution.py:188
  113.7 164.4 %reduce-scatter.7.cloned.1.call-start = ((), (), s32[]{:S(2)}) async-start(), calls=%async_computation.7 | async-start | bytes 2621440 | tf_op jit(solution)/shard_map/reduce_scatter | solution.py:161
  167.9 4.9 copy-start.7
  172.8 132.9 %reduce-scatter.17.cloned.1.call-start = ((), (), s32[]{:S(2)}) async-start(), calls=%async_computation.14 | async-start | bytes 5242880 | tf_op jit(solution)/shard_map/reduce_scatter | solution.py:228
  177.9 207.9 %reduce-scatter.15.cloned.1.call-start = ((), (), s32[]{:S(2)}) async-start(), calls=%async_computation.13 | async-start | bytes 5242880 | tf_op jit(solution)/shard_map/reduce_scatter | solution.py:225
  191.2 1.6 copy-start
  191.3 274.7 %reduce-scatter.13.cloned.1.call-start = ((), (), s32[]{:S(2)}) async-start(), calls=%async_computation.12 | async-start | bytes 5242880 | tf_op jit(solution)/shard_map/reduce_scatter | solution.py:222
  196.1 350.2 %reduce-scatter.11.cloned.1.call-start = ((), (), s32[]{:S(2)}) async-start(), calls=%async_computation.11 | async-start | bytes 5242880 | tf_op jit(solution)/shard_map/reduce_scatter | solution.py:219
Sparse Core Ops, SparseCore 0:
  13.4 38.0 all-gather.5
  73.0 35.1 reduce-scatter.8
  113.3 35.3 all-gather.3
  151.0 35.2 all-gather.7
  189.5 35.4 reduce-scatter.6
  227.7 77.9 reduce-scatter.16
  308.6 77.1 reduce-scatter.14
  388.7 77.2 reduce-scatter.12
  469.0 77.2 reduce-scatter.10
where the time goes:
time: 554 us; the launch traced here: 553 us
  waiting for transfers between devices  374 us (68%)
  blocking collectives  78.6 us (14%)
  matrix products  58 us (10%)
  between operations  14.3 us (3%)
  other arithmetic  11.6 us (2%)
  local copies, waits for them, and re-layouts  11.3 us (2%)
    reduce_scatter x1, waiting for transfers between devices, local(): lax.psum_scatter(query_total.astype(jnp.bfloat16), 'dp', scatter_dimensio...  80.3 us
    reduce_scatter x1, waiting for transfers between devices, local(): lax.psum_scatter(key_total.astype(jnp.bfloat16), 'dp', scatter_dimension=...  80.2 us
    reduce_scatter x1, waiting for transfers between devices, local(): lax.psum_scatter(value_total.astype(jnp.bfloat16), 'dp', scatter_dimensio...  80.2 us
    psum x1, blocking collectives, local(): grad_gain = lax.psum(gain_part, ('seq', 'dp'))  78.6 us
    all_gather x1, waiting for transfers between devices, local(): segment = lax.all_gather(normed, 'seq', axis=0, tiled=True)  34.7 us
    all_gather x1, waiting for transfers between devices, local(): segment = lax.all_gather(cot_in, 'seq', axis=0, tiled=True)  30.6 us
    reduce_scatter x1, waiting for transfers between devices, local(): lax.psum_scatter((result + jnp.einsum('tc,dc->td', value_grads, value_wei...  30.4 us
    reduce_scatter x1, waiting for transfers between devices, local(): lax.psum_scatter(weight_total.astype(jnp.bfloat16), 'dp', scatter_dimensi...  25.6 us
  transfers between devices with their start and end apart: 11, of which 10 were waited for; matrix products, arithmetic and copies ran while one was open for 9% of the time, Pallas kernels for 0%

commit v1 on v0

v1 whole, which is shorter than its diff:
```python
import functools
import math

import jax
import jax.numpy as jnp
from jax import lax
from jax.experimental import pallas as pl
from jax.experimental.pallas import tpu as pltpu
from jax.sharding import PartitionSpec as P

HD = 128
BLOCK = 128
EPSILON = 1e-05
CHUNK = 512
MIB = 1024 * 1024

BF16 = jnp.bfloat16
F32 = jnp.float32
HBM = pl.BlockSpec(memory_space=pl.ANY)
SMEM = pl.BlockSpec(memory_space=pltpu.SMEM)


def dot_nn(a, b):
    return lax.dot_general(a, b, (((1,), (0,)), ((), ())), preferred_element_type=F32)


def dot_nt(a, b):
    return lax.dot_general(a, b, (((1,), (1,)), ((), ())), preferred_element_type=F32)


def dot_tn(a, b):
    return lax.dot_general(a, b, (((0,), (0,)), ((), ())), preferred_element_type=F32)


def sds(shape, dtype):
    return jax.ShapeDtypeStruct(shape, dtype)


def params(mib, grid=0):
    semantics = ("arbitrary",) * grid if grid else None
    return pltpu.CompilerParams(vmem_limit_bytes=mib * MIB, dimension_semantics=semantics)


def cost(flops, moved):
    return pl.CostEstimate(flops=int(flops), bytes_accessed=int(moved), transcendentals=0)


def run_copies(copies):
    for copy in copies:
        copy.start()
    for copy in copies:
        copy.wait()


def normalized(rows, gain):
    widened = rows.astype(F32)
    inverse = lax.rsqrt(jnp.mean(widened * widened, axis=-1, keepdims=True) + EPSILON)
    unit = widened * inverse
    return unit, inverse, (unit * gain).astype(BF16)


def seen_pairs(blocks_ref, counts_ref, tokens):
    count, slots = blocks_ref.shape
    row_block = lax.broadcasted_iota(jnp.int32, (tokens, tokens), 0) // BLOCK
    col_block = lax.broadcasted_iota(jnp.int32, (tokens, tokens), 1) // BLOCK
    seen = jnp.zeros((tokens, tokens), jnp.int32)
    for i in range(count):
        for j in range(count):
            flag = jnp.int32(0)
            for t in range(slots):
                listed = (t < counts_ref[i]) & (blocks_ref[i, t] == j)
                flag = flag | listed.astype(jnp.int32)
            seen = jnp.where((row_block == i) & (col_block == j), flag, seen)
    return seen


def soft_scores(query, key, factor, seen):
    scores = dot_nt(query, key) * factor
    scores = jnp.where(seen > 0, scores, -1e30)
    lifted = jnp.exp(scores - jnp.max(scores, axis=-1, keepdims=True))
    return lifted / jnp.sum(lifted, axis=-1, keepdims=True)


def pick_kernel(forward_ref, encoded_ref, grad_ref, head_ref, out_f, out_c, sem):
    section = lax.axis_index("pipe")

    def both(first, second):
        run_copies(
            [
                pltpu.make_async_copy(first, out_f, sem.at[0]),
                pltpu.make_async_copy(second, out_c, sem.at[1]),
            ]
        )

    @pl.when(section == 0)
    def _():
        both(forward_ref, head_ref)

    @pl.when(section != 0)
    def _():
        both(encoded_ref, grad_ref)


def pick(sent_forward, encoded, grad_sent, head):
    shape = encoded.shape
    return pl.pallas_call(
        pick_kernel,
        out_shape=(sds(shape, BF16), sds(shape, BF16)),
        in_specs=[HBM] * 4,
        out_specs=(HBM, HBM),
        scratch_shapes=[pltpu.SemaphoreType.DMA((2,))],
        cost_estimate=cost(0, 4 * encoded.size * 2),
        name="pick",
    )(sent_forward, encoded, grad_sent, head)


def columns_kernel(x_ref, cot_ref, gain_ref, *rest):
    outs, held = rest[:-1], rest[-1]
    me = lax.axis_index("dp")
    n = len(outs)
    width = outs[0].shape[-1]
    held[...] = normalized(x_ref[...], gain_ref[...])[2]
    for k, out in enumerate(outs):
        start = pl.multiple_of(lax.rem(me + k, n) * width, width)
        out[0] = held[:, pl.ds(start, width)]
        out[1] = cot_ref[:, pl.ds(start, width)]


def column_parts(x, cot, gain, n):
    rows, width = x.shape
    part = (2, rows, width // n)
    return pl.pallas_call(
        columns_kernel,
        out_shape=tuple(sds(part, BF16) for _ in range(n)),
        scratch_shapes=[pltpu.VMEM((rows, width), BF16)],
        compiler_params=params(16),
        cost_estimate=cost(0, 4 * x.size * 2),
        name="columns",
    )(x, cot, gain)


def saved_kernel(blocks_ref, counts_ref, factor_ref, q_ref, k_ref, v_ref, soft_ref, att_ref):
    tokens, width = q_ref.shape
    seen = seen_pairs(blocks_ref, counts_ref, tokens)
    for h in range(width // HD):
        cols = slice(h * HD, (h + 1) * HD)
        soft = soft_scores(q_ref[:, cols], k_ref[:, cols], factor_ref[0, h], seen)
        soft_ref[h] = soft
        att_ref[:, cols] = dot_nn(soft.astype(BF16), v_ref[:, cols]).astype(BF16)


def saved_attention(blocks, counts, factor, q, k, v):
    tokens, width = q.shape
    heads = width // HD
    return pl.pallas_call(
        saved_kernel,
        out_shape=(sds((heads, tokens, tokens), F32), sds((tokens, width), BF16)),
        in_specs=[SMEM] * 3 + [pl.BlockSpec(memory_space=pltpu.VMEM)] * 3,
        compiler_params=params(24),
        cost_estimate=cost(4 * tokens * tokens * width, 4 * heads * tokens * tokens),
        name="saved_attention",
    )(blocks, counts, factor, q, k, v)


def block_copies(refs, held, rows, sems):
    me = lax.axis_index("seq")
    copies = []
    for j, ref in enumerate(refs):
        at = pl.multiple_of((me ^ j) * rows, rows)
        copies.append(pltpu.make_async_copy(ref, held.at[pl.ds(at, rows)], sems.at[j]))
    return copies


def backward_kernel(
    n, factor_ref, *rest
):
    cots, rest = rest[:n], rest[n:]
    w_ref, soft_ref, att_ref, q_ref, k_ref, v_ref, out_ref, held, total, sems = rest
    step = pl.program_id(0)
    rows = cots[0].shape[0]
    tokens, width = q_ref.shape

    @pl.when(step == 0)
    def _():
        run_copies(block_copies(cots, held, rows, sems))
        total[...] = jnp.zeros_like(total)

    at = pl.multiple_of(step * CHUNK, CHUNK)
    total[...] += dot_nt(held[:, pl.ds(at, CHUNK)], w_ref[...])

    @pl.when(step == pl.num_programs(0) - 1)
    def _():
        for h in range(width // HD):
            cols = slice(h * HD, (h + 1) * HD)
            cot = total[:, cols].astype(BF16)
            soft = soft_ref[h]
            products = cot.astype(F32) * att_ref[:, cols].astype(F32)
            dots = jnp.sum(products, axis=-1, keepdims=True)
            grads = soft * (dot_nt(cot, v_ref[:, cols]) - dots) * factor_ref[0, h]
            grads = grads.astype(BF16)
            low = soft.astype(BF16)
            out_ref[:, h * HD : (h + 1) * HD] = dot_nn(grads, k_ref[:, cols]).astype(BF16)
            key_at = width + h * HD
            out_ref[:, key_at : key_at + HD] = dot_tn(grads, q_ref[:, cols]).astype(BF16)
            value_at = 2 * width + h * HD
            out_ref[:, value_at : value_at + HD] = dot_tn(low, cot).astype(BF16)


def backward_attention(factor, cots, w_out, soft, att, q, k, v):
    tokens, width = q.shape
    model = w_out.shape[1]
    n = len(cots)
    whole = lambda a: pl.BlockSpec(a.shape, lambda i: (0,) * a.ndim)
    return pl.pallas_call(
        functools.partial(backward_kernel, n),
        grid=(model // CHUNK,),
        out_shape=sds((tokens, 3 * width), BF16),
        in_specs=[SMEM]
        + [HBM] * n
        + [pl.BlockSpec((width, CHUNK), lambda i: (0, i))]
        + [whole(a) for a in (soft, att, q, k, v)],
        out_specs=pl.BlockSpec((tokens, 3 * width), lambda i: (0, 0)),
        scratch_shapes=[
            pltpu.VMEM((tokens, model), BF16),
            pltpu.VMEM((tokens, width), F32),
            pltpu.SemaphoreType.DMA((n,)),
        ],
        compiler_params=params(28, 1),
        cost_estimate=cost(2 * tokens * model * width, 2 * w_out.size + 8 * MIB),
        name="backward_attention",
    )(factor, *cots, w_out, soft, att, q, k, v)


def input_grad_kernel(g_ref, wq_ref, wk_ref, wv_ref, *rest):
    outs, held = rest[:-1], rest[-1]
    width = wq_ref.shape[1]
    total = dot_nt(g_ref[:, :width], wq_ref[...])
    total += dot_nt(g_ref[:, width : 2 * width], wk_ref[...])
    total += dot_nt(g_ref[:, 2 * width :], wv_ref[...])
    held[...] = total.astype(BF16)
    rows = outs[0].shape[0]
    me = lax.axis_index("seq")
    for j, out in enumerate(outs):
        out[...] = held[pl.ds(pl.multiple_of((me ^ j) * rows, rows), rows), :]


def input_grads(grads, wq, wk, wv, n):
    tokens = grads.shape[0]
    model, width = wq.shape
    rows = tokens // n
    tile = pl.BlockSpec((CHUNK, width), lambda i: (i, 0))
    return pl.pallas_call(
        input_grad_kernel,
        grid=(model // CHUNK,),
        out_shape=tuple(sds((rows, model), BF16) for _ in range(n)),
        in_specs=[pl.BlockSpec(grads.shape, lambda i: (0, 0)), tile, tile, tile],
        out_specs=tuple(pl.BlockSpec((rows, CHUNK), lambda i: (0, i)) for _ in range(n)),
        scratch_shapes=[pltpu.VMEM((tokens, CHUNK), BF16)],
        compiler_params=params(20, 1),
        cost_estimate=cost(6 * tokens * model * width, 6 * wq.size),
        name="input_grads",
    )(grads, wq, wk, wv)


def forward_kernel(n, blocks_ref, counts_ref, factor_ref, *rest):
    xs, rest = rest[:n], rest[n:]
    gain_ref, wq_ref, wk_ref, wv_ref, wo_ref = rest[:5]
    outs, rest = rest[5 : 5 + n], rest[5 + n :]
    held, wo, tq, tk, tv, att, sems = rest
    step = pl.program_id(0)
    rows = xs[0].shape[0]
    me = lax.axis_index("seq")
    load_wo = pltpu.make_async_copy(wo_ref, wo, sems.at[n])

    @pl.when(step == 0)
    def _():
        copies = block_copies(xs, held, rows, sems)
        for copy in copies:
            copy.start()
        load_wo.start()
        for copy in copies:
            copy.wait()

        @pl.loop(0, held.shape[0] // 32)
        def _(i):
            at = pl.ds(pl.multiple_of(i * 32, 32), 32)
            held[at, :] = normalized(held[at, :], gain_ref[...])[2]

        for total in (tq, tk, tv):
            total[...] = jnp.zeros_like(total)

    part = held[:, pl.ds(pl.multiple_of(step * CHUNK, CHUNK), CHUNK)]
    tq[...] += dot_nn(part, wq_ref[...])
    tk[...] += dot_nn(part, wk_ref[...])
    tv[...] += dot_nn(part, wv_ref[...])

    @pl.when(step == pl.num_programs(0) - 1)
    def _():
        tokens, width = tq.shape
        seen = seen_pairs(blocks_ref, counts_ref, tokens)
        for h in range(width // HD):
            cols = slice(h * HD, (h + 1) * HD)
            query, key, value = (t[:, cols].astype(BF16) for t in (tq, tk, tv))
            soft = soft_scores(query, key, factor_ref[0, h], seen)
            att[:, cols] = dot_nn(soft.astype(BF16), value).astype(BF16)
        load_wo.wait()

        @pl.loop(0, wo.shape[1] // CHUNK)
        def _(i):
            at = pl.ds(pl.multiple_of(i * CHUNK, CHUNK), CHUNK)
            held[:, at] = dot_nn(att[...], wo[:, at]).astype(BF16)

        for j, out in enumerate(outs):
            out[...] = held[pl.ds(pl.multiple_of((me ^ j) * rows, rows), rows), :]


def forward_terms(blocks, counts, factor, xs, gain, wq, wk, wv, wo):
    n = len(xs)
    rows, model = xs[0].shape
    width = wq.shape[1]
    tokens = rows * n
    tile = pl.BlockSpec((CHUNK, width), lambda i: (i, 0))
    return pl.pallas_call(
        functools.partial(forward_kernel, n),
        grid=(model // CHUNK,),
        out_shape=tuple(sds((rows, model), BF16) for _ in range(n)),
        in_specs=[SMEM] * 3
        + [HBM] * n
        + [pl.BlockSpec((1, model), lambda i: (0, 0)), tile, tile, tile, HBM],
        out_specs=tuple(pl.BlockSpec((rows, model), lambda i: (0, 0)) for _ in range(n)),
        scratch_shapes=[
            pltpu.VMEM((tokens, model), BF16),
            pltpu.VMEM((width, model), BF16),
        ]
        + [pltpu.VMEM((tokens, width), F32)] * 3
        + [pltpu.VMEM((tokens, width), BF16), pltpu.SemaphoreType.DMA((n + 1,))],
        compiler_params=params(36, 1),
        cost_estimate=cost(8 * tokens * model * width, 8 * wq.size),
        name="forward_terms",
    )(blocks, counts, factor, *xs, gain, wq, wk, wv, wo)


def back_kernel(n, *rest):
    terms, rest = rest[:n], rest[n:]
    x_ref, cot_ref, gain_ref, back_ref, part_ref = rest
    gain = gain_ref[...]
    unit, inverse, _ = normalized(x_ref[...], gain)
    grad = terms[0][...].astype(F32)
    for term in terms[1:]:
        grad += term[...].astype(F32)
    scaled = gain * grad
    part_ref[...] = jnp.sum(grad * unit, axis=0, keepdims=True)
    inner = jnp.mean(scaled * unit, axis=-1, keepdims=True)
    back_ref[...] = (cot_ref[...].astype(F32) + inverse * (scaled - unit * inner)).astype(BF16)


def back(terms, x, cot, gain):
    return pl.pallas_call(
        functools.partial(back_kernel, len(terms)),
        out_shape=(sds(x.shape, BF16), sds(gain.shape, F32)),
        compiler_params=params(24),
        cost_estimate=cost(0, 7 * x.size * 2),
        name="back",
    )(*terms, x, cot, gain)


def column_copies(parts, which, held, sems):
    me = lax.axis_index("seq")
    copies = []
    for j, part in enumerate(parts):
        rows = part.shape[2]
        at = pl.multiple_of((me ^ j) * rows, rows)
        copies.append(
            pltpu.make_async_copy(part.at[:, which], held.at[:, pl.ds(at, rows)], sems.at[j])
        )
    return copies


def weight_kernel(n_seq, n_dp, *rest):
    parts, rest = rest[:n_seq], rest[n_seq:]
    own, rest = rest[0], rest[1:]
    lower, rest = rest[: n_dp - 1], rest[n_dp - 1 :]
    upper, rest = rest[: n_dp - 1], rest[n_dp - 1 :]
    out_q, out_k, out_v, cols, grads, sems, own_sems = rest
    me = lax.axis_index("dp")

    def grad_copies(k, act):
        if k == 0:
            act(pltpu.make_async_copy(own, grads.at[0], own_sems.at[0]))
            return

        @pl.when(me >= k)
        def _():
            act(pltpu.make_async_copy(lower[k - 1], grads.at[k], own_sems.at[k]))

        @pl.when(me < k)
        def _():
            act(pltpu.make_async_copy(upper[n_dp - k - 1], grads.at[k], own_sems.at[k]))

    for k in range(n_dp):
        grad_copies(k, lambda copy: copy.start())
    run_copies(column_copies(parts, 0, cols, sems))
    for k in range(n_dp):
        grad_copies(k, lambda copy: copy.wait())
    width = out_q.shape[1]
    tile = min(256, out_q.shape[0])
    tokens = cols.shape[1]

    @pl.loop(0, out_q.shape[0] // tile)
    def _(i):
        at = pl.ds(pl.multiple_of(i * tile, tile), tile)
        total = dot_tn(
            cols[:, :, at].reshape(n_dp * tokens, tile),
            grads[...].reshape(n_dp * tokens, 3 * width),
        ).astype(BF16)
        out_q[at, :] = total[:, :width]
        out_k[at, :] = total[:, width : 2 * width]
        out_v[at, :] = total[:, 2 * width :]


def weight_grads(parts, own, lower, upper):
    n_dp, _, rows, slice_width = parts[0].shape
    tokens, triple = own.shape
    width = triple // 3
    held_mib = n_dp * tokens * (slice_width + triple) * 2 // MIB
    return pl.pallas_call(
        functools.partial(weight_kernel, len(parts), n_dp),
        out_shape=tuple(sds((slice_width, width), BF16) for _ in range(3)),
        in_specs=[HBM] * (len(parts) + 2 * n_dp - 1),
        scratch_shapes=[
            pltpu.VMEM((n_dp, tokens, slice_width), BF16),
            pltpu.VMEM((n_dp, tokens, triple), BF16),
            pltpu.SemaphoreType.DMA((len(parts),)),
            pltpu.SemaphoreType.DMA((n_dp,)),
        ],
        compiler_params=params(min(60, held_mib + 24)),
        cost_estimate=cost(2 * n_dp * tokens * slice_width * triple, 8 * MIB),
        name="weight_grads",
    )(*parts, own, *lower, *upper)


def out_weight_kernel(n_seq, n_dp, *rest):
    parts, rest = rest[:n_seq], rest[n_seq:]
    atts, rest = rest[:n_dp], rest[n_dp:]
    out_ref, cols, held, sems, own_sems = rest
    copies = column_copies(parts, 1, cols, sems)
    for k, att in enumerate(atts):
        copies.append(pltpu.make_async_copy(att, held.at[k], own_sems.at[k]))
    run_copies(copies)
    tokens = cols.shape[1]
    tile = 128

    @pl.loop(0, out_ref.shape[0] // tile)
    def _(i):
        at = pl.ds(pl.multiple_of(i * tile, tile), tile)
        out_ref[at, :] = dot_tn(
            held[:, :, at].reshape(n_dp * tokens, tile),
            cols[...].reshape(n_dp * tokens, out_ref.shape[1]),
        ).astype(BF16)


def out_weight_grads(parts, atts):
    n_dp, _, rows, slice_width = parts[0].shape
    tokens, width = atts[0].shape
    held_mib = n_dp * tokens * (slice_width + width) * 2 // MIB
    return pl.pallas_call(
        functools.partial(out_weight_kernel, len(parts), n_dp),
        out_shape=sds((width, slice_width), BF16),
        in_specs=[HBM] * (len(parts) + n_dp),
        scratch_shapes=[
            pltpu.VMEM((n_dp, tokens, slice_width), BF16),
            pltpu.VMEM((n_dp, tokens, width), BF16),
            pltpu.SemaphoreType.DMA((len(parts),)),
            pltpu.SemaphoreType.DMA((n_dp,)),
        ],
        compiler_params=params(min(60, held_mib + 20)),
        cost_estimate=cost(2 * n_dp * tokens * slice_width * width, 5 * MIB),
        name="out_weight_grads",
    )(*parts, *atts)


def swapped(value, axis, j):
    return lax.ppermute(value, axis, [(i, i ^ j) for i in range(lax.axis_size(axis))])


def crossed(value, j):
    n = lax.axis_size("seq")
    pairs = [(p * n + i, (1 - p) * n + (i ^ j)) for p in range(2) for i in range(n)]
    return lax.ppermute(value, ("pipe", "seq"), pairs)


def rotated(value, axis, k):
    n = lax.axis_size(axis)
    return lax.ppermute(value, axis, [(i, (i + k) % n) for i in range(n)])


def shifted(value, axis, by):
    n = lax.axis_size(axis)
    return lax.ppermute(value, axis, [(i, i + by) for i in range(n) if 0 <= i + by < n])


def line_gather(value, axis):
    lower, upper, up, down = [], [], value, value
    for _ in range(lax.axis_size(axis) - 1):
        up, down = shifted(up, axis, 1), shifted(down, axis, -1)
        lower.append(up)
        upper.append(down)
    return lower, upper


def local(
    encoded,
    sent_forward,
    head_cotangent,
    grad_sent,
    x_saved,
    q_saved,
    k_saved,
    v_saved,
    norm_gain,
    logit_scale,
    w_query,
    w_key,
    w_value,
    w_out,
    key_blocks,
    key_counts,
):
    n_seq, n_dp = lax.axis_size("seq"), lax.axis_size("dp")
    factor = logit_scale / math.sqrt(HD)
    blocks, counts = key_blocks[0], key_counts[0]
    wq, wk, wv, wo = w_query[0], w_key[0], w_value[0], w_out[0]
    q, k, v, x = q_saved[0, 0], k_saved[0, 0], v_saved[0, 0], x_saved[0, 0]

    send_x, send_cot = pick(sent_forward[0, 0], encoded[0], grad_sent[0, 0], head_cotangent[0])
    cots = [crossed(send_cot, j) for j in range(n_seq)]
    xs = [crossed(send_x, j) for j in range(n_seq)]

    soft, att = saved_attention(blocks, counts, factor, q, k, v)
    columns = column_parts(x, cots[0], norm_gain, n_dp)
    columns = [columns[0]] + [rotated(columns[i], "dp", i) for i in range(1, n_dp)]
    atts = [att] + [rotated(att, "dp", i) for i in range(1, n_dp)]

    grads = backward_attention(factor, cots, wo, soft, att, q, k, v)
    lower, upper = line_gather(grads, "dp")
    dx = input_grads(grads, wq, wk, wv, n_seq)
    dx = [dx[0]] + [swapped(dx[j], "seq", j) for j in range(1, n_seq)]

    mixed = forward_terms(blocks, counts, factor, xs, norm_gain, wq, wk, wv, wo)
    mixed = [mixed[0]] + [swapped(mixed[j], "seq", j) for j in range(1, n_seq)]

    parts = jnp.stack(columns)
    parts = [parts] + [swapped(parts, "seq", j) for j in range(1, n_seq)]

    back_out, gain_part = back(dx, x, cots[0], norm_gain)
    for axis in ("seq", "dp"):
        hop = 1
        while hop < lax.axis_size(axis):
            gain_part = gain_part + swapped(gain_part, axis, hop)
            hop *= 2

    total = mixed[0].astype(F32)
    for term in mixed[1:]:
        total = total + term.astype(F32)
    forward_out = (xs[0].astype(F32) + total).astype(BF16)

    grad_out = out_weight_grads(parts, atts)
    grad_q, grad_k, grad_v = weight_grads(parts, grads, lower, upper)
    return (
        forward_out[None, None],
        back_out[None, None],
        grad_q[None],
        grad_k[None],
        grad_v[None],
        grad_out[None],
        gain_part,
    )


def solution(mesh):
    in_specs = (
        P("dp", "seq", None),
        P("pipe", "dp", "seq", None),
        P("dp", "seq", None),
        P("pipe", "dp", "seq", None),
        P("pipe", "dp", "seq", None),
        P("pipe", "dp", None, "seq"),
        P("pipe", "dp", None, "seq"),
        P("pipe", "dp", None, "seq"),
        P("pipe", None),
        P("pipe", "seq"),
        P("pipe", None, "seq"),
        P("pipe", None, "seq"),
        P("pipe", None, "seq"),
        P("pipe", "seq", None),
        P("dp", None, None),
        P("dp", None),
    )
    out_specs = (
        P("pipe", "dp", "seq", None),
        P("pipe", "dp", "seq", None),
        P("pipe", "dp", "seq"),
        P("pipe", "dp", "seq"),
        P("pipe", "dp", "seq"),
        P("pipe", "seq", "dp"),
        P("pipe", None),
    )
    return jax.shard_map(local, mesh=mesh, in_specs=in_specs, out_specs=out_specs, check_vma=False)
```

time: 554 us -> 240 us (0.43)
  waiting for transfers between devices: 374 us -> 111 us
  blocking collectives: 78.6 us -> 0 us
  Pallas kernels: 0 us -> 67.5 us
  matrix products: 58 us -> 0 us
  starting transfers between devices: 4.67 us -> 45.9 us
  between operations: 14.3 us -> 0.92 us
  other arithmetic: 11.6 us -> 2.6 us
    reduce_scatter x6 -> x0, waiting for transfers between devices: 297 us -> none  [the longest x1 80.3 us: local(): lax.psum_scatter(query_total.astype(jnp.bfloat16), 'dp', scatter_dimensio...]
    ppermute x2 -> x33, waiting for transfers between devices: 3.32 us -> 111 us  [the longest x13 86.4 us: swapped(): lax.ppermute(value, axis, [(i, i ^ j) for i in range(lax.axis_size(axis))])]
    psum x1 -> x0, blocking collectives: 78.6 us -> none  [local(): grad_gain = lax.psum(gain_part, ('seq', 'dp'))]
    all_gather x3 -> x0, waiting for transfers between devices: 73.7 us -> none  [the longest x1 34.7 us: local(): segment = lax.all_gather(normed, 'seq', axis=0, tiled=True)]
    pallas_call x0 -> x9, Pallas kernels: none -> 67.5 us  [the longest x1 32.9 us: pick(): pl.pallas_call(pick_kernel, out_shape=(sds(shape, BF16), sds(shape, BF16)...]
    dot_general x21 -> x0, matrix products: 55.9 us -> none  [the longest x3 11.4 us: local(): jnp.einsum('td,tc->dc', segment, row_block, preferred_element_type=jnp.fl...]
    ppermute x2 -> x33, starting transfers between devices: 4.12 us -> 45.9 us  [the longest x13 18 us: swapped(): lax.ppermute(value, axis, [(i, i ^ j) for i in range(lax.axis_size(axis))])]
    unnamed x26 -> x34, local copies, waits for them, and re-layouts: 2.53 us -> 11.4 us
  transfers between devices with their start and end apart: 11 -> 33, of which waited for: 10 -> 14; matrix products, arithmetic and copies ran while one was open for 9% -> 1% of each run, Pallas kernels for 0% -> 12%
where the time goes in v1:
time: 240 us
  waiting for transfers between devices  111 us (46%)
  Pallas kernels  67.5 us (28%)
  starting transfers between devices  45.9 us (19%)
  local copies, waits for them, and re-layouts  11.4 us (5%)
  other arithmetic  2.6 us (1%)
    ppermute x13, waiting for transfers between devices, swapped(): lax.ppermute(value, axis, [(i, i ^ j) for i in range(lax.axis_size(axis))])  86.4 us
    pallas_call x1, Pallas kernels, pick(): pl.pallas_call(pick_kernel, out_shape=(sds(shape, BF16), sds(shape, BF16)...  32.9 us
    ppermute x13, starting transfers between devices, swapped(): lax.ppermute(value, axis, [(i, i ^ j) for i in range(lax.axis_size(axis))])  18 us
    ppermute x8, waiting for transfers between devices, crossed(): return lax.ppermute(value, ('pipe', 'seq'), pairs)  17.5 us
    ppermute x6, starting transfers between devices, rotated(): return lax.ppermute(value, axis, [(i, (i + k) % n) for i in range(n)])  11.9 us
    unnamed x34, local copies, waits for them, and re-layouts  11.4 us
    pallas_call x1, Pallas kernels, forward_terms(): pl.pallas_call(functools.partial(forward_kernel, n), grid=(model // CHUNK...  11 us
    ppermute x6, starting transfers between devices, shifted(): lax.ppermute(value, axis, [(i, i + by) for i in range(n) if 0 <= i + by <...  8.81 us
  transfers between devices with their start and end apart: 33, of which 14 were waited for; matrix products, arithmetic and copies ran while one was open for 1% of the time, Pallas kernels for 12%

profile of v1, /device:TPU:0, one launch (start us, length us, event | category | flops | bytes accessed | tf_op | source)
XLA Modules:
  0.0 239.6 jit_solution(4365247036122207938)
XLA Ops:
  0.6 32.9 %pick.1 = (bf16[64,4096]{1,0:T(8,128)(2,1)}, bf16[64,4096]{1,0:T(8,128)(2,1)}) custom-call(bf16[64,4096]{1,0:T(8,128)(2,1)} %bitcast.47, bf16[64,4096]{1,0:T(8,128)(2,1)} %bitcast.48, bf16[64,4096]{1,0:T(8,128)(2,1)} %bitcast.49, bf16[64,4096]{1,0:T(8,128)(2,1)} %bitcast.50), custom_call_target="tpu_custom_call" | custom-call | bytes 2097152 | tf_op jit(solution)/shard_map/pick/pallas_call | solution.py:106
  33.5 0.5 collective-permute-start.7
  34.1 2.6 %collective-permute-start.8 = (bf16[64,4096]{1,0:T(8,128)(2,1)}, bf16[64,4096]{1,0:T(8,128)(2,1)S(1)}, u32[]{:S(2)}, u32[]{:S(2)}) collective-permute-start(bf16[64,4096]{1,0:T(8,128)(2,1)} %get-tuple-element.33), channel_id=1, source_target_pairs={{0,20},{4,16},{8,28},{12,24},{16,4},{20,0},{24,12},{28,8},{1,21},{... | collective-permute-start | bytes 1572872 | tf_op jit(solution)/shard_map/ppermute | solution.py:489
  36.7 1.2 collective-permute-start.9
  37.9 0.7 broadcast_multiply_fusion.factor_ref
  38.5 0.9 copy-done.5
  39.5 0.9 copy-done.7
  40.5 0.9 copy-done.9
  41.4 0.7 copy-done.12
  42.1 0.7 copy-done.14
  42.7 1.7 saved_attention.1
  44.4 2.1 collective-permute-start.26
  46.5 2.6 %collective-permute-start.27 = (bf16[256,512]{1,0:T(8,128)(2,1)S(1)}, bf16[256,512]{1,0:T(8,128)(2,1)S(1)}, u32[]{:S(2)}, u32[]{:S(2)}) collective-permute-start(bf16[256,512]{1,0:T(8,128)(2,1)S(1)} %get-tuple-element.35.rest_6_.rest_4_), channel_id=1, source_target_pairs={{0,2},{1,3},{2,0},{3,1},{4,6},{5,7},{6,4},{7,5},{8,10},{9,11},{10,... | collective-permute-start | bytes 786440 | tf_op jit(solution)/shard_map/ppermute | solution.py:494
  49.1 0.1 collective-permute-done.8.rest_1_
  49.2 0.5 collective-permute-start
  49.7 12.4 %collective-permute-done.9.rest_2_ = bf16[64,4096]{1,0:T(8,128)(2,1)S(1)} collective-permute-done((bf16[64,4096]{1,0:T(8,128)(2,1)}, bf16[64,4096]{1,0:T(8,128)(2,1)S(1)}, u32[]{:S(2)}, u32[]{:S(2)}) %collective-permute-start.9) | collective-permute-done | bytes 524320 | tf_op jit(solution)/shard_map/ppermute | solution.py:489
  62.1 2.2 copy-done.3
  64.3 0.9 copy-done.6
  65.2 0.9 copy-done.8
  66.2 0.9 copy-done.10
  67.1 5.3 %backward_attention.1.g_ref.rest_4_ = bf16[256,1536]{1,0:T(8,128)(2,1)S(1)} custom-call(f32[1,4]{1,0:T(1,128)S(1)} %broadcast_multiply_fusion.factor_ref, bf16[64,4096]{1,0:T(8,128)(2,1)S(1)} %collective-permute-done.7.rest_0_.rest_5_.cot_ref, bf16[64,4096]{1,0:T(8,128)(2,1)S(1)} %collective-permute-done.8.rest_1_, ...), custom_call_target="tpu_custom_call" | custom-call | flops 1073741824 | bytes 12582912 | tf_op jit(solution)/shard_map/backward_attention/pallas_call | solution.py:214
  72.5 2.2 copy-done.2
  74.7 5.3 %input_grads.1 = (bf16[64,4096]{1,0:T(8,128)(2,1)S(1)}, bf16[64,4096]{1,0:T(8,128)(2,1)S(1)}, bf16[64,4096]{1,0:T(8,128)(2,1)S(1)}, bf16[64,4096]{1,0:T(8,128)(2,1)S(1)}) custom-call(bf16[256,1536]{1,0:T(8,128)(2,1)S(1)} %backward_attention.1.g_ref.rest_4_, bf16[4096,512]{1,0:T(8,128)(2,1)S(1)} %bitcast.25, bf16[4096,512]{1,0:T(8,128)(2,1)S(1)} %bitcast.27, ...), custom_call_target="tpu_custom_call" | custom-call | flops 3221225472 | bytes 12582912 | tf_op jit(solution)/shard_map/input_grads/pallas_call | solution.py:252
  80.0 0.6 collective-permute-start.11
  80.7 3.6 %collective-permute-start.28 = (bf16[256,512]{1,0:T(8,128)(2,1)S(1)}, bf16[256,512]{1,0:T(8,128)(2,1)S(1)}, u32[]{:S(2)}, u32[]{:S(2)}) collective-permute-start(bf16[256,512]{1,0:T(8,128)(2,1)S(1)} %get-tuple-element.35.rest_6_.rest_4_), channel_id=1, source_target_pairs={{0,3},{1,0},{2,1},{3,2},{4,7},{5,4},{6,5},{7,6},{8,11},{9,8},{10,9... | collective-permute-start | bytes 786440 | tf_op jit(solution)/shard_map/ppermute | solution.py:494
  84.3 1.5 collective-permute-start.12
  85.8 1.4 collective-permute-start.13
  87.2 3.2 %collective-permute-done.28.rest_7_ = bf16[256,512]{1,0:T(8,128)(2,1)S(1)} collective-permute-done((bf16[256,512]{1,0:T(8,128)(2,1)S(1)}, bf16[256,512]{1,0:T(8,128)(2,1)S(1)}, u32[]{:S(2)}, u32[]{:S(2)}) %collective-permute-start.28) | collective-permute-done | bytes 262176 | tf_op jit(solution)/shard_map/ppermute | solution.py:494
  90.4 2.1 collective-permute-start.20
  92.6 2.3 collective-permute-done.11.rest_1_
  94.9 1.3 collective-permute-start.23
  96.2 13.3 %collective-permute-done.12.rest_2_ = bf16[64,4096]{1,0:T(8,128)(2,1)S(1)} collective-permute-done((bf16[64,4096]{1,0:T(8,128)(2,1)S(1)}, bf16[64,4096]{1,0:T(8,128)(2,1)S(1)}, u32[]{:S(2)}, u32[]{:S(2)}) %collective-permute-start.12) | collective-permute-done | bytes 524320 | tf_op jit(solution)/shard_map/ppermute | solution.py:483
  109.5 2.3 collective-permute-start.3
  111.8 2.0 back.1
  113.8 2.4 %collective-permute-done.1.rest_1_ = bf16[64,4096]{1,0:T(8,128)(2,1)S(1)} collective-permute-done((bf16[64,4096]{1,0:T(8,128)(2,1)S(1)}, bf16[64,4096]{1,0:T(8,128)(2,1)S(1)}, u32[]{:S(2)}, u32[]{:S(2)}) %collective-permute-start.1) | collective-permute-done | bytes 524320 | tf_op jit(solution)/shard_map/ppermute | solution.py:489
  116.2 1.2 collective-permute-start.29
  117.4 0.4 columns.1
  117.8 10.7 %collective-permute-done.29 = f32[1,4096]{1,0:T(1,128)S(1)} collective-permute-done((f32[1,4096]{1,0:T(1,128)S(1)}, f32[1,4096]{1,0:T(1,128)S(1)}, u32[]{:S(2)}, u32[]{:S(2)}) %collective-permute-start.29) | collective-permute-done | bytes 16416 | tf_op jit(solution)/shard_map/ppermute | solution.py:483
  128.4 3.6 %collective-permute-start.16 = (bf16[2,64,1024]{2,1,0:T(8,128)(2,1)S(1)}, bf16[2,64,1024]{2,1,0:T(8,128)(2,1)S(1)}, u32[]{:S(2)}, u32[]{:S(2)}) collective-permute-start(bf16[2,64,1024]{2,1,0:T(8,128)(2,1)S(1)} %get-tuple-element.44), channel_id=1, source_target_pairs={{0,3},{1,0},{2,1},{3,2},{4,7},{5,4},{6,5},{7,6},{8,11},{9,8},{10,9... | collective-permute-start | bytes 786440 | tf_op jit(solution)/shard_map/ppermute | solution.py:494
  132.1 2.6 %collective-permute-done.2.rest_2_ = bf16[64,4096]{1,0:T(8,128)(2,1)S(1)} collective-permute-done((bf16[64,4096]{1,0:T(8,128)(2,1)S(1)}, bf16[64,4096]{1,0:T(8,128)(2,1)S(1)}, u32[]{:S(2)}, u32[]{:S(2)}) %collective-permute-start.2) | collective-permute-done | bytes 524320 | tf_op jit(solution)/shard_map/ppermute | solution.py:489
  134.7 4.2 %collective-permute-done.16 = bf16[2,64,1024]{2,1,0:T(8,128)(2,1)S(1)} collective-permute-done((bf16[2,64,1024]{2,1,0:T(8,128)(2,1)S(1)}, bf16[2,64,1024]{2,1,0:T(8,128)(2,1)S(1)}, u32[]{:S(2)}, u32[]{:S(2)}) %collective-permute-start.16) | collective-permute-done | bytes 262176 | tf_op jit(solution)/shard_map/ppermute | solution.py:494
  138.8 1.4 collective-permute-start.30
  140.3 1.3 collective-permute-start.21
  141.6 1.3 collective-permute-start.24
  143.0 11.0 %forward_terms.1 = (bf16[64,4096]{1,0:T(8,128)(2,1)S(1)}, bf16[64,4096]{1,0:T(8,128)(2,1)S(1)}, bf16[64,4096]{1,0:T(8,128)(2,1)S(1)}, bf16[64,4096]{1,0:T(8,128)(2,1)S(1)}) custom-call(s32[2,2]{1,0:T(2,128)S(1)} %bitcast.43, s32[2]{0:T(128)S(1)} %bitcast.45, f32[1,4]{1,0:T(1,128)S(1)} %broadcast_multiply_fusion.factor_ref, ...), custom_call_target="tpu_custom_call" | custom-call | flops 4294967296 | bytes 16777216 | tf_op jit(solution)/shard_map/forward_terms/pallas_call | solution.py:323
  154.0 1.3 collective-permute-start.6
  155.4 2.7 %collective-permute-start.31 = (f32[1,4096]{1,0:T(1,128)S(1)}, f32[1,4096]{1,0:T(1,128)S(1)}, u32[]{:S(2)}, u32[]{:S(2)}) collective-permute-start(f32[1,4096]{1,0:T(1,128)S(1)} %add.29), channel_id=1, source_target_pairs={{0,1},{1,0},{2,3},{3,2},{4,5},{5,4},{6,7},{7,6},{8,9},{9,8},{10,11... | collective-permute-start | bytes 49160 | tf_op jit(solution)/shard_map/ppermute | solution.py:483
  158.1 1.1 collective-permute-start.5
  159.2 11.6 %collective-permute-done.31 = f32[1,4096]{1,0:T(1,128)S(1)} collective-permute-done((f32[1,4096]{1,0:T(1,128)S(1)}, f32[1,4096]{1,0:T(1,128)S(1)}, u32[]{:S(2)}, u32[]{:S(2)}) %collective-permute-start.31) | collective-permute-done | bytes 16416 | tf_op jit(solution)/shard_map/ppermute | solution.py:483
  170.8 1.9 collective-permute-start.4
  172.8 0.1 pad_maximum_fusion.rest_0_
  172.9 4.9 %collective-permute-done.5 = bf16[64,4096]{1,0:T(8,128)(2,1)S(1)} collective-permute-done((bf16[64,4096]{1,0:T(8,128)(2,1)S(1)}, bf16[64,4096]{1,0:T(8,128)(2,1)S(1)}, u32[]{:S(2)}, u32[]{:S(2)}) %collective-permute-start.5) | collective-permute-done | bytes 524320 | tf_op jit(solution)/shard_map/ppermute | solution.py:483
  177.8 1.4 collective-permute-start.17
  179.2 6.4 %collective-permute-done.4 = bf16[64,4096]{1,0:T(8,128)(2,1)S(1)} collective-permute-done((bf16[64,4096]{1,0:T(8,128)(2,1)S(1)}, bf16[64,4096]{1,0:T(8,128)(2,1)S(1)}, u32[]{:S(2)}, u32[]{:S(2)}) %collective-permute-start.4) | collective-permute-done | bytes 524320 | tf_op jit(solution)/shard_map/ppermute | solution.py:483
  185.6 1.0 collective-permute-start.18
  186.7 2.3 collective-permute-start.19
  189.0 1.5 collective-permute-start.22
  190.5 1.3 collective-permute-start.25
  191.8 1.1 fusion
  192.9 0.6 add.31
  193.5 14.6 %collective-permute-done.17.rest_1_ = bf16[4,2,64,1024]{3,2,1,0:T(8,128)(2,1)S(1)} collective-permute-done((bf16[4,2,64,1024]{3,2,1,0:T(8,128)(2,1)S(1)}, bf16[4,2,64,1024]{3,2,1,0:T(8,128)(2,1)S(1)}, u32[]{:S(2)}, u32[]{:S(2)}) %collective-permute-start.17) | collective-permute-done | bytes 1048608 | tf_op jit(solution)/shard_map/ppermute | solution.py:483
  208.1 22.6 %collective-permute-done.18.rest_2_ = bf16[4,2,64,1024]{3,2,1,0:T(8,128)(2,1)S(1)} collective-permute-done((bf16[4,2,64,1024]{3,2,1,0:T(8,128)(2,1)S(1)}, bf16[4,2,64,1024]{3,2,1,0:T(8,128)(2,1)S(1)}, u32[]{:S(2)}, u32[]{:S(2)}) %collective-permute-start.18) | collective-permute-done | bytes 1048608 | tf_op jit(solution)/shard_map/ppermute | solution.py:483
  230.7 3.2 %out_weight_grads.1 = bf16[512,1024]{1,0:T(8,128)(2,1)} custom-call(bf16[4,2,64,1024]{3,2,1,0:T(8,128)(2,1)S(1)} %pad_maximum_fusion.rest_0_, bf16[4,2,64,1024]{3,2,1,0:T(8,128)(2,1)S(1)} %collective-permute-done.17.rest_1_, bf16[4,2,64,1024]{3,2,1,0:T(8,128)(2,1)S(1)} %collective-permute-done.18.rest_2_, ...), custom_call_target="tpu_custom_call" | custom-call | flops 1073741824 | bytes 5242880 | tf_op jit(solution)/shard_map/out_weight_grads/pallas_call | solution.py:466
  234.0 5.7 %weight_grads.1 = (bf16[1024,512]{1,0:T(8,128)(2,1)}, bf16[1024,512]{1,0:T(8,128)(2,1)}, bf16[1024,512]{1,0:T(8,128)(2,1)}) custom-call(bf16[4,2,64,1024]{3,2,1,0:T(8,128)(2,1)S(1)} %pad_maximum_fusion.rest_0_, bf16[4,2,64,1024]{3,2,1,0:T(8,128)(2,1)S(1)} %collective-permute-done.17.rest_1_, bf16[4,2,64,1024]{3,2,1,0:T(8,128)(2,1)S(1)} %collective-permute-done.18.rest_2_, ...), custom_call_target="tpu_custom_call" | custom-call | flops 3221225472 | bytes 8388608 | tf_op jit(solution)/shard_map/weight_grads/pallas_call | solution.py:426
  (52 shorter events, 0.3 us)
Async XLA Ops:
  33.5 13.0 %collective-permute-start.7 = (bf16[64,4096]{1,0:T(8,128)(2,1)}, bf16[64,4096]{1,0:T(8,128)(2,1)S(1)}, u32[]{:S(2)}, u32[]{:S(2)}) collective-permute-start(bf16[64,4096]{1,0:T(8,128)(2,1)} %get-tuple-element.33), channel_id=1, source_target_pairs={{0,16},{4,20},{8,24},{12,28},{16,0},{20,4},{24,8},{28,12},{1,17},{... | collective-permute-start | bytes 1572872 | tf_op jit(solution)/shard_map/ppermute | solution.py:489
  34.1 15.2 %collective-permute-start.8 = (bf16[64,4096]{1,0:T(8,128)(2,1)}, bf16[64,4096]{1,0:T(8,128)(2,1)S(1)}, u32[]{:S(2)}, u32[]{:S(2)}) collective-permute-start(bf16[64,4096]{1,0:T(8,128)(2,1)} %get-tuple-element.33), channel_id=1, source_target_pairs={{0,20},{4,16},{8,28},{12,24},{16,4},{20,0},{24,12},{28,8},{1,21},{... | collective-permute-start | bytes 1572872 | tf_op jit(solution)/shard_map/ppermute | solution.py:489
  36.7 25.4 %collective-permute-start.9 = (bf16[64,4096]{1,0:T(8,128)(2,1)}, bf16[64,4096]{1,0:T(8,128)(2,1)S(1)}, u32[]{:S(2)}, u32[]{:S(2)}) collective-permute-start(bf16[64,4096]{1,0:T(8,128)(2,1)} %get-tuple-element.33), channel_id=1, source_target_pairs={{0,24},{4,28},{8,16},{12,20},{16,8},{20,12},{24,0},{28,4},{1,25},{... | collective-permute-start | bytes 1572872 | tf_op jit(solution)/shard_map/ppermute | solution.py:489
  37.9 24.2 %collective-permute-start.10 = (bf16[64,4096]{1,0:T(8,128)(2,1)}, bf16[64,4096]{1,0:T(8,128)(2,1)S(1)}, u32[]{:S(2)}, u32[]{:S(2)}) collective-permute-start(bf16[64,4096]{1,0:T(8,128)(2,1)} %get-tuple-element.33), channel_id=1, source_target_pairs={{0,28},{4,24},{8,20},{12,16},{16,12},{20,8},{24,4},{28,0},{1,29},{... | collective-permute-start | bytes 1572872 | tf_op jit(solution)/shard_map/ppermute | solution.py:489
  38.5 0.9 copy-start.5
  39.5 0.9 copy-start.7
  40.4 0.9 copy-start.9
  41.4 0.7 copy-start.12
  42.1 0.7 copy-start.14
  44.4 39.9 %collective-permute-start.26 = (bf16[256,512]{1,0:T(8,128)(2,1)S(1)}, bf16[256,512]{1,0:T(8,128)(2,1)S(1)}, u32[]{:S(2)}, u32[]{:S(2)}) collective-permute-start(bf16[256,512]{1,0:T(8,128)(2,1)S(1)} %get-tuple-element.35.rest_6_.rest_4_), channel_id=1, source_target_pairs={{0,1},{1,2},{2,3},{3,0},{4,5},{5,6},{6,7},{7,4},{8,9},{9,10},{10,1... | collective-permute-start | bytes 786440 | tf_op jit(solution)/shard_map/ppermute | solution.py:494
  46.5 39.3 %collective-permute-start.27 = (bf16[256,512]{1,0:T(8,128)(2,1)S(1)}, bf16[256,512]{1,0:T(8,128)(2,1)S(1)}, u32[]{:S(2)}, u32[]{:S(2)}) collective-permute-start(bf16[256,512]{1,0:T(8,128)(2,1)S(1)} %get-tuple-element.35.rest_6_.rest_4_), channel_id=1, source_target_pairs={{0,2},{1,3},{2,0},{3,1},{4,6},{5,7},{6,4},{7,5},{8,10},{9,11},{10,... | collective-permute-start | bytes 786440 | tf_op jit(solution)/shard_map/ppermute | solution.py:494
  49.2 41.2 %collective-permute-start = (bf16[64,4096]{1,0:T(8,128)(2,1)}, bf16[64,4096]{1,0:T(8,128)(2,1)S(1)}, u32[]{:S(2)}, u32[]{:S(2)}) collective-permute-start(bf16[64,4096]{1,0:T(8,128)(2,1)} %get-tuple-element.28), channel_id=1, source_target_pairs={{0,16},{4,20},{8,24},{12,28},{16,0},{20,4},{24,8},{28,12},{1,17},{... | collective-permute-start | bytes 1572872 | tf_op jit(solution)/shard_map/ppermute | solution.py:489
  62.1 2.2 copy-start.3
  64.3 0.9 copy-start.6
  65.2 0.9 copy-start.8
  66.2 0.9 copy-start.10
  67.1 5.3 %copy-start = (bf16[1,4096,512]{2,1,0:T(8,128)(2,1)S(1)}, bf16[1,4096,512]{2,1,0:T(8,128)(2,1)}, u32[]{:S(2)}) copy-start(bf16[1,4096,512]{2,1,0:T(8,128)(2,1)} %param.26) | copy-start | bytes 12582916
  67.1 5.3 %copy-start.1 = (bf16[1,4096,512]{2,1,0:T(8,128)(2,1)S(1)}, bf16[1,4096,512]{2,1,0:T(8,128)(2,1)}, u32[]{:S(2)}) copy-start(bf16[1,4096,512]{2,1,0:T(8,128)(2,1)} %param.27) | copy-start | bytes 12582916
  72.5 2.2 copy-start.2
  74.7 15.8 %copy-start.16 = (bf16[64,4096]{1,0:T(8,128)(2,1)S(1)}, bf16[64,4096]{1,0:T(8,128)(2,1)}, u32[]{:S(2)}) copy-start(bf16[64,4096]{1,0:T(8,128)(2,1)} %get-tuple-element.28) | copy-start | bytes 1572868
  74.7 37.1 %copy-start.4 = (bf16[1,1,64,4096]{3,2,1,0:T(8,128)(2,1)S(1)}, bf16[1,1,64,4096]{3,2,1,0:T(8,128)(2,1)}, u32[]{:S(2)}) copy-start(bf16[1,1,64,4096]{3,2,1,0:T(8,128)(2,1)} %param.20) | copy-start | bytes 1572868
  74.7 37.1 %copy-start.11 = (f32[1,4096]{1,0:T(1,128)S(1)}, f32[1,4096]{1,0:T(1,128)}, u32[]{:S(2)}) copy-start(f32[1,4096]{1,0:T(1,128)} %gain_ref.1) | copy-start | bytes 49156
  80.0 62.9 %copy-start.13 = (s32[1,2,2]{2,1,0:T(2,128)S(1)}, s32[1,2,2]{2,1,0:T(2,128)}, u32[]{:S(2)}) copy-start(s32[1,2,2]{2,1,0:T(2,128)} %param.30) | copy-start | bytes 52
  80.0 62.9 %copy-start.15 = (s32[1,2]{1,0:T(1,128)S(1)}, s32[1,2]{1,0:T(1,128)}, u32[]{:S(2)}) copy-start(s32[1,2]{1,0:T(1,128)} %param.31) | copy-start | bytes 28
  80.0 14.8 %collective-permute-start.11 = (bf16[64,4096]{1,0:T(8,128)(2,1)S(1)}, bf16[64,4096]{1,0:T(8,128)(2,1)S(1)}, u32[]{:S(2)}, u32[]{:S(2)}) collective-permute-start(bf16[64,4096]{1,0:T(8,128)(2,1)S(1)} %get-tuple-element.37), channel_id=1, source_target_pairs={{0,4},{4,0},{8,12},{12,8},{1,5},{5,1},{9,13},{13,9},{2,6},{6,2},{1... | collective-permute-start | bytes 1572872 | tf_op jit(solution)/shard_map/ppermute | solution.py:483
  80.7 9.8 %collective-permute-start.28 = (bf16[256,512]{1,0:T(8,128)(2,1)S(1)}, bf16[256,512]{1,0:T(8,128)(2,1)S(1)}, u32[]{:S(2)}, u32[]{:S(2)}) collective-permute-start(bf16[256,512]{1,0:T(8,128)(2,1)S(1)} %get-tuple-element.35.rest_6_.rest_4_), channel_id=1, source_target_pairs={{0,3},{1,0},{2,1},{3,2},{4,7},{5,4},{6,5},{7,6},{8,11},{9,8},{10,9... | collective-permute-start | bytes 786440 | tf_op jit(solution)/shard_map/ppermute | solution.py:494
  84.3 25.2 %collective-permute-start.12 = (bf16[64,4096]{1,0:T(8,128)(2,1)S(1)}, bf16[64,4096]{1,0:T(8,128)(2,1)S(1)}, u32[]{:S(2)}, u32[]{:S(2)}) collective-permute-start(bf16[64,4096]{1,0:T(8,128)(2,1)S(1)} %get-tuple-element.38), channel_id=1, source_target_pairs={{0,8},{4,12},{8,0},{12,4},{1,9},{5,13},{9,1},{13,5},{2,10},{6,14},... | collective-permute-start | bytes 1572872 | tf_op jit(solution)/shard_map/ppermute | solution.py:483
  85.8 23.7 %collective-permute-start.13 = (bf16[64,4096]{1,0:T(8,128)(2,1)S(1)}, bf16[64,4096]{1,0:T(8,128)(2,1)S(1)}, u32[]{:S(2)}, u32[]{:S(2)}) collective-permute-start(bf16[64,4096]{1,0:T(8,128)(2,1)S(1)} %get-tuple-element.39), channel_id=1, source_target_pairs={{0,12},{4,8},{8,4},{12,0},{1,13},{5,9},{9,5},{13,1},{2,14},{6,10},... | collective-permute-start | bytes 1572872 | tf_op jit(solution)/shard_map/ppermute | solution.py:483
  90.4 25.8 %collective-permute-start.1 = (bf16[64,4096]{1,0:T(8,128)(2,1)S(1)}, bf16[64,4096]{1,0:T(8,128)(2,1)S(1)}, u32[]{:S(2)}, u32[]{:S(2)}) collective-permute-start(bf16[64,4096]{1,0:T(8,128)(2,1)S(1)} %copy-done.16), channel_id=1, source_target_pairs={{0,20},{4,16},{8,28},{12,24},{16,4},{20,0},{24,12},{28,8},{1,21},{... | collective-permute-start | bytes 1572872 | tf_op jit(solution)/shard_map/ppermute | solution.py:489
  90.4 49.9 %collective-permute-start.20 = (bf16[256,1536]{1,0:T(8,128)(2,1)S(1)}, bf16[256,1536]{1,0:T(8,128)(2,1)S(1)}, u32[]{:S(2)}, u32[]{:S(2)}) collective-permute-start(bf16[256,1536]{1,0:T(8,128)(2,1)S(1)} %backward_attention.1.g_ref.rest_4_), channel_id=1, source_target_pairs={{0,1},{1,2},{2,3},{4,5},{5,6},{6,7},{8,9},{9,10},{10,11},{12,13},{... | collective-permute-start | bytes 2359304 | tf_op jit(solution)/shard_map/ppermute | solution.py:499
  94.9 46.8 %collective-permute-start.23 = (bf16[256,1536]{1,0:T(8,128)(2,1)S(1)}, bf16[256,1536]{1,0:T(8,128)(2,1)S(1)}, u32[]{:S(2)}, u32[]{:S(2)}) collective-permute-start(bf16[256,1536]{1,0:T(8,128)(2,1)S(1)} %backward_attention.1.g_ref.rest_4_), channel_id=1, source_target_pairs={{1,0},{2,1},{3,2},{5,4},{6,5},{7,6},{9,8},{10,9},{11,10},{13,12},{... | collective-permute-start | bytes 2359304 | tf_op jit(solution)/shard_map/ppermute | solution.py:499
  109.5 25.2 %collective-permute-start.2 = (bf16[64,4096]{1,0:T(8,128)(2,1)S(1)}, bf16[64,4096]{1,0:T(8,128)(2,1)S(1)}, u32[]{:S(2)}, u32[]{:S(2)}) collective-permute-start(bf16[64,4096]{1,0:T(8,128)(2,1)S(1)} %copy-done.16), channel_id=1, source_target_pairs={{0,24},{4,28},{8,16},{12,20},{16,8},{20,12},{24,0},{28,4},{1,25},{... | collective-permute-start | bytes 1572872 | tf_op jit(solution)/shard_map/ppermute | solution.py:489
  109.5 25.2 %collective-permute-start.3 = (bf16[64,4096]{1,0:T(8,128)(2,1)S(1)}, bf16[64,4096]{1,0:T(8,128)(2,1)S(1)}, u32[]{:S(2)}, u32[]{:S(2)}) collective-permute-start(bf16[64,4096]{1,0:T(8,128)(2,1)S(1)} %copy-done.16), channel_id=1, source_target_pairs={{0,28},{4,24},{8,20},{12,16},{16,12},{20,8},{24,4},{28,0},{1,29},{... | collective-permute-start | bytes 1572872 | tf_op jit(solution)/shard_map/ppermute | solution.py:489
  116.2 12.2 %collective-permute-start.29 = (f32[1,4096]{1,0:T(1,128)S(1)}, f32[1,4096]{1,0:T(1,128)S(1)}, u32[]{:S(2)}, u32[]{:S(2)}) collective-permute-start(f32[1,4096]{1,0:T(1,128)S(1)} %get-tuple-element.48), channel_id=1, source_target_pairs={{0,4},{4,0},{8,12},{12,8},{1,5},{5,1},{9,13},{13,9},{2,6},{6,2},{1... | collective-permute-start | bytes 49160 | tf_op jit(solution)/shard_map/ppermute | solution.py:483
  128.4 10.4 %collective-permute-start.16 = (bf16[2,64,1024]{2,1,0:T(8,128)(2,1)S(1)}, bf16[2,64,1024]{2,1,0:T(8,128)(2,1)S(1)}, u32[]{:S(2)}, u32[]{:S(2)}) collective-permute-start(bf16[2,64,1024]{2,1,0:T(8,128)(2,1)S(1)} %get-tuple-element.44), channel_id=1, source_target_pairs={{0,3},{1,0},{2,1},{3,2},{4,7},{5,4},{6,5},{7,6},{8,11},{9,8},{10,9... | collective-permute-start | bytes 786440 | tf_op jit(solution)/shard_map/ppermute | solution.py:494
  134.7 20.7 %collective-permute-start.15 = (bf16[2,64,1024]{2,1,0:T(8,128)(2,1)S(1)}, bf16[2,64,1024]{2,1,0:T(8,128)(2,1)S(1)}, u32[]{:S(2)}, u32[]{:S(2)}) collective-permute-start(bf16[2,64,1024]{2,1,0:T(8,128)(2,1)S(1)} %get-tuple-element.43), channel_id=1, source_target_pairs={{0,2},{1,3},{2,0},{3,1},{4,6},{5,7},{6,4},{7,5},{8,10},{9,11},{10,... | collective-permute-start | bytes 786440 | tf_op jit(solution)/shard_map/ppermute | solution.py:494
  134.7 23.4 %collective-permute-start.14 = (bf16[2,64,1024]{2,1,0:T(8,128)(2,1)S(1)}, bf16[2,64,1024]{2,1,0:T(8,128)(2,1)S(1)}, u32[]{:S(2)}, u32[]{:S(2)}) collective-permute-start(bf16[2,64,1024]{2,1,0:T(8,128)(2,1)S(1)} %get-tuple-element.42), channel_id=1, source_target_pairs={{0,1},{1,2},{2,3},{3,0},{4,5},{5,6},{6,7},{7,4},{8,9},{9,10},{10,1... | collective-permute-start | bytes 786440 | tf_op jit(solution)/shard_map/ppermute | solution.py:494
  138.8 15.2 %collective-permute-start.30 = (f32[1,4096]{1,0:T(1,128)S(1)}, f32[1,4096]{1,0:T(1,128)S(1)}, u32[]{:S(2)}, u32[]{:S(2)}) collective-permute-start(f32[1,4096]{1,0:T(1,128)S(1)} %add.28), channel_id=1, source_target_pairs={{0,8},{4,12},{8,0},{12,4},{1,9},{5,13},{9,1},{13,5},{2,10},{6,14},... | collective-permute-start | bytes 49160 | tf_op jit(solution)/shard_map/ppermute | solution.py:483
  140.3 48.7 %collective-permute-start.21 = (bf16[256,1536]{1,0:T(8,128)(2,1)S(1)}, bf16[256,1536]{1,0:T(8,128)(2,1)S(1)}, u32[]{:S(2)}, u32[]{:S(2)}) collective-permute-start(bf16[256,1536]{1,0:T(8,128)(2,1)S(1)} %collective-permute-done.20.rest_5_), channel_id=1, source_target_pairs={{0,1},{1,2},{2,3},{4,5},{5,6},{6,7},{8,9},{9,10},{10,11},{12,13},{... | collective-permute-start | bytes 2359304 | tf_op jit(solution)/shard_map/ppermute | solution.py:499
  141.6 48.8 %collective-permute-start.24 = (bf16[256,1536]{1,0:T(8,128)(2,1)S(1)}, bf16[256,1536]{1,0:T(8,128)(2,1)S(1)}, u32[]{:S(2)}, u32[]{:S(2)}) collective-permute-start(bf16[256,1536]{1,0:T(8,128)(2,1)S(1)} %collective-permute-done.23.rest_8_), channel_id=1, source_target_pairs={{1,0},{2,1},{3,2},{5,4},{6,5},{7,6},{9,8},{10,9},{11,10},{13,12},{... | collective-permute-start | bytes 2359304 | tf_op jit(solution)/shard_map/ppermute | solution.py:499
  154.0 18.7 %collective-permute-start.6 = (bf16[64,4096]{1,0:T(8,128)(2,1)S(1)}, bf16[64,4096]{1,0:T(8,128)(2,1)S(1)}, u32[]{:S(2)}, u32[]{:S(2)}) collective-permute-start(bf16[64,4096]{1,0:T(8,128)(2,1)S(1)} %get-tuple-element.32), channel_id=1, source_target_pairs={{0,12},{4,8},{8,4},{12,0},{1,13},{5,9},{9,5},{13,1},{2,14},{6,10},... | collective-permute-start | bytes 1572872 | tf_op jit(solution)/shard_map/ppermute | solution.py:483
  155.4 15.4 %collective-permute-start.31 = (f32[1,4096]{1,0:T(1,128)S(1)}, f32[1,4096]{1,0:T(1,128)S(1)}, u32[]{:S(2)}, u32[]{:S(2)}) collective-permute-start(f32[1,4096]{1,0:T(1,128)S(1)} %add.29), channel_id=1, source_target_pairs={{0,1},{1,0},{2,3},{3,2},{4,5},{5,4},{6,7},{7,6},{8,9},{9,8},{10,11... | collective-permute-start | bytes 49160 | tf_op jit(solution)/shard_map/ppermute | solution.py:483
  158.1 19.8 %collective-permute-start.5 = (bf16[64,4096]{1,0:T(8,128)(2,1)S(1)}, bf16[64,4096]{1,0:T(8,128)(2,1)S(1)}, u32[]{:S(2)}, u32[]{:S(2)}) collective-permute-start(bf16[64,4096]{1,0:T(8,128)(2,1)S(1)} %get-tuple-element.31), channel_id=1, source_target_pairs={{0,8},{4,12},{8,0},{12,4},{1,9},{5,13},{9,1},{13,5},{2,10},{6,14},... | collective-permute-start | bytes 1572872 | tf_op jit(solution)/shard_map/ppermute | solution.py:483
  170.8 14.8 %collective-permute-start.4 = (bf16[64,4096]{1,0:T(8,128)(2,1)S(1)}, bf16[64,4096]{1,0:T(8,128)(2,1)S(1)}, u32[]{:S(2)}, u32[]{:S(2)}) collective-permute-start(bf16[64,4096]{1,0:T(8,128)(2,1)S(1)} %get-tuple-element.30), channel_id=1, source_target_pairs={{0,4},{4,0},{8,12},{12,8},{1,5},{5,1},{9,13},{13,9},{2,6},{6,2},{1... | collective-permute-start | bytes 1572872 | tf_op jit(solution)/shard_map/ppermute | solution.py:483
  172.7 14.0 %collective-permute-start.32 = (f32[1,4096]{1,0:T(1,128)S(1)}, f32[1,4096]{1,0:T(1,128)S(1)}, u32[]{:S(2)}, u32[]{:S(2)}) collective-permute-start(f32[1,4096]{1,0:T(1,128)S(1)} %add.30), channel_id=1, source_target_pairs={{0,2},{1,3},{2,0},{3,1},{4,6},{5,7},{6,4},{7,5},{8,10},{9,11},{10,... | collective-permute-start | bytes 49160 | tf_op jit(solution)/shard_map/ppermute | solution.py:483
  177.8 30.2 %collective-permute-start.17 = (bf16[4,2,64,1024]{3,2,1,0:T(8,128)(2,1)S(1)}, bf16[4,2,64,1024]{3,2,1,0:T(8,128)(2,1)S(1)}, u32[]{:S(2)}, u32[]{:S(2)}) collective-permute-start(bf16[4,2,64,1024]{3,2,1,0:T(8,128)(2,1)S(1)} %pad_maximum_fusion.rest_0_), channel_id=1, source_target_pairs={{0,4},{4,0},{8,12},{12,8},{1,5},{5,1},{9,13},{13,9},{2,6},{6,2},{1... | collective-permute-start | bytes 3145736 | tf_op jit(solution)/shard_map/ppermute | solution.py:483
  185.6 45.1 %collective-permute-start.18 = (bf16[4,2,64,1024]{3,2,1,0:T(8,128)(2,1)S(1)}, bf16[4,2,64,1024]{3,2,1,0:T(8,128)(2,1)S(1)}, u32[]{:S(2)}, u32[]{:S(2)}) collective-permute-start(bf16[4,2,64,1024]{3,2,1,0:T(8,128)(2,1)S(1)} %pad_maximum_fusion.rest_0_), channel_id=1, source_target_pairs={{0,8},{4,12},{8,0},{12,4},{1,9},{5,13},{9,1},{13,5},{2,10},{6,14},... | collective-permute-start | bytes 3145736 | tf_op jit(solution)/shard_map/ppermute | solution.py:483
  186.7 44.1 %collective-permute-start.19 = (bf16[4,2,64,1024]{3,2,1,0:T(8,128)(2,1)S(1)}, bf16[4,2,64,1024]{3,2,1,0:T(8,128)(2,1)S(1)}, u32[]{:S(2)}, u32[]{:S(2)}) collective-permute-start(bf16[4,2,64,1024]{3,2,1,0:T(8,128)(2,1)S(1)} %pad_maximum_fusion.rest_0_), channel_id=1, source_target_pairs={{0,12},{4,8},{8,4},{12,0},{1,13},{5,9},{9,5},{13,1},{2,14},{6,10},... | collective-permute-start | bytes 3145736 | tf_op jit(solution)/shard_map/ppermute | solution.py:483
  189.0 45.0 %collective-permute-start.22 = (bf16[256,1536]{1,0:T(8,128)(2,1)S(1)}, bf16[256,1536]{1,0:T(8,128)(2,1)S(1)}, u32[]{:S(2)}, u32[]{:S(2)}) collective-permute-start(bf16[256,1536]{1,0:T(8,128)(2,1)S(1)} %collective-permute-done.21.rest_6_), channel_id=1, source_target_pairs={{0,1},{1,2},{2,3},{4,5},{5,6},{6,7},{8,9},{9,10},{10,11},{12,13},{... | collective-permute-start | bytes 2359304 | tf_op jit(solution)/shard_map/ppermute | solution.py:499
  190.5 43.5 %collective-permute-start.25 = (bf16[256,1536]{1,0:T(8,128)(2,1)S(1)}, bf16[256,1536]{1,0:T(8,128)(2,1)S(1)}, u32[]{:S(2)}, u32[]{:S(2)}) collective-permute-start(bf16[256,1536]{1,0:T(8,128)(2,1)S(1)} %collective-permute-done.24.rest_9_), channel_id=1, source_target_pairs={{1,0},{2,1},{3,2},{5,4},{6,5},{7,6},{9,8},{10,9},{11,10},{13,12},{... | collective-permute-start | bytes 2359304 | tf_op jit(solution)/shard_map/ppermute | solution.py:499

commit v2 on v1

v2 whole, which is shorter than its diff:
```python
import functools
import math

import jax
import jax.numpy as jnp
from jax import lax
from jax.experimental import pallas as pl
from jax.experimental.pallas import tpu as pltpu
from jax.sharding import PartitionSpec as P

HD = 128
BLOCK = 128
EPSILON = 1e-05
CHUNK = 512
MIB = 1024 * 1024

BF16 = jnp.bfloat16
F32 = jnp.float32
HBM = pl.BlockSpec(memory_space=pl.ANY)
VMEM = pl.BlockSpec(memory_space=pltpu.VMEM)
SMEM = pl.BlockSpec(memory_space=pltpu.SMEM)


def dot_nn(a, b):
    return lax.dot_general(a, b, (((1,), (0,)), ((), ())), preferred_element_type=F32)


def dot_nt(a, b):
    return lax.dot_general(a, b, (((1,), (1,)), ((), ())), preferred_element_type=F32)


def dot_tn(a, b):
    return lax.dot_general(a, b, (((0,), (0,)), ((), ())), preferred_element_type=F32)


def sds(shape, dtype):
    return jax.ShapeDtypeStruct(shape, dtype)


def params(grid=0):
    semantics = ("arbitrary",) * grid if grid else None
    return pltpu.CompilerParams(vmem_limit_bytes=64 * MIB, dimension_semantics=semantics)


SMALL = pl.CostEstimate(flops=1024, bytes_accessed=1024, transcendentals=0)


def run_copies(copies):
    for copy in copies:
        copy.start()
    for copy in copies:
        copy.wait()


def normalized(rows, gain):
    widened = rows.astype(F32)
    inverse = lax.rsqrt(jnp.mean(widened * widened, axis=-1, keepdims=True) + EPSILON)
    unit = widened * inverse
    return unit, inverse, (unit * gain).astype(BF16)


def seen_pairs(blocks_ref, counts_ref, tokens):
    count, slots = blocks_ref.shape
    row_block = lax.broadcasted_iota(jnp.int32, (tokens, tokens), 0) // BLOCK
    col_block = lax.broadcasted_iota(jnp.int32, (tokens, tokens), 1) // BLOCK
    seen = jnp.zeros((tokens, tokens), jnp.int32)
    for i in range(count):
        for j in range(count):
            flag = jnp.int32(0)
            for t in range(slots):
                listed = (t < counts_ref[i]) & (blocks_ref[i, t] == j)
                flag = flag | listed.astype(jnp.int32)
            seen = jnp.where((row_block == i) & (col_block == j), flag, seen)
    return seen


def soft_scores(query, key, factor, seen):
    scores = dot_nt(query, key) * factor
    scores = jnp.where(seen > 0, scores, -1e30)
    lifted = jnp.exp(scores - jnp.max(scores, axis=-1, keepdims=True))
    return lifted / jnp.sum(lifted, axis=-1, keepdims=True)


def pick_kernel(forward_ref, encoded_ref, grad_ref, head_ref, out_ref, sems):
    section = lax.axis_index("pipe")

    def both(first, second):
        run_copies(
            [
                pltpu.make_async_copy(first, out_ref.at[0], sems.at[0]),
                pltpu.make_async_copy(second, out_ref.at[1], sems.at[1]),
            ]
        )

    @pl.when(section == 0)
    def _():
        both(head_ref, forward_ref)

    @pl.when(section != 0)
    def _():
        both(grad_ref, encoded_ref)


def pick(sent_forward, encoded, grad_sent, head):
    return pl.pallas_call(
        pick_kernel,
        out_shape=sds((2,) + encoded.shape, BF16),
        in_specs=[HBM] * 4,
        scratch_shapes=[pltpu.SemaphoreType.DMA((2,))],
        compiler_params=params(),
        cost_estimate=SMALL,
        name="pick",
    )(sent_forward, encoded, grad_sent, head)


def columns_kernel(x_ref, ins_ref, gain_ref, *rest):
    outs, held = rest[:-1], rest[-1]
    me = lax.axis_index("dp")
    n = len(outs)
    width = outs[0].shape[-1]
    held[...] = normalized(x_ref[...], gain_ref[...])[2]
    for k, out in enumerate(outs):
        start = pl.multiple_of(lax.rem(me + k, n) * width, width)
        out[0] = held[:, pl.ds(start, width)]
        out[1] = ins_ref[0, :, pl.ds(start, width)]


def column_parts(x, ins, gain, n):
    rows, width = x.shape
    part = (2, rows, width // n)
    return pl.pallas_call(
        columns_kernel,
        out_shape=tuple(sds(part, BF16) for _ in range(n)),
        scratch_shapes=[pltpu.VMEM((rows, width), BF16)],
        compiler_params=params(),
        cost_estimate=SMALL,
        name="columns",
    )(x, ins, gain)


def saved_kernel(blocks_ref, counts_ref, factor_ref, q_ref, k_ref, v_ref, *rest):
    soft_ref, att_ref = rest[-2:]
    tokens, width = q_ref.shape
    seen = seen_pairs(blocks_ref, counts_ref, tokens)
    for h in range(width // HD):
        cols = slice(h * HD, (h + 1) * HD)
        soft = soft_scores(q_ref[:, cols], k_ref[:, cols], factor_ref[0, h], seen)
        soft_ref[h] = soft
        att_ref[:, cols] = dot_nn(soft.astype(BF16), v_ref[:, cols]).astype(BF16)


def saved_attention(blocks, counts, factor, q, k, v, after=()):
    tokens, width = q.shape
    heads = width // HD
    return pl.pallas_call(
        saved_kernel,
        out_shape=(sds((heads, tokens, tokens), F32), sds((tokens, width), BF16)),
        in_specs=[SMEM] * 3 + [VMEM] * 3 + [HBM] * len(after),
        compiler_params=params(),
        cost_estimate=SMALL,
        name="saved_attention",
    )(blocks, counts, factor, q, k, v, *after)


def placed(refs, which):
    return [ref.at[which] for ref in refs[:3]] + [refs[3]]


def block_copies(refs, which, held, sems):
    me = lax.axis_index("seq")
    rows = refs[0].shape[1]
    copies = []
    for j, ref in enumerate(refs):
        at = (me ^ min(j, 3)) * rows + (rows // 2 if j == 4 else 0)
        spot = held.at[pl.ds(pl.multiple_of(at, rows // 2), ref.shape[1])]
        copies.append(pltpu.make_async_copy(ref.at[which], spot, sems.at[j]))
    return copies


def split_rows(held, near_ref, far_ref, first, second, cols_in, cols_out):
    me = lax.axis_index("seq")
    rows = near_ref.shape[1]
    for ref, hop in ((near_ref, 0), (far_ref, first)):
        for i, other in enumerate((0, second)):
            at = pl.multiple_of((me ^ hop ^ other) * rows, rows)
            ref[i, :, cols_out] = held[pl.ds(at, rows), cols_in]


def chunk_loads(source, held, sems, rows):
    return [
        pltpu.make_async_copy(
            source.at[pl.ds(i * rows, rows)], held.at[pl.ds(i * rows, rows)], sems.at[i]
        )
        for i in range(source.shape[0] // rows)
    ]


def backward_kernel(n, factor_ref, *rest):
    cots, rest = rest[:n], rest[n:]
    w_ref, soft_in, att_ref, q_ref, k_ref, v_ref, rest = *rest[:6], rest[6:]
    out_ref, held, w, soft_ref, sems, w_sems = rest[-6:]
    rows = cots[0].shape[1]
    tokens, width = q_ref.shape
    copies = block_copies(cots, 0, held, sems)
    for copy in copies:
        copy.start()
    loads = chunk_loads(w_ref, w, w_sems, HD)
    for load in loads:
        load.start()
    load_soft = pltpu.make_async_copy(soft_in, soft_ref, w_sems.at[len(loads)])
    load_soft.start()
    for copy in copies:
        copy.wait()
    for h in range(width // HD):
        loads[h].wait()
        cols = slice(h * HD, (h + 1) * HD)
        cot = dot_nt(held[...], w[cols, :]).astype(BF16)
        if h == 0:
            load_soft.wait()
        soft = soft_ref[h]
        products = cot.astype(F32) * att_ref[:, cols].astype(F32)
        dots = jnp.sum(products, axis=-1, keepdims=True)
        grads = soft * (dot_nt(cot, v_ref[:, cols]) - dots) * factor_ref[0, h]
        grads = grads.astype(BF16)
        low = soft.astype(BF16)
        out_ref[:, h * HD : (h + 1) * HD] = dot_nn(grads, k_ref[:, cols]).astype(BF16)
        key_at = width + h * HD
        out_ref[:, key_at : key_at + HD] = dot_tn(grads, q_ref[:, cols]).astype(BF16)
        value_at = 2 * width + h * HD
        out_ref[:, value_at : value_at + HD] = dot_tn(low, cot).astype(BF16)


def backward_attention(factor, cots, w_out, soft, att, q, k, v, after=()):
    tokens, width = q.shape
    model = w_out.shape[1]
    n = len(cots)
    return pl.pallas_call(
        functools.partial(backward_kernel, n),
        out_shape=sds((tokens, 3 * width), BF16),
        in_specs=[SMEM] + [HBM] * (n + 2) + [VMEM] * 4 + [HBM] * len(after),
        scratch_shapes=[
            pltpu.VMEM((tokens, model), BF16),
            pltpu.VMEM(w_out.shape, BF16),
            pltpu.VMEM(soft.shape, F32),
            pltpu.SemaphoreType.DMA((n,)),
            pltpu.SemaphoreType.DMA((width // HD + 1,)),
        ],
        compiler_params=params(),
        cost_estimate=SMALL,
        name="backward_attention",
    )(factor, *cots, w_out, soft, att, q, k, v, *after)


def input_grad_kernel(n_after, g_ref, *rest):
    weights, rest = rest[:3], rest[3 + n_after :]
    near_ref, far_ref, held, wq, wk, wv, sems = rest
    width = wq.shape[1]
    loads = [
        chunk_loads(source, w, sems.at[i], CHUNK)
        for i, (source, w) in enumerate(zip(weights, (wq, wk, wv)))
    ]
    for group in zip(*loads):
        for load in group:
            load.start()
    for i, group in enumerate(zip(*loads)):
        for load in group:
            load.wait()
        at = slice(i * CHUNK, (i + 1) * CHUNK)
        total = dot_nt(g_ref[:, :width], wq[at, :])
        total += dot_nt(g_ref[:, width : 2 * width], wk[at, :])
        total += dot_nt(g_ref[:, 2 * width :], wv[at, :])
        held[...] = total.astype(BF16)
        split_rows(held, near_ref, far_ref, 1, 2, slice(None), at)


def input_grads(grads, wq, wk, wv, after=()):
    tokens = grads.shape[0]
    model, width = wq.shape
    rows = tokens // 4
    return pl.pallas_call(
        functools.partial(input_grad_kernel, len(after)),
        out_shape=(sds((2, rows, model), BF16),) * 2,
        in_specs=[VMEM] + [HBM] * (3 + len(after)),
        scratch_shapes=[pltpu.VMEM((tokens, CHUNK), BF16)]
        + [pltpu.VMEM(wq.shape, BF16)] * 3
        + [pltpu.SemaphoreType.DMA((3, model // CHUNK))],
        compiler_params=params(),
        cost_estimate=SMALL,
        name="input_grads",
    )(grads, wq, wk, wv, *after)


def forward_kernel(n, n_after, blocks_ref, counts_ref, factor_ref, *rest):
    xs, rest = rest[:n], rest[n:]
    gain_ref, weights, wo_ref = rest[0], rest[1:4], rest[4]
    rest = rest[5 + n_after :]
    near_ref, far_ref, held, wq, wk, wv, wo, tq, tk, tv, att, x_sems, sems = rest
    rows = xs[0].shape[1]
    copies = block_copies(xs, 1, held, x_sems)
    loads = [
        chunk_loads(source, w, sems.at[i], CHUNK)
        for i, (source, w) in enumerate(zip(weights, (wq, wk, wv)))
    ]
    load_wo = pltpu.make_async_copy(wo_ref, wo, x_sems.at[n])
    for copy in copies:
        copy.start()
    for group in zip(*loads):
        for load in group:
            load.start()
    load_wo.start()
    for copy in copies:
        copy.wait()

    @pl.loop(0, held.shape[0] // 32)
    def _(i):
        at = pl.ds(pl.multiple_of(i * 32, 32), 32)
        held[at, :] = normalized(held[at, :], gain_ref[...])[2]

    for i, group in enumerate(zip(*loads)):
        at = slice(i * CHUNK, (i + 1) * CHUNK)
        for load, w, total in zip(group, (wq, wk, wv), (tq, tk, tv)):
            load.wait()
            product = dot_nn(held[:, at], w[at, :])
            total[...] = product if i == 0 else total[...] + product
    tokens, width = tq.shape
    seen = seen_pairs(blocks_ref, counts_ref, tokens)
    for h in range(width // HD):
        cols = slice(h * HD, (h + 1) * HD)
        query, key, value = (t[:, cols].astype(BF16) for t in (tq, tk, tv))
        soft = soft_scores(query, key, factor_ref[0, h], seen)
        att[:, cols] = dot_nn(soft.astype(BF16), value).astype(BF16)
    load_wo.wait()
    for i in range(wo.shape[1] // CHUNK):
        at = slice(i * CHUNK, (i + 1) * CHUNK)
        held[:, at] = dot_nn(att[...], wo[:, at]).astype(BF16)
        split_rows(held, near_ref, far_ref, 1, 2, at, at)


def forward_terms(blocks, counts, factor, xs, gain, wq, wk, wv, wo, after=()):
    n = len(xs)
    _, rows, model = xs[0].shape
    width = wq.shape[1]
    tokens = 4 * rows
    return pl.pallas_call(
        functools.partial(forward_kernel, n, len(after)),
        out_shape=(sds((2, rows, model), BF16),) * 2,
        in_specs=[SMEM] * 3 + [HBM] * n + [VMEM] + [HBM] * (4 + len(after)),
        scratch_shapes=[pltpu.VMEM((tokens, model), BF16)]
        + [pltpu.VMEM(wq.shape, BF16)] * 3
        + [pltpu.VMEM(wo.shape, BF16)]
        + [pltpu.VMEM((tokens, width), F32)] * 3
        + [
            pltpu.VMEM((tokens, width), BF16),
            pltpu.SemaphoreType.DMA((n + 1,)),
            pltpu.SemaphoreType.DMA((3, model // CHUNK)),
        ],
        compiler_params=params(),
        cost_estimate=SMALL,
        name="forward_terms",
    )(blocks, counts, factor, *xs, gain, wq, wk, wv, wo, *after)


def back_kernel(near_ref, came_ref, last_ref, x_ref, ins_ref, gain_ref, *rest):
    back_ref, part_ref = rest[-2:]
    gain = gain_ref[...]
    unit, inverse, _ = normalized(x_ref[...], gain)
    grad = near_ref[0].astype(F32) + came_ref[0].astype(F32) + last_ref[...].astype(F32)
    scaled = gain * grad
    part_ref[...] = jnp.sum(grad * unit, axis=0, keepdims=True)
    inner = jnp.mean(scaled * unit, axis=-1, keepdims=True)
    back_ref[...] = (ins_ref[0].astype(F32) + inverse * (scaled - unit * inner)).astype(BF16)


def back(near, came, last, x, ins, gain, after=()):
    return pl.pallas_call(
        back_kernel,
        out_shape=(sds(x.shape, BF16), sds(gain.shape, F32)),
        in_specs=[VMEM] * 6 + [HBM] * len(after),
        compiler_params=params(),
        cost_estimate=SMALL,
        name="back",
    )(near, came, last, x, ins, gain, *after)


def slice_copies(which, parts, cols, sems):
    seq, dp = lax.axis_index("seq"), lax.axis_index("dp")
    copies = []
    for j, part in enumerate(parts):
        _, n, rows, _ = part.shape
        at = pl.ds(pl.multiple_of((seq ^ j) * rows, rows), rows)
        for k in range(n):
            sample = lax.rem(dp + n - k, n)
            source = part.at[which, k]
            copies.append(pltpu.make_async_copy(source, cols.at[sample, at], sems.at[j, k]))
    return copies


def weight_kernel(n_seq, n_dp, *rest):
    parts, own, rest = rest[:n_seq], rest[n_seq], rest[n_seq + 1 :]
    lower, upper = rest[: n_dp - 1], rest[n_dp - 1 : 2 * n_dp - 2]
    out_q, out_k, out_v, cols, grads, sems, own_sems = rest[-7:]
    me = lax.axis_index("dp")

    def grad_copies(act):
        act(pltpu.make_async_copy(own, grads.at[me], own_sems.at[0]))
        for k in range(1, n_dp):
            spot = grads.at[lax.rem(me + n_dp - k, n_dp)]

            @pl.when(me >= k)
            def _():
                act(pltpu.make_async_copy(lower[k - 1], spot, own_sems.at[k]))

            @pl.when(me < k)
            def _():
                act(pltpu.make_async_copy(upper[n_dp - k - 1], spot, own_sems.at[k]))

    grad_copies(lambda copy: copy.start())
    run_copies(slice_copies(0, parts, cols, sems))
    grad_copies(lambda copy: copy.wait())
    width = out_q.shape[1]
    tile = min(256, out_q.shape[0])
    samples, tokens, _ = cols.shape

    @pl.loop(0, out_q.shape[0] // tile)
    def _(i):
        at = pl.ds(pl.multiple_of(i * tile, tile), tile)
        total = dot_tn(
            cols[:, :, at].reshape(samples * tokens, tile),
            grads[...].reshape(samples * tokens, 3 * width),
        ).astype(BF16)
        for o, out in enumerate((out_q, out_k, out_v)):
            out[at, :] = total[:, o * width : (o + 1) * width]


def out_weight_kernel(n_seq, n_dp, *rest):
    parts, factors_in = rest[:n_seq], rest[n_seq : n_seq + n_dp]
    out_ref, cols, factors, sems, own_sems = rest[-5:]
    dp = lax.axis_index("dp")
    copies = slice_copies(1, parts, cols, sems)
    for k, source in enumerate(factors_in):
        spot = factors.at[lax.rem(dp + n_dp - k, n_dp)]
        copies.append(pltpu.make_async_copy(source, spot, own_sems.at[k]))
    run_copies(copies)
    samples, tokens, slice_width = cols.shape
    tile = 128

    @pl.loop(0, out_ref.shape[0] // tile)
    def _(i):
        at = pl.ds(pl.multiple_of(i * tile, tile), tile)
        out_ref[at, :] = dot_tn(
            factors[:, :, at].reshape(samples * tokens, tile),
            cols[...].reshape(samples * tokens, slice_width),
        ).astype(BF16)


def contracted(kernel, name, parts, factors, out_shape, after=()):
    _, samples, rows, slice_width = parts[0].shape
    tokens, width = factors[0].shape
    return pl.pallas_call(
        functools.partial(kernel, len(parts), samples),
        out_shape=out_shape,
        in_specs=[HBM] * (len(parts) + len(factors) + len(after)),
        scratch_shapes=[
            pltpu.VMEM((samples, len(parts) * rows, slice_width), BF16),
            pltpu.VMEM((samples, tokens, width), BF16),
            pltpu.SemaphoreType.DMA((len(parts), samples)),
            pltpu.SemaphoreType.DMA((samples,)),
        ],
        compiler_params=params(),
        cost_estimate=SMALL,
        name=name,
    )(*parts, *factors, *after)


def weight_grads(parts, own, lower, upper):
    shape = sds((parts[0].shape[3], own.shape[1] // 3), BF16)
    return contracted(weight_kernel, "weight_grads", parts, [own, *lower, *upper], (shape,) * 3)


def out_weight_grads(parts, atts, after=()):
    shape = sds((atts[0].shape[1], parts[0].shape[3]), BF16)
    return contracted(out_weight_kernel, "out_weight_grads", parts, atts, shape, after)


def half_relay_kernel(first_ref, second_ref, *rest):
    for_x, for_y = rest[-2:]
    half = for_x.shape[1]
    for_x[...] = second_ref[:, :half]
    for_y[...] = first_ref[:, half:]


def half_relayed(first, second, after=()):
    pair, rows, model = first.shape
    for_x, for_y = pl.pallas_call(
        half_relay_kernel,
        out_shape=(sds((pair, rows // 2, model), BF16),) * 2,
        in_specs=[VMEM] * 2 + [HBM] * len(after),
        compiler_params=params(),
        cost_estimate=SMALL,
        name="half_relay",
    )(first, second, *after)
    return [swapped(for_x, "seq", 1), swapped(for_y, "seq", 2)], for_x


def stack_kernel(n, *rest):
    out_ref = rest[-1]
    for k in range(n):
        out_ref[:, k] = rest[k][...]


def stacked(parts, after=()):
    n = len(parts)
    pair, rows, width = parts[0].shape
    return pl.pallas_call(
        functools.partial(stack_kernel, n),
        out_shape=sds((pair, n, rows, width), BF16),
        in_specs=[VMEM] * n + [HBM] * len(after),
        compiler_params=params(),
        cost_estimate=SMALL,
        name="stack",
    )(*parts, *after)


def add_kernel(near_ref, came_ref, *rest):
    rest[-1][...] = (near_ref[1].astype(F32) + came_ref[1].astype(F32)).astype(BF16)


def added(near, came, after=()):
    return pl.pallas_call(
        add_kernel,
        out_shape=sds(near.shape[1:], BF16),
        in_specs=[VMEM] * 2 + [HBM] * len(after),
        compiler_params=params(),
        cost_estimate=SMALL,
        name="add",
    )(near, came, *after)


def swapped(value, axis, j):
    return lax.ppermute(value, axis, [(i, i ^ j) for i in range(lax.axis_size(axis))])


def crossed(value, j):
    n = lax.axis_size("seq")
    pairs = [(p * n + i, (1 - p) * n + (i ^ j)) for p in range(2) for i in range(n)]
    return lax.ppermute(value, ("pipe", "seq"), pairs)


def rotated(value, axis, k):
    n = lax.axis_size(axis)
    return lax.ppermute(value, axis, [(i, (i + k) % n) for i in range(n)])


def shifted(value, axis, by):
    n = lax.axis_size(axis)
    return lax.ppermute(value, axis, [(i, i + by) for i in range(n) if 0 <= i + by < n])


def line_gathered(value, axis):
    lower, upper, up, down = [], [], value, value
    for _ in range(lax.axis_size(axis) - 1):
        up, down = shifted(up, axis, 1), shifted(down, axis, -1)
        lower.append(up)
        upper.append(down)
    return lower, upper


def exchanged(parts, axis):
    return [parts[0]] + [rotated(parts[k], axis, k) for k in range(1, len(parts))]


def summed(value, axis):
    hop = 1
    while hop < lax.axis_size(axis):
        value, hop = value + swapped(value, axis, hop), 2 * hop
    return value


def local(
    encoded,
    sent_forward,
    head_cotangent,
    grad_sent,
    x_saved,
    q_saved,
    k_saved,
    v_saved,
    norm_gain,
    logit_scale,
    w_query,
    w_key,
    w_value,
    w_out,
    key_blocks,
    key_counts,
):
    n_dp = lax.axis_size("dp")
    factor = logit_scale / math.sqrt(HD)
    blocks, counts = key_blocks[0], key_counts[0]
    wq, wk, wv, wo = w_query[0], w_key[0], w_value[0], w_out[0]
    q, k, v, x = q_saved[0, 0], k_saved[0, 0], v_saved[0, 0], x_saved[0, 0]

    sent = pick(sent_forward[0, 0], encoded[0], grad_sent[0, 0], head_cotangent[0])
    ins = [crossed(sent, j) for j in range(3)]
    column_sets = column_parts(x, ins[0], norm_gain, n_dp)
    moved = exchanged(column_sets, "dp")
    soft, att = saved_attention(blocks, counts, factor, q, k, v, after=column_sets[:1])
    halves, token = half_relayed(ins[1], ins[2], after=[att, *moved[1:]])
    ins = ins + halves
    atts = exchanged([att] * n_dp, "dp")
    cols = stacked(moved, after=halves + atts[1::2])
    cols = [cols] + [swapped(cols, "seq", j) for j in (1, 2)]

    grads = backward_attention(factor, ins, wo, soft, att, q, k, v, after=[cols[0]])
    lower, upper = line_gathered(grads, "dp")
    dx_near, dx_far = input_grads(grads, wq, wk, wv, after=cols[1:])
    dx_came = swapped(dx_far, "seq", 1)
    cols = cols + [swapped(cols[1], "seq", 2)]
    mix_near, mix_far = forward_terms(
        blocks,
        counts,
        factor,
        ins,
        norm_gain,
        wq,
        wk,
        wv,
        wo,
        after=[dx_near, *cols[1:3], *lower[:1], *upper[:1]],
    )
    mix_came = swapped(mix_far, "seq", 1)
    dx_sum = added(dx_near, dx_came, after=[mix_near])
    dx_last = swapped(dx_sum, "seq", 2)
    grad_out = out_weight_grads(cols, atts, after=[dx_sum, *lower[1:2], *upper[1:2]])
    back_out, gain_part = back(dx_near, dx_came, dx_last, x, ins[0], norm_gain, after=[grad_out])
    mix_sum = added(mix_near, mix_came, after=[back_out, *lower[2:3], *upper[2:3]])
    mix_last = swapped(mix_sum, "seq", 2)

    gain_part = summed(summed(gain_part, "seq"), "dp")
    total = mix_near[0].astype(F32) + mix_came[0].astype(F32) + mix_last.astype(F32)
    forward_out = (ins[0][1].astype(F32) + total).astype(BF16)

    grad_q, grad_k, grad_v = weight_grads(cols, grads, lower, upper)
    return (
        forward_out[None, None],
        back_out[None, None],
        grad_q[None],
        grad_k[None],
        grad_v[None],
        grad_out[None],
        gain_part,
    )


def solution(mesh):
    in_specs = (
        P("dp", "seq", None),
        P("pipe", "dp", "seq", None),
        P("dp", "seq", None),
        P("pipe", "dp", "seq", None),
        P("pipe", "dp", "seq", None),
        P("pipe", "dp", None, "seq"),
        P("pipe", "dp", None, "seq"),
        P("pipe", "dp", None, "seq"),
        P("pipe", None),
        P("pipe", "seq"),
        P("pipe", None, "seq"),
        P("pipe", None, "seq"),
        P("pipe", None, "seq"),
        P("pipe", "seq", None),
        P("dp", None, None),
        P("dp", None),
    )
    out_specs = (
        P("pipe", "dp", "seq", None),
        P("pipe", "dp", "seq", None),
        P("pipe", "dp", "seq"),
        P("pipe", "dp", "seq"),
        P("pipe", "dp", "seq"),
        P("pipe", "seq", "dp"),
        P("pipe", None),
    )
    return jax.shard_map(local, mesh=mesh, in_specs=in_specs, out_specs=out_specs, check_vma=False)
```

time: 240 us -> 179 us (0.75)
  waiting for transfers between devices: 111 us -> 47.9 us
  local copies, waits for them, and re-layouts: 11.4 us -> 0 us
  starting transfers between devices: 45.9 us -> 52.4 us
  other arithmetic: 2.6 us -> 6.47 us
  Pallas kernels: 67.5 us -> 71.2 us
    ppermute x13, waiting for transfers between devices: 86.4 us -> 19 us  [swapped(): lax.ppermute(value, axis, [(i, i ^ j) for i in range(lax.axis_size(axis))])]
    unnamed x34 -> x0, local copies, waits for them, and re-layouts: 11.4 us -> none
    ppermute x6, waiting for transfers between devices: 7.38 us -> 15.4 us  [rotated(): return lax.ppermute(value, axis, [(i, (i + k) % n) for i in range(n)])]
    ppermute x6, starting transfers between devices: 8.81 us -> 14.8 us  [shifted(): lax.ppermute(value, axis, [(i, i + by) for i in range(n) if 0 <= i + by <...]
    ppermute x8 -> x3, waiting for transfers between devices: 17.5 us -> 11.6 us  [crossed(): return lax.ppermute(value, ('pipe', 'seq'), pairs)]
    ppermute x8 -> x3, starting transfers between devices: 7.13 us -> 4.32 us  [crossed(): return lax.ppermute(value, ('pipe', 'seq'), pairs)]
    pallas_call x7 -> x11, Pallas kernels: 65.5 us -> 65.3 us  [the longest x1 15.8 us: forward_terms(): pl.pallas_call(functools.partial(forward_kernel, n, len(after)), out_shap...]
  transfers between devices with their start and end apart: 33 -> 28, of which waited for: 14 -> 13; matrix products, arithmetic and copies ran while one was open for 1% -> 2% of each run, Pallas kernels for 12% -> 35%
where the time goes in v2:
time: 179 us
  Pallas kernels  71.2 us (40%)
  starting transfers between devices  52.4 us (29%)
  waiting for transfers between devices  47.9 us (27%)
  other arithmetic  6.47 us (4%)
    ppermute x13, starting transfers between devices, swapped(): lax.ppermute(value, axis, [(i, i ^ j) for i in range(lax.axis_size(axis))])  19 us
    ppermute x13, waiting for transfers between devices, swapped(): lax.ppermute(value, axis, [(i, i ^ j) for i in range(lax.axis_size(axis))])  19 us
    pallas_call x1, Pallas kernels, forward_terms(): pl.pallas_call(functools.partial(forward_kernel, n, len(after)), out_shap...  15.8 us
    ppermute x6, waiting for transfers between devices, rotated(): return lax.ppermute(value, axis, [(i, (i + k) % n) for i in range(n)])  15.4 us
    ppermute x6, starting transfers between devices, shifted(): lax.ppermute(value, axis, [(i, i + by) for i in range(n) if 0 <= i + by <...  14.8 us
    ppermute x6, starting transfers between devices, rotated(): return lax.ppermute(value, axis, [(i, (i + k) % n) for i in range(n)])  14.2 us
    pallas_call x2, Pallas kernels, contracted(): pl.pallas_call(functools.partial(kernel, len(parts), samples), out_shape=...  13 us
    ppermute x3, waiting for transfers between devices, crossed(): return lax.ppermute(value, ('pipe', 'seq'), pairs)  11.6 us
  transfers between devices with their start and end apart: 28, of which 13 were waited for; matrix products, arithmetic and copies ran while one was open for 2% of the time, Pallas kernels for 35%

profile of v2, /device:TPU:0, one launch (start us, length us, event | category | flops | bytes accessed | tf_op | source)
XLA Modules:
  0.0 178.7 jit_solution(1538018721275070315)
XLA Ops:
  0.6 2.2 %pick.1 = bf16[2,64,4096]{2,1,0:T(8,128)(2,1)} custom-call(bf16[64,4096]{1,0:T(8,128)(2,1)} %bitcast.50, bf16[64,4096]{1,0:T(8,128)(2,1)} %bitcast.51, bf16[64,4096]{1,0:T(8,128)(2,1)} %bitcast.52, bf16[64,4096]{1,0:T(8,128)(2,1)} %bitcast.53), custom_call_target="tpu_custom_call" | custom-call | flops 1024 | bytes 1024 | tf_op jit(solution)/shard_map/pick/pallas_call | solution.py:105
  2.8 0.5 collective-permute-start
  3.4 2.6 %collective-permute-start.1 = (bf16[2,64,4096]{2,1,0:T(8,128)(2,1)}, bf16[2,64,4096]{2,1,0:T(8,128)(2,1)}, u32[]{:S(2)}, u32[]{:S(2)}) collective-permute-start(bf16[2,64,4096]{2,1,0:T(8,128)(2,1)} %pick.1), channel_id=1, source_target_pairs={{0,20},{4,16},{8,28},{12,24},{16,4},{20,0},{24,12},{28,8},{1,21},{... | collective-permute-start | bytes 3145736 | tf_op jit(solution)/shard_map/ppermute | solution.py:546
  6.0 1.2 collective-permute-start.2
  7.2 0.0 collective-permute-done.ins_ref.rest_0_
  7.2 2.7 %columns.1 = (bf16[2,64,1024]{2,1,0:T(8,128)(2,1)}, bf16[2,64,1024]{2,1,0:T(8,128)(2,1)}, bf16[2,64,1024]{2,1,0:T(8,128)(2,1)}, bf16[2,64,1024]{2,1,0:T(8,128)(2,1)}) custom-call(bf16[64,4096]{1,0:T(8,128)(2,1)} %bitcast.41, bf16[2,64,4096]{2,1,0:T(8,128)(2,1)} %collective-permute-done.ins_ref.rest_0_, f32[1,4096]{1,0:T(1,128)} %gain_ref.3), custom_call_target="tpu_custom_call" | custom-call | flops 1024 | bytes 1024 | tf_op jit(solution)/shard_map/columns/pallas_call | solution.py:131
  9.8 1.8 collective-permute-start.3
  11.6 2.6 %collective-permute-start.4 = (bf16[2,64,1024]{2,1,0:T(8,128)(2,1)}, bf16[2,64,1024]{2,1,0:T(8,128)(2,1)}, u32[]{:S(2)}, u32[]{:S(2)}) collective-permute-start(bf16[2,64,1024]{2,1,0:T(8,128)(2,1)} %get-tuple-element.27), channel_id=1, source_target_pairs={{0,2},{1,3},{2,0},{3,1},{4,6},{5,7},{6,4},{7,5},{8,10},{9,11},{10,... | collective-permute-start | bytes 786440 | tf_op jit(solution)/shard_map/ppermute | solution.py:551
  14.2 1.3 collective-permute-start.5
  15.5 1.2 broadcast_multiply_fusion.factor_ref
  16.7 3.2 %saved_attention.1 = (f32[4,256,256]{2,1,0:T(8,128)}, bf16[256,512]{1,0:T(8,128)(2,1)}) custom-call(s32[2,2]{1,0:T(2,128)} %bitcast.54, s32[2]{0:T(128)} %bitcast.56, f32[1,4]{1,0:T(1,128)} %broadcast_multiply_fusion.factor_ref, bf16[256,512]{1,0:T(8,128)(2,1)} %bitcast.43, bf16[256,512]{1,0:T(8,128)(2,1)} %bitcast.45, bf16[256,512]{1,0:T(8,128)(2,1)} %bitcast.47, ...), custom_call_target="tpu_custom_call" | custom-call | flops 1024 | bytes 1024 | tf_op jit(solution)/shard_map/saved_attention/pallas_call | solution.py:155
  19.9 9.9 %collective-permute-done.1.first_ref.rest_1_ = bf16[2,64,4096]{2,1,0:T(8,128)(2,1)} collective-permute-done((bf16[2,64,4096]{2,1,0:T(8,128)(2,1)}, bf16[2,64,4096]{2,1,0:T(8,128)(2,1)}, u32[]{:S(2)}, u32[]{:S(2)}) %collective-permute-start.1) | collective-permute-done | bytes 1048608 | tf_op jit(solution)/shard_map/ppermute | solution.py:546
  29.7 1.8 collective-permute-done.2.second_ref.rest_2_
  31.5 0.5 collective-permute-done.4.rest_2_
  32.0 0.0 collective-permute-done.5.rest_3_
  32.0 2.5 %half_relay.1 = (bf16[2,32,4096]{2,1,0:T(8,128)(2,1)}, bf16[2,32,4096]{2,1,0:T(8,128)(2,1)}) custom-call(bf16[2,64,4096]{2,1,0:T(8,128)(2,1)} %collective-permute-done.1.first_ref.rest_1_, bf16[2,64,4096]{2,1,0:T(8,128)(2,1)} %collective-permute-done.2.second_ref.rest_2_, bf16[256,512]{1,0:T(8,128)(2,1)} %get-tuple-element.25.rest_0_.rest_7_.rest_4_, ...), custom_call_target="tpu_custom_call" | custom-call | flops 1024 | bytes 1024 | tf_op jit(solution)/shard_map/half_relay/pallas_call | solution.py:494
  34.6 1.4 collective-permute-start.6
  35.9 1.5 collective-permute-start.7
  37.5 6.1 %collective-permute-start.8 = (bf16[256,512]{1,0:T(8,128)(2,1)}, bf16[256,512]{1,0:T(8,128)(2,1)}, u32[]{:S(2)}, u32[]{:S(2)}) collective-permute-start(bf16[256,512]{1,0:T(8,128)(2,1)} %get-tuple-element.25.rest_0_.rest_7_.rest_4_), channel_id=1, source_target_pairs={{0,1},{1,2},{2,3},{3,0},{4,5},{5,6},{6,7},{7,4},{8,9},{9,10},{10,1... | collective-permute-start | bytes 786440 | tf_op jit(solution)/shard_map/ppermute | solution.py:551
  43.5 1.0 collective-permute-start.9
  44.6 7.6 %collective-permute-done.8.rest_6_.rest_5_ = bf16[256,512]{1,0:T(8,128)(2,1)} collective-permute-done((bf16[256,512]{1,0:T(8,128)(2,1)}, bf16[256,512]{1,0:T(8,128)(2,1)}, u32[]{:S(2)}, u32[]{:S(2)}) %collective-permute-start.8) | collective-permute-done | bytes 262176 | tf_op jit(solution)/shard_map/ppermute | solution.py:551
  52.2 3.6 %collective-permute-done.9.rest_7_ = bf16[256,512]{1,0:T(8,128)(2,1)} collective-permute-done((bf16[256,512]{1,0:T(8,128)(2,1)}, bf16[256,512]{1,0:T(8,128)(2,1)}, u32[]{:S(2)}, u32[]{:S(2)}) %collective-permute-start.9) | collective-permute-done | bytes 262176 | tf_op jit(solution)/shard_map/ppermute | solution.py:551
  55.8 2.2 %stack.1.rest_11_.rest_0_ = bf16[2,4,64,1024]{3,2,1,0:T(8,128)(2,1)} custom-call(bf16[2,64,1024]{2,1,0:T(8,128)(2,1)} %get-tuple-element.24.rest_0_, bf16[2,64,1024]{2,1,0:T(8,128)(2,1)} %collective-permute-done.3.rest_1_, bf16[2,64,1024]{2,1,0:T(8,128)(2,1)} %collective-permute-done.4.rest_2_, bf16[2,64,1024]{2,1,0:T(8,128)(2,1)} %collective-permute-done.5.rest_3_, ...), custom_call_target="tpu_custom_call" | custom-call | flops 1024 | bytes 1024 | tf_op jit(solution)/shard_map/stack/pallas_call | solution.py:514
  58.0 0.5 collective-permute-start.10
  58.5 0.8 collective-permute-start.11
  59.3 11.6 %backward_attention.1.g_ref.rest_4_ = bf16[256,1536]{1,0:T(8,128)(2,1)} custom-call(f32[1,4]{1,0:T(1,128)} %broadcast_multiply_fusion.factor_ref, bf16[2,64,4096]{2,1,0:T(8,128)(2,1)} %collective-permute-done.ins_ref.rest_0_, bf16[2,64,4096]{2,1,0:T(8,128)(2,1)} %collective-permute-done.1.first_ref.rest_1_, ...), custom_call_target="tpu_custom_call" | custom-call | flops 1024 | bytes 1024 | tf_op jit(solution)/shard_map/backward_attention/pallas_call | solution.py:237
  70.9 3.7 %collective-permute-start.12 = (bf16[256,1536]{1,0:T(8,128)(2,1)}, bf16[256,1536]{1,0:T(8,128)(2,1)}, u32[]{:S(2)}, u32[]{:S(2)}) collective-permute-start(bf16[256,1536]{1,0:T(8,128)(2,1)} %backward_attention.1.g_ref.rest_4_), channel_id=1, source_target_pairs={{0,1},{1,2},{2,3},{4,5},{5,6},{6,7},{8,9},{9,10},{10,11},{12,13},{... | collective-permute-start | bytes 2359304 | tf_op jit(solution)/shard_map/ppermute | solution.py:556
  74.6 1.3 collective-permute-start.13
  75.9 7.5 %collective-permute-done.10.rest_3_.rest_11_.rest_1_ = bf16[2,4,64,1024]{3,2,1,0:T(8,128)(2,1)} collective-permute-done((bf16[2,4,64,1024]{3,2,1,0:T(8,128)(2,1)}, bf16[2,4,64,1024]{3,2,1,0:T(8,128)(2,1)}, u32[]{:S(2)}, u32[]{:S(2)}) %collective-permute-start.10) | collective-permute-done | bytes 1048608 | tf_op jit(solution)/shard_map/ppermute | solution.py:540
  83.3 0.3 collective-permute-done.11.rest_4_.rest_12_.rest_2_
  83.6 9.0 %input_grads.1 = (bf16[2,64,4096]{2,1,0:T(8,128)(2,1)}, bf16[2,64,4096]{2,1,0:T(8,128)(2,1)}) custom-call(bf16[256,1536]{1,0:T(8,128)(2,1)} %backward_attention.1.g_ref.rest_4_, bf16[4096,512]{1,0:T(8,128)(2,1)} %bitcast.34, bf16[4096,512]{1,0:T(8,128)(2,1)} %bitcast.36, bf16[4096,512]{1,0:T(8,128)(2,1)} %bitcast.38, ...), custom_call_target="tpu_custom_call" | custom-call | flops 1024 | bytes 1024 | tf_op jit(solution)/shard_map/input_grads/pallas_call | solution.py:280
  92.6 1.6 collective-permute-start.15
  94.2 0.0 collective-permute-done.12.rest_13_.rest_5_
  94.2 3.4 %collective-permute-start.19 = (bf16[256,1536]{1,0:T(8,128)(2,1)}, bf16[256,1536]{1,0:T(8,128)(2,1)}, u32[]{:S(2)}, u32[]{:S(2)}) collective-permute-start(bf16[256,1536]{1,0:T(8,128)(2,1)} %collective-permute-done.12.rest_13_.rest_5_), channel_id=1, source_target_pairs={{0,1},{1,2},{2,3},{4,5},{5,6},{6,7},{8,9},{9,10},{10,11},{12,13},{... | collective-permute-start | bytes 2359304 | tf_op jit(solution)/shard_map/ppermute | solution.py:556
  97.6 0.0 collective-permute-done.13.rest_14_.rest_8_
  97.6 1.5 collective-permute-start.20
  99.0 0.6 collective-permute-start.17
  99.7 15.8 %forward_terms.1 = (bf16[2,64,4096]{2,1,0:T(8,128)(2,1)}, bf16[2,64,4096]{2,1,0:T(8,128)(2,1)}) custom-call(s32[2,2]{1,0:T(2,128)} %bitcast.55, s32[2]{0:T(128)} %bitcast.57, f32[1,4]{1,0:T(1,128)} %broadcast_multiply_fusion.factor_ref, bf16[2,64,4096]{2,1,0:T(8,128)(2,1)} %collective-permute-done.ins_ref.rest_0_, ...), custom_call_target="tpu_custom_call" | custom-call | flops 1024 | bytes 1024 | tf_op jit(solution)/shard_map/forward_terms/pallas_call | solution.py:344
  115.5 0.8 collective-permute-start.14
  116.2 1.3 collective-permute-start.18
  117.6 1.8 %collective-permute-done.20.rest_10_.rest_9_ = bf16[256,1536]{1,0:T(8,128)(2,1)} collective-permute-done((bf16[256,1536]{1,0:T(8,128)(2,1)}, bf16[256,1536]{1,0:T(8,128)(2,1)}, u32[]{:S(2)}, u32[]{:S(2)}) %collective-permute-start.20) | collective-permute-done | bytes 786464 | tf_op jit(solution)/shard_map/ppermute | solution.py:556
  119.4 3.7 %collective-permute-start.21 = (bf16[256,1536]{1,0:T(8,128)(2,1)}, bf16[256,1536]{1,0:T(8,128)(2,1)}, u32[]{:S(2)}, u32[]{:S(2)}) collective-permute-start(bf16[256,1536]{1,0:T(8,128)(2,1)} %collective-permute-done.19.rest_9_.rest_6_), channel_id=1, source_target_pairs={{0,1},{1,2},{2,3},{4,5},{5,6},{6,7},{8,9},{9,10},{10,11},{12,13},{... | collective-permute-start | bytes 2359304 | tf_op jit(solution)/shard_map/ppermute | solution.py:556
  123.1 0.0 collective-permute-done.15.came_ref
  123.1 1.3 collective-permute-start.22
  124.4 2.5 %add.47.rest_8_ = bf16[64,4096]{1,0:T(8,128)(2,1)} custom-call(bf16[2,64,4096]{2,1,0:T(8,128)(2,1)} %get-tuple-element.32.rest_10_.near_ref, bf16[2,64,4096]{2,1,0:T(8,128)(2,1)} %collective-permute-done.15.came_ref, bf16[2,64,4096]{2,1,0:T(8,128)(2,1)} %get-tuple-element.33.rest_0_.near_ref), custom_call_target="tpu_custom_call" | custom-call | flops 1024 | bytes 1024 | tf_op jit(solution)/shard_map/add/pallas_call | solution.py:529
  126.9 3.7 %collective-permute-done.18.rest_6_ = bf16[256,512]{1,0:T(8,128)(2,1)} collective-permute-done((bf16[256,512]{1,0:T(8,128)(2,1)}, bf16[256,512]{1,0:T(8,128)(2,1)}, u32[]{:S(2)}, u32[]{:S(2)}) %collective-permute-start.18) | collective-permute-done | bytes 262176 | tf_op jit(solution)/shard_map/ppermute | solution.py:551
  130.6 1.7 collective-permute-start.16
  132.3 5.0 %out_weight_grads.1.rest_0_ = bf16[512,1024]{1,0:T(8,128)(2,1)} custom-call(bf16[2,4,64,1024]{3,2,1,0:T(8,128)(2,1)} %stack.1.rest_11_.rest_0_, bf16[2,4,64,1024]{3,2,1,0:T(8,128)(2,1)} %collective-permute-done.10.rest_3_.rest_11_.rest_1_, bf16[2,4,64,1024]{3,2,1,0:T(8,128)(2,1)} %collective-permute-done.11.rest_4_.rest_12_.rest_2_, ...), custom_call_target="tpu_custom_call" | custom-call | flops 1024 | bytes 1024 | tf_op jit(solution)/shard_map/out_weight_grads/pallas_call | solution.py:459
  137.3 3.6 %collective-permute-done.16.last_ref = bf16[64,4096]{1,0:T(8,128)(2,1)} collective-permute-done((bf16[64,4096]{1,0:T(8,128)(2,1)}, bf16[64,4096]{1,0:T(8,128)(2,1)}, u32[]{:S(2)}, u32[]{:S(2)}) %collective-permute-start.16) | collective-permute-done | bytes 524320 | tf_op jit(solution)/shard_map/ppermute | solution.py:540
  140.9 4.1 %back.1 = (bf16[64,4096]{1,0:T(8,128)(2,1)}, f32[1,4096]{1,0:T(1,128)}) custom-call(bf16[2,64,4096]{2,1,0:T(8,128)(2,1)} %get-tuple-element.32.rest_10_.near_ref, bf16[2,64,4096]{2,1,0:T(8,128)(2,1)} %collective-permute-done.15.came_ref, bf16[64,4096]{1,0:T(8,128)(2,1)} %collective-permute-done.16.last_ref, bf16[64,4096]{1,0:T(8,128)(2,1)} %bitcast.42, ...), custom_call_target="tpu_custom_call" | custom-call | flops 1024 | bytes 1024 | tf_op jit(solution)/shard_map/back/pallas_call | solution.py:375
  145.0 2.5 %add.48 = bf16[64,4096]{1,0:T(8,128)(2,1)} custom-call(bf16[2,64,4096]{2,1,0:T(8,128)(2,1)} %get-tuple-element.33.rest_0_.near_ref, bf16[2,64,4096]{2,1,0:T(8,128)(2,1)} %collective-permute-done.14.came_ref, bf16[64,4096]{1,0:T(8,128)(2,1)} %get-tuple-element.36.rest_0_, bf16[256,1536]{1,0:T(8,128)(2,1)} %collective-permute-done.21.rest_1_.rest_7_, ...), custom_call_target="tpu_custom_call" | custom-call | flops 1024 | bytes 1024 | tf_op jit(solution)/shard_map/add/pallas_call | solution.py:529
  147.5 1.7 collective-permute-start.23
  149.2 1.4 collective-permute-start.24
  150.6 2.5 %collective-permute-done.24 = f32[1,4096]{1,0:T(1,128)S(1)} collective-permute-done((f32[1,4096]{1,0:T(1,128)}, f32[1,4096]{1,0:T(1,128)S(1)}, u32[]{:S(2)}, u32[]{:S(2)}) %collective-permute-start.24) | collective-permute-done | bytes 16416 | tf_op jit(solution)/shard_map/ppermute | solution.py:540
  153.2 0.7 add.30
  153.9 0.3 collective-permute-start.25
  154.3 3.5 %collective-permute-done.25 = f32[1,4096]{1,0:T(1,128)S(1)} collective-permute-done((f32[1,4096]{1,0:T(1,128)S(1)}, f32[1,4096]{1,0:T(1,128)S(1)}, u32[]{:S(2)}, u32[]{:S(2)}) %collective-permute-start.25) | collective-permute-done | bytes 16416 | tf_op jit(solution)/shard_map/ppermute | solution.py:540
  157.8 3.5 %collective-permute-start.26 = (f32[1,4096]{1,0:T(1,128)S(1)}, f32[1,4096]{1,0:T(1,128)S(1)}, u32[]{:S(2)}, u32[]{:S(2)}) collective-permute-start(f32[1,4096]{1,0:T(1,128)S(1)} %add.31), channel_id=1, source_target_pairs={{0,1},{1,0},{2,3},{3,2},{4,5},{5,4},{6,7},{7,6},{8,9},{9,8},{10,11... | collective-permute-start | bytes 49160 | tf_op jit(solution)/shard_map/ppermute | solution.py:540
  161.2 1.7 collective-permute-done.26
  162.9 0.6 add.32
  163.5 3.2 %collective-permute-start.27 = (f32[1,4096]{1,0:T(1,128)}, f32[1,4096]{1,0:T(1,128)}, u32[]{:S(2)}, u32[]{:S(2)}) collective-permute-start(f32[1,4096]{1,0:T(1,128)} %add.32), channel_id=1, source_target_pairs={{0,2},{1,3},{2,0},{3,1},{4,6},{5,7},{6,4},{7,5},{8,10},{9,11},{10,... | collective-permute-start | bytes 49160 | tf_op jit(solution)/shard_map/ppermute | solution.py:540
  166.8 8.0 %weight_grads.1 = (bf16[1024,512]{1,0:T(8,128)(2,1)}, bf16[1024,512]{1,0:T(8,128)(2,1)}, bf16[1024,512]{1,0:T(8,128)(2,1)}) custom-call(bf16[2,4,64,1024]{3,2,1,0:T(8,128)(2,1)} %stack.1.rest_11_.rest_0_, bf16[2,4,64,1024]{3,2,1,0:T(8,128)(2,1)} %collective-permute-done.10.rest_3_.rest_11_.rest_1_, ...), custom_call_target="tpu_custom_call" | custom-call | flops 1024 | bytes 1024 | tf_op jit(solution)/shard_map/weight_grads/pallas_call | solution.py:459
  174.7 1.4 add.33
  176.1 2.6 %fusion.1 = bf16[1,1,64,4096]{3,2,1,0:T(8,128)(2,1)} fusion(bf16[64,4096]{1,0:T(8,128)(2,1)} %collective-permute-done.23, bf16[2,64,4096]{2,1,0:T(8,128)(2,1)} %collective-permute-done.14.came_ref, bf16[2,64,4096]{2,1,0:T(8,128)(2,1)} %collective-permute-done.ins_ref.rest_0_, bf16[2,64,4096]{2,1,0:T(8,128)(2,1)} %get-tuple-element.33.rest_0_.near_ref), kind=kLoop, calls=%fused_computation.3 | loop fusion | flops 2097152 | bytes 2621440 | tf_op jit(solution)/shard_map/broadcast_in_dim | solution.py:645
  (11 shorter events, 0.0 us)
Async XLA Ops:
  2.8 4.3 %collective-permute-start = (bf16[2,64,4096]{2,1,0:T(8,128)(2,1)}, bf16[2,64,4096]{2,1,0:T(8,128)(2,1)}, u32[]{:S(2)}, u32[]{:S(2)}) collective-permute-start(bf16[2,64,4096]{2,1,0:T(8,128)(2,1)} %pick.1), channel_id=1, source_target_pairs={{0,16},{4,20},{8,24},{12,28},{16,0},{20,4},{24,8},{28,12},{1,17},{... | collective-permute-start | bytes 3145736 | tf_op jit(solution)/shard_map/ppermute | solution.py:546
  3.4 26.4 %collective-permute-start.1 = (bf16[2,64,4096]{2,1,0:T(8,128)(2,1)}, bf16[2,64,4096]{2,1,0:T(8,128)(2,1)}, u32[]{:S(2)}, u32[]{:S(2)}) collective-permute-start(bf16[2,64,4096]{2,1,0:T(8,128)(2,1)} %pick.1), channel_id=1, source_target_pairs={{0,20},{4,16},{8,28},{12,24},{16,4},{20,0},{24,12},{28,8},{1,21},{... | collective-permute-start | bytes 3145736 | tf_op jit(solution)/shard_map/ppermute | solution.py:546
  6.0 25.5 %collective-permute-start.2 = (bf16[2,64,4096]{2,1,0:T(8,128)(2,1)}, bf16[2,64,4096]{2,1,0:T(8,128)(2,1)}, u32[]{:S(2)}, u32[]{:S(2)}) collective-permute-start(bf16[2,64,4096]{2,1,0:T(8,128)(2,1)} %pick.1), channel_id=1, source_target_pairs={{0,24},{4,28},{8,16},{12,20},{16,8},{20,12},{24,0},{28,4},{1,25},{... | collective-permute-start | bytes 3145736 | tf_op jit(solution)/shard_map/ppermute | solution.py:546
  9.8 21.7 %collective-permute-start.3 = (bf16[2,64,1024]{2,1,0:T(8,128)(2,1)}, bf16[2,64,1024]{2,1,0:T(8,128)(2,1)}, u32[]{:S(2)}, u32[]{:S(2)}) collective-permute-start(bf16[2,64,1024]{2,1,0:T(8,128)(2,1)} %get-tuple-element.26), channel_id=1, source_target_pairs={{0,1},{1,2},{2,3},{3,0},{4,5},{5,6},{6,7},{7,4},{8,9},{9,10},{10,1... | collective-permute-start | bytes 786440 | tf_op jit(solution)/shard_map/ppermute | solution.py:551
  11.6 20.4 %collective-permute-start.4 = (bf16[2,64,1024]{2,1,0:T(8,128)(2,1)}, bf16[2,64,1024]{2,1,0:T(8,128)(2,1)}, u32[]{:S(2)}, u32[]{:S(2)}) collective-permute-start(bf16[2,64,1024]{2,1,0:T(8,128)(2,1)} %get-tuple-element.27), channel_id=1, source_target_pairs={{0,2},{1,3},{2,0},{3,1},{4,6},{5,7},{6,4},{7,5},{8,10},{9,11},{10,... | collective-permute-start | bytes 786440 | tf_op jit(solution)/shard_map/ppermute | solution.py:551
  14.2 17.9 %collective-permute-start.5 = (bf16[2,64,1024]{2,1,0:T(8,128)(2,1)}, bf16[2,64,1024]{2,1,0:T(8,128)(2,1)}, u32[]{:S(2)}, u32[]{:S(2)}) collective-permute-start(bf16[2,64,1024]{2,1,0:T(8,128)(2,1)} %get-tuple-element.28), channel_id=1, source_target_pairs={{0,3},{1,0},{2,1},{3,2},{4,7},{5,4},{6,5},{7,6},{8,11},{9,8},{10,9... | collective-permute-start | bytes 786440 | tf_op jit(solution)/shard_map/ppermute | solution.py:551
  34.6 21.2 %collective-permute-start.6 = (bf16[2,32,4096]{2,1,0:T(8,128)(2,1)}, bf16[2,32,4096]{2,1,0:T(8,128)(2,1)}, u32[]{:S(2)}, u32[]{:S(2)}) collective-permute-start(bf16[2,32,4096]{2,1,0:T(8,128)(2,1)} %get-tuple-element.29), channel_id=1, source_target_pairs={{0,4},{4,0},{8,12},{12,8},{1,5},{5,1},{9,13},{13,9},{2,6},{6,2},{1... | collective-permute-start | bytes 1572872 | tf_op jit(solution)/shard_map/ppermute | solution.py:540
  35.9 19.8 %collective-permute-start.7 = (bf16[2,32,4096]{2,1,0:T(8,128)(2,1)}, bf16[2,32,4096]{2,1,0:T(8,128)(2,1)}, u32[]{:S(2)}, u32[]{:S(2)}) collective-permute-start(bf16[2,32,4096]{2,1,0:T(8,128)(2,1)} %get-tuple-element.30), channel_id=1, source_target_pairs={{0,8},{4,12},{8,0},{12,4},{1,9},{5,13},{9,1},{13,5},{2,10},{6,14},... | collective-permute-start | bytes 1572872 | tf_op jit(solution)/shard_map/ppermute | solution.py:540
  37.5 14.7 %collective-permute-start.8 = (bf16[256,512]{1,0:T(8,128)(2,1)}, bf16[256,512]{1,0:T(8,128)(2,1)}, u32[]{:S(2)}, u32[]{:S(2)}) collective-permute-start(bf16[256,512]{1,0:T(8,128)(2,1)} %get-tuple-element.25.rest_0_.rest_7_.rest_4_), channel_id=1, source_target_pairs={{0,1},{1,2},{2,3},{3,0},{4,5},{5,6},{6,7},{7,4},{8,9},{9,10},{10,1... | collective-permute-start | bytes 786440 | tf_op jit(solution)/shard_map/ppermute | solution.py:551
  43.5 12.2 %collective-permute-start.9 = (bf16[256,512]{1,0:T(8,128)(2,1)}, bf16[256,512]{1,0:T(8,128)(2,1)}, u32[]{:S(2)}, u32[]{:S(2)}) collective-permute-start(bf16[256,512]{1,0:T(8,128)(2,1)} %get-tuple-element.25.rest_0_.rest_7_.rest_4_), channel_id=1, source_target_pairs={{0,3},{1,0},{2,1},{3,2},{4,7},{5,4},{6,5},{7,6},{8,11},{9,8},{10,9... | collective-permute-start | bytes 786440 | tf_op jit(solution)/shard_map/ppermute | solution.py:551
  58.0 25.4 %collective-permute-start.10 = (bf16[2,4,64,1024]{3,2,1,0:T(8,128)(2,1)}, bf16[2,4,64,1024]{3,2,1,0:T(8,128)(2,1)}, u32[]{:S(2)}, u32[]{:S(2)}) collective-permute-start(bf16[2,4,64,1024]{3,2,1,0:T(8,128)(2,1)} %stack.1.rest_11_.rest_0_), channel_id=1, source_target_pairs={{0,4},{4,0},{8,12},{12,8},{1,5},{5,1},{9,13},{13,9},{2,6},{6,2},{1... | collective-permute-start | bytes 3145736 | tf_op jit(solution)/shard_map/ppermute | solution.py:540
  58.5 25.1 %collective-permute-start.11 = (bf16[2,4,64,1024]{3,2,1,0:T(8,128)(2,1)}, bf16[2,4,64,1024]{3,2,1,0:T(8,128)(2,1)}, u32[]{:S(2)}, u32[]{:S(2)}) collective-permute-start(bf16[2,4,64,1024]{3,2,1,0:T(8,128)(2,1)} %stack.1.rest_11_.rest_0_), channel_id=1, source_target_pairs={{0,8},{4,12},{8,0},{12,4},{1,9},{5,13},{9,1},{13,5},{2,10},{6,14},... | collective-permute-start | bytes 3145736 | tf_op jit(solution)/shard_map/ppermute | solution.py:540
  70.9 23.3 %collective-permute-start.12 = (bf16[256,1536]{1,0:T(8,128)(2,1)}, bf16[256,1536]{1,0:T(8,128)(2,1)}, u32[]{:S(2)}, u32[]{:S(2)}) collective-permute-start(bf16[256,1536]{1,0:T(8,128)(2,1)} %backward_attention.1.g_ref.rest_4_), channel_id=1, source_target_pairs={{0,1},{1,2},{2,3},{4,5},{5,6},{6,7},{8,9},{9,10},{10,11},{12,13},{... | collective-permute-start | bytes 2359304 | tf_op jit(solution)/shard_map/ppermute | solution.py:556
  74.6 23.0 %collective-permute-start.13 = (bf16[256,1536]{1,0:T(8,128)(2,1)}, bf16[256,1536]{1,0:T(8,128)(2,1)}, u32[]{:S(2)}, u32[]{:S(2)}) collective-permute-start(bf16[256,1536]{1,0:T(8,128)(2,1)} %backward_attention.1.g_ref.rest_4_), channel_id=1, source_target_pairs={{1,0},{2,1},{3,2},{5,4},{6,5},{7,6},{9,8},{10,9},{11,10},{13,12},{... | collective-permute-start | bytes 2359304 | tf_op jit(solution)/shard_map/ppermute | solution.py:556
  92.6 30.5 %collective-permute-start.15 = (bf16[2,64,4096]{2,1,0:T(8,128)(2,1)}, bf16[2,64,4096]{2,1,0:T(8,128)(2,1)}, u32[]{:S(2)}, u32[]{:S(2)}) collective-permute-start(bf16[2,64,4096]{2,1,0:T(8,128)(2,1)} %get-tuple-element.35), channel_id=1, source_target_pairs={{0,4},{4,0},{8,12},{12,8},{1,5},{5,1},{9,13},{13,9},{2,6},{6,2},{1... | collective-permute-start | bytes 3145736 | tf_op jit(solution)/shard_map/ppermute | solution.py:540
  94.2 22.0 %collective-permute-start.19 = (bf16[256,1536]{1,0:T(8,128)(2,1)}, bf16[256,1536]{1,0:T(8,128)(2,1)}, u32[]{:S(2)}, u32[]{:S(2)}) collective-permute-start(bf16[256,1536]{1,0:T(8,128)(2,1)} %collective-permute-done.12.rest_13_.rest_5_), channel_id=1, source_target_pairs={{0,1},{1,2},{2,3},{4,5},{5,6},{6,7},{8,9},{9,10},{10,11},{12,13},{... | collective-permute-start | bytes 2359304 | tf_op jit(solution)/shard_map/ppermute | solution.py:556
  97.6 21.8 %collective-permute-start.20 = (bf16[256,1536]{1,0:T(8,128)(2,1)}, bf16[256,1536]{1,0:T(8,128)(2,1)}, u32[]{:S(2)}, u32[]{:S(2)}) collective-permute-start(bf16[256,1536]{1,0:T(8,128)(2,1)} %collective-permute-done.13.rest_14_.rest_8_), channel_id=1, source_target_pairs={{1,0},{2,1},{3,2},{5,4},{6,5},{7,6},{9,8},{10,9},{11,10},{13,12},{... | collective-permute-start | bytes 2359304 | tf_op jit(solution)/shard_map/ppermute | solution.py:556
  99.0 33.3 %collective-permute-start.17 = (bf16[2,4,64,1024]{3,2,1,0:T(8,128)(2,1)}, bf16[2,4,64,1024]{3,2,1,0:T(8,128)(2,1)}, u32[]{:S(2)}, u32[]{:S(2)}) collective-permute-start(bf16[2,4,64,1024]{3,2,1,0:T(8,128)(2,1)} %collective-permute-done.10.rest_3_.rest_11_.rest_1_), channel_id=1, source_target_pairs={{0,8},{4,12},{8,0},{12,4},{1,9},{5,13},{9,1},{13,5},{2,10},{6,14},... | collective-permute-start | bytes 3145736 | tf_op jit(solution)/shard_map/ppermute | solution.py:540
  115.5 29.6 %collective-permute-start.14 = (bf16[2,64,4096]{2,1,0:T(8,128)(2,1)}, bf16[2,64,4096]{2,1,0:T(8,128)(2,1)}, u32[]{:S(2)}, u32[]{:S(2)}) collective-permute-start(bf16[2,64,4096]{2,1,0:T(8,128)(2,1)} %get-tuple-element.34), channel_id=1, source_target_pairs={{0,4},{4,0},{8,12},{12,8},{1,5},{5,1},{9,13},{13,9},{2,6},{6,2},{1... | collective-permute-start | bytes 3145736 | tf_op jit(solution)/shard_map/ppermute | solution.py:540
  116.2 14.3 %collective-permute-start.18 = (bf16[256,512]{1,0:T(8,128)(2,1)}, bf16[256,512]{1,0:T(8,128)(2,1)}, u32[]{:S(2)}, u32[]{:S(2)}) collective-permute-start(bf16[256,512]{1,0:T(8,128)(2,1)} %get-tuple-element.25.rest_0_.rest_7_.rest_4_), channel_id=1, source_target_pairs={{0,2},{1,3},{2,0},{3,1},{4,6},{5,7},{6,4},{7,5},{8,10},{9,11},{10,... | collective-permute-start | bytes 786440 | tf_op jit(solution)/shard_map/ppermute | solution.py:551
  119.4 25.7 %collective-permute-start.21 = (bf16[256,1536]{1,0:T(8,128)(2,1)}, bf16[256,1536]{1,0:T(8,128)(2,1)}, u32[]{:S(2)}, u32[]{:S(2)}) collective-permute-start(bf16[256,1536]{1,0:T(8,128)(2,1)} %collective-permute-done.19.rest_9_.rest_6_), channel_id=1, source_target_pairs={{0,1},{1,2},{2,3},{4,5},{5,6},{6,7},{8,9},{9,10},{10,11},{12,13},{... | collective-permute-start | bytes 2359304 | tf_op jit(solution)/shard_map/ppermute | solution.py:556
  123.1 21.9 %collective-permute-start.22 = (bf16[256,1536]{1,0:T(8,128)(2,1)}, bf16[256,1536]{1,0:T(8,128)(2,1)}, u32[]{:S(2)}, u32[]{:S(2)}) collective-permute-start(bf16[256,1536]{1,0:T(8,128)(2,1)} %collective-permute-done.20.rest_10_.rest_9_), channel_id=1, source_target_pairs={{1,0},{2,1},{3,2},{5,4},{6,5},{7,6},{9,8},{10,9},{11,10},{13,12},{... | collective-permute-start | bytes 2359304 | tf_op jit(solution)/shard_map/ppermute | solution.py:556
  130.6 10.4 %collective-permute-start.16 = (bf16[64,4096]{1,0:T(8,128)(2,1)}, bf16[64,4096]{1,0:T(8,128)(2,1)}, u32[]{:S(2)}, u32[]{:S(2)}) collective-permute-start(bf16[64,4096]{1,0:T(8,128)(2,1)} %add.47.rest_8_), channel_id=1, source_target_pairs={{0,8},{4,12},{8,0},{12,4},{1,9},{5,13},{9,1},{13,5},{2,10},{6,14},... | collective-permute-start | bytes 1572872 | tf_op jit(solution)/shard_map/ppermute | solution.py:540
  147.5 28.6 %collective-permute-start.23 = (bf16[64,4096]{1,0:T(8,128)(2,1)}, bf16[64,4096]{1,0:T(8,128)(2,1)}, u32[]{:S(2)}, u32[]{:S(2)}) collective-permute-start(bf16[64,4096]{1,0:T(8,128)(2,1)} %add.48), channel_id=1, source_target_pairs={{0,8},{4,12},{8,0},{12,4},{1,9},{5,13},{9,1},{13,5},{2,10},{6,14},... | collective-permute-start | bytes 1572872 | tf_op jit(solution)/shard_map/ppermute | solution.py:540
  149.2 3.9 %collective-permute-start.24 = (f32[1,4096]{1,0:T(1,128)}, f32[1,4096]{1,0:T(1,128)S(1)}, u32[]{:S(2)}, u32[]{:S(2)}) collective-permute-start(f32[1,4096]{1,0:T(1,128)} %get-tuple-element.40), channel_id=1, source_target_pairs={{0,4},{4,0},{8,12},{12,8},{1,5},{5,1},{9,13},{13,9},{2,6},{6,2},{1... | collective-permute-start | bytes 49160 | tf_op jit(solution)/shard_map/ppermute | solution.py:540
  153.9 3.8 %collective-permute-start.25 = (f32[1,4096]{1,0:T(1,128)S(1)}, f32[1,4096]{1,0:T(1,128)S(1)}, u32[]{:S(2)}, u32[]{:S(2)}) collective-permute-start(f32[1,4096]{1,0:T(1,128)S(1)} %add.30), channel_id=1, source_target_pairs={{0,8},{4,12},{8,0},{12,4},{1,9},{5,13},{9,1},{13,5},{2,10},{6,14},... | collective-permute-start | bytes 49160 | tf_op jit(solution)/shard_map/ppermute | solution.py:540
  157.8 5.2 %collective-permute-start.26 = (f32[1,4096]{1,0:T(1,128)S(1)}, f32[1,4096]{1,0:T(1,128)S(1)}, u32[]{:S(2)}, u32[]{:S(2)}) collective-permute-start(f32[1,4096]{1,0:T(1,128)S(1)} %add.31), channel_id=1, source_target_pairs={{0,1},{1,0},{2,3},{3,2},{4,5},{5,4},{6,7},{7,6},{8,9},{9,8},{10,11... | collective-permute-start | bytes 49160 | tf_op jit(solution)/shard_map/ppermute | solution.py:540
  163.5 11.2 %collective-permute-start.27 = (f32[1,4096]{1,0:T(1,128)}, f32[1,4096]{1,0:T(1,128)}, u32[]{:S(2)}, u32[]{:S(2)}) collective-permute-start(f32[1,4096]{1,0:T(1,128)} %add.32), channel_id=1, source_target_pairs={{0,2},{1,3},{2,0},{3,1},{4,6},{5,7},{6,4},{7,5},{8,10},{9,11},{10,... | collective-permute-start | bytes 49160 | tf_op jit(solution)/shard_map/ppermute | solution.py:540

commit v3 on v2

--- a/solution.py
+++ b/solution.py
@@ -186,178 +186,176 @@
             ref[i, :, cols_out] = held[pl.ds(at, rows), cols_in]
 
 
-def chunk_loads(source, held, sems, rows):
+LOADS = 8
+
+
+def chunk_loads(source, held, sems):
+    rows = source.shape[0] // LOADS
     return [
         pltpu.make_async_copy(
             source.at[pl.ds(i * rows, rows)], held.at[pl.ds(i * rows, rows)], sems.at[i]
         )
-        for i in range(source.shape[0] // rows)
+        for i in range(LOADS)
     ]
+
+
+def start_all(copies):
+    for copy in copies:
+        copy.start()
+
+
+def wait_all(copies):
+    for copy in copies:
+        copy.wait()
 
 
 def backward_kernel(n, factor_ref, *rest):
     cots, rest = rest[:n], rest[n:]
-    w_ref, soft_in, att_ref, q_ref, k_ref, v_ref, rest = *rest[:6], rest[6:]
-    out_ref, held, w, soft_ref, sems, w_sems = rest[-6:]
-    rows = cots[0].shape[1]
-    tokens, width = q_ref.shape
+    soft_in, source, att_ref, q_ref, k_ref, v_ref = rest[:6]
+    out_ref, held, soft_ref, low, wo, sems, soft_sem, w_sems = rest[-8:]
+    width = q_ref.shape[1]
     copies = block_copies(cots, 0, held, sems)
-    for copy in copies:
-        copy.start()
-    loads = chunk_loads(w_ref, w, w_sems, HD)
-    for load in loads:
-        load.start()
-    load_soft = pltpu.make_async_copy(soft_in, soft_ref, w_sems.at[len(loads)])
+    loads = chunk_loads(source, wo, w_sems)
+    load_soft = pltpu.make_async_copy(soft_in, soft_ref, soft_sem.at[0])
+    start_all(copies)
+    start_all(loads)
+    wait_all(copies)
     load_soft.start()
-    for copy in copies:
-        copy.wait()
+    wait_all(loads)
+    low[...] = dot_nt(held[...], wo[...]).astype(BF16)
+    load_soft.wait()
     for h in range(width // HD):
-        loads[h].wait()
         cols = slice(h * HD, (h + 1) * HD)
-        cot = dot_nt(held[...], w[cols, :]).astype(BF16)
-        if h == 0:
-            load_soft.wait()
+        cot = low[:, cols]
         soft = soft_ref[h]
         products = cot.astype(F32) * att_ref[:, cols].astype(F32)
         dots = jnp.sum(products, axis=-1, keepdims=True)
         grads = soft * (dot_nt(cot, v_ref[:, cols]) - dots) * factor_ref[0, h]
         grads = grads.astype(BF16)
-        low = soft.astype(BF16)
+        soft = soft.astype(BF16)
         out_ref[:, h * HD : (h + 1) * HD] = dot_nn(grads, k_ref[:, cols]).astype(BF16)
         key_at = width + h * HD
         out_ref[:, key_at : key_at + HD] = dot_tn(grads, q_ref[:, cols]).astype(BF16)
         value_at = 2 * width + h * HD
-        out_ref[:, value_at : value_at + HD] = dot_tn(low, cot).astype(BF16)
-
-
-def backward_attention(factor, cots, w_out, soft, att, q, k, v, after=()):
+        out_ref[:, value_at : value_at + HD] = dot_tn(soft, cot).astype(BF16)
+
+
+def backward_attention(factor, cots, soft, wo, att, q, k, v, after=()):
     tokens, width = q.shape
-    model = w_out.shape[1]
     n = len(cots)
     return pl.pallas_call(
         functools.partial(backward_kernel, n),
         out_shape=sds((tokens, 3 * width), BF16),
         in_specs=[SMEM] + [HBM] * (n + 2) + [VMEM] * 4 + [HBM] * len(after),
         scratch_shapes=[
-            pltpu.VMEM((tokens, model), BF16),
-            pltpu.VMEM(w_out.shape, BF16),
+            pltpu.VMEM((tokens, wo.shape[1]), BF16),
             pltpu.VMEM(soft.shape, F32),
+            pltpu.VMEM((tokens, width), BF16),
+            pltpu.VMEM(wo.shape, BF16),
             pltpu.SemaphoreType.DMA((n,)),
-            pltpu.SemaphoreType.DMA((width // HD + 1,)),
+            pltpu.SemaphoreType.DMA((1,)),
+            pltpu.SemaphoreType.DMA((LOADS,)),
         ],
         compiler_params=params(),
         cost_estimate=SMALL,
         name="backward_attention",
-    )(factor, *cots, w_out, soft, att, q, k, v, *after)
-
-
-def input_grad_kernel(n_after, g_ref, *rest):
-    weights, rest = rest[:3], rest[3 + n_after :]
-    near_ref, far_ref, held, wq, wk, wv, sems = rest
-    width = wq.shape[1]
-    loads = [
-        chunk_loads(source, w, sems.at[i], CHUNK)
-        for i, (source, w) in enumerate(zip(weights, (wq, wk, wv)))
-    ]
-    for group in zip(*loads):
-        for load in group:
-            load.start()
-    for i, group in enumerate(zip(*loads)):
-        for load in group:
-            load.wait()
-        at = slice(i * CHUNK, (i + 1) * CHUNK)
+    )(factor, *cots, soft, wo, att, q, k, v, *after)
+
+
+def input_grad_kernel(g_ref, *rest):
+    near_ref, far_ref, tile, wq, wk, wv, sems = rest[-7:]
+    rows, width = wq.shape[0] // LOADS, wq.shape[1]
+    groups = list(
+        zip(*(chunk_loads(rest[i], w, sems.at[i]) for i, w in enumerate((wq, wk, wv))))
+    )
+    for group in groups[:3]:
+        start_all(group)
+    for i, group in enumerate(groups):
+        wait_all(group)
+        if i + 3 < LOADS:
+            start_all(groups[i + 3])
+        at = slice(i * rows, (i + 1) * rows)
         total = dot_nt(g_ref[:, :width], wq[at, :])
         total += dot_nt(g_ref[:, width : 2 * width], wk[at, :])
         total += dot_nt(g_ref[:, 2 * width :], wv[at, :])
-        held[...] = total.astype(BF16)
-        split_rows(held, near_ref, far_ref, 1, 2, slice(None), at)
+        tile[...] = total.astype(BF16)
+        split_rows(tile, near_ref, far_ref, 1, 2, slice(None), at)
 
 
 def input_grads(grads, wq, wk, wv, after=()):
     tokens = grads.shape[0]
-    model, width = wq.shape
-    rows = tokens // 4
-    return pl.pallas_call(
-        functools.partial(input_grad_kernel, len(after)),
-        out_shape=(sds((2, rows, model), BF16),) * 2,
+    model = wq.shape[0]
+    return pl.pallas_call(
+        input_grad_kernel,
+        out_shape=(sds((2, tokens // 4, model), BF16),) * 2,
         in_specs=[VMEM] + [HBM] * (3 + len(after)),
-        scratch_shapes=[pltpu.VMEM((tokens, CHUNK), BF16)]
+        scratch_shapes=[pltpu.VMEM((tokens, model // LOADS), BF16)]
         + [pltpu.VMEM(wq.shape, BF16)] * 3
-        + [pltpu.SemaphoreType.DMA((3, model // CHUNK))],
+        + [pltpu.SemaphoreType.DMA((3, LOADS))],
         compiler_params=params(),
         cost_estimate=SMALL,
         name="input_grads",
     )(grads, wq, wk, wv, *after)
 
 
-def forward_kernel(n, n_after, blocks_ref, counts_ref, factor_ref, *rest):
+def forward_kernel(n, blocks_ref, counts_ref, factor_ref, *rest):
     xs, rest = rest[:n], rest[n:]
-    gain_ref, weights, wo_ref = rest[0], rest[1:4], rest[4]
-    rest = rest[5 + n_after :]
-    near_ref, far_ref, held, wq, wk, wv, wo, tq, tk, tv, att, x_sems, sems = rest
-    rows = xs[0].shape[1]
-    copies = block_copies(xs, 1, held, x_sems)
+    gain_ref, sources = rest[0], rest[1:5]
+    near_ref, far_ref, held, low, att, wq, wk, wv, wo, sems, w_sems = rest[-11:]
+    copies = block_copies(xs, 1, held, sems)
     loads = [
-        chunk_loads(source, w, sems.at[i], CHUNK)
-        for i, (source, w) in enumerate(zip(weights, (wq, wk, wv)))
+        chunk_loads(source, w, w_sems.at[i])
+        for i, (source, w) in enumerate(zip(sources, (wq, wk, wv, wo)))
     ]
-    load_wo = pltpu.make_async_copy(wo_ref, wo, x_sems.at[n])
-    for copy in copies:
-        copy.start()
-    for group in zip(*loads):
-        for load in group:
-            load.start()
-    load_wo.start()
-    for copy in copies:
-        copy.wait()
-
-    @pl.loop(0, held.shape[0] // 32)
+    start_all(copies)
+    start_all(loads[0])
+    wait_all(copies)
+    tokens = held.shape[0]
+    width = wq.shape[1]
+
+    @pl.loop(0, tokens // 32)
     def _(i):
         at = pl.ds(pl.multiple_of(i * 32, 32), 32)
         held[at, :] = normalized(held[at, :], gain_ref[...])[2]
 
-    for i, group in enumerate(zip(*loads)):
-        at = slice(i * CHUNK, (i + 1) * CHUNK)
-        for load, w, total in zip(group, (wq, wk, wv), (tq, tk, tv)):
-            load.wait()
-            product = dot_nn(held[:, at], w[at, :])
-            total[...] = product if i == 0 else total[...] + product
-    tokens, width = tq.shape
+    for i, w in enumerate((wq, wk, wv)):
+        start_all(loads[i + 1])
+        wait_all(loads[i])
+        low[:, i * width : (i + 1) * width] = dot_nn(held[...], w[...]).astype(BF16)
     seen = seen_pairs(blocks_ref, counts_ref, tokens)
     for h in range(width // HD):
-        cols = slice(h * HD, (h + 1) * HD)
-        query, key, value = (t[:, cols].astype(BF16) for t in (tq, tk, tv))
+        query, key, value = (
+            low[:, i * width + h * HD : i * width + (h + 1) * HD] for i in range(3)
+        )
         soft = soft_scores(query, key, factor_ref[0, h], seen)
-        att[:, cols] = dot_nn(soft.astype(BF16), value).astype(BF16)
-    load_wo.wait()
+        att[:, h * HD : (h + 1) * HD] = dot_nn(soft.astype(BF16), value).astype(BF16)
+    wait_all(loads[3])
     for i in range(wo.shape[1] // CHUNK):
         at = slice(i * CHUNK, (i + 1) * CHUNK)
         held[:, at] = dot_nn(att[...], wo[:, at]).astype(BF16)
         split_rows(held, near_ref, far_ref, 1, 2, at, at)
 
 
-def forward_terms(blocks, counts, factor, xs, gain, wq, wk, wv, wo, after=()):
+def forward_terms(blocks, counts, factor, xs, gain, weights, after=()):
     n = len(xs)
     _, rows, model = xs[0].shape
-    width = wq.shape[1]
+    width = weights[0].shape[1]
     tokens = 4 * rows
     return pl.pallas_call(
-        functools.partial(forward_kernel, n, len(after)),
+        functools.partial(forward_kernel, n),
         out_shape=(sds((2, rows, model), BF16),) * 2,
         in_specs=[SMEM] * 3 + [HBM] * n + [VMEM] + [HBM] * (4 + len(after)),
-        scratch_shapes=[pltpu.VMEM((tokens, model), BF16)]
-        + [pltpu.VMEM(wq.shape, BF16)] * 3
-        + [pltpu.VMEM(wo.shape, BF16)]
-        + [pltpu.VMEM((tokens, width), F32)] * 3
-        + [
+        scratch_shapes=[
+            pltpu.VMEM((tokens, model), BF16),
+            pltpu.VMEM((tokens, 3 * width), BF16),
             pltpu.VMEM((tokens, width), BF16),
-            pltpu.SemaphoreType.DMA((n + 1,)),
-            pltpu.SemaphoreType.DMA((3, model // CHUNK)),
-        ],
+        ]
+        + [pltpu.VMEM(w.shape, BF16) for w in weights]
+        + [pltpu.SemaphoreType.DMA((n,)), pltpu.SemaphoreType.DMA((4, LOADS))],
         compiler_params=params(),
         cost_estimate=SMALL,
         name="forward_terms",
-    )(blocks, counts, factor, *xs, gain, wq, wk, wv, wo, *after)
+    )(blocks, counts, factor, *xs, gain, *weights, *after)
 
 
 def back_kernel(near_ref, came_ref, last_ref, x_ref, ins_ref, gain_ref, *rest):
@@ -472,9 +470,10 @@
     )(*parts, *factors, *after)
 
 
-def weight_grads(parts, own, lower, upper):
+def weight_grads(parts, own, lower, upper, after=()):
     shape = sds((parts[0].shape[3], own.shape[1] // 3), BF16)
-    return contracted(weight_kernel, "weight_grads", parts, [own, *lower, *upper], (shape,) * 3)
+    factors = [own, *lower, *upper]
+    return contracted(weight_kernel, "weight_grads", parts, factors, (shape,) * 3, after)
 
 
 def out_weight_grads(parts, atts, after=()):
@@ -483,10 +482,14 @@
 
 
 def half_relay_kernel(first_ref, second_ref, *rest):
-    for_x, for_y = rest[-2:]
+    for_x, for_y, sems = rest[-3:]
     half = for_x.shape[1]
-    for_x[...] = second_ref[:, :half]
-    for_y[...] = first_ref[:, half:]
+    run_copies(
+        [
+            pltpu.make_async_copy(second_ref.at[:, pl.ds(0, half)], for_x, sems.at[0]),
+            pltpu.make_async_copy(first_ref.at[:, pl.ds(half, half)], for_y, sems.at[1]),
+        ]
+    )
 
 
 def half_relayed(first, second, after=()):
@@ -494,7 +497,8 @@
     for_x, for_y = pl.pallas_call(
         half_relay_kernel,
         out_shape=(sds((pair, rows // 2, model), BF16),) * 2,
-        in_specs=[VMEM] * 2 + [HBM] * len(after),
+        in_specs=[HBM] * (2 + len(after)),
+        scratch_shapes=[pltpu.SemaphoreType.DMA((2,))],
         compiler_params=params(),
         cost_estimate=SMALL,
         name="half_relay",
@@ -503,9 +507,8 @@
 
 
 def stack_kernel(n, *rest):
-    out_ref = rest[-1]
-    for k in range(n):
-        out_ref[:, k] = rest[k][...]
+    out_ref, sems = rest[-2:]
+    run_copies([pltpu.make_async_copy(rest[k], out_ref.at[:, k], sems.at[k]) for k in range(n)])
 
 
 def stacked(parts, after=()):
@@ -514,7 +517,8 @@
     return pl.pallas_call(
         functools.partial(stack_kernel, n),
         out_shape=sds((pair, n, rows, width), BF16),
-        in_specs=[VMEM] * n + [HBM] * len(after),
+        in_specs=[HBM] * (n + len(after)),
+        scratch_shapes=[pltpu.SemaphoreType.DMA((n,))],
         compiler_params=params(),
         cost_estimate=SMALL,
         name="stack",
@@ -522,18 +526,63 @@
 
 
 def add_kernel(near_ref, came_ref, *rest):
-    rest[-1][...] = (near_ref[1].astype(F32) + came_ref[1].astype(F32)).astype(BF16)
+    out_ref, near, came, sems = rest[-4:]
+    run_copies(
+        [
+            pltpu.make_async_copy(near_ref.at[1], near, sems.at[0]),
+            pltpu.make_async_copy(came_ref.at[1], came, sems.at[1]),
+        ]
+    )
+    out_ref[...] = (near[...].astype(F32) + came[...].astype(F32)).astype(BF16)
 
 
 def added(near, came, after=()):
+    shape = near.shape[1:]
     return pl.pallas_call(
         add_kernel,
-        out_shape=sds(near.shape[1:], BF16),
-        in_specs=[VMEM] * 2 + [HBM] * len(after),
+        out_shape=sds(shape, BF16),
+        in_specs=[HBM] * (2 + len(after)),
+        scratch_shapes=[
+            pltpu.VMEM(shape, BF16),
+            pltpu.VMEM(shape, BF16),
+            pltpu.SemaphoreType.DMA((2,)),
+        ],
         compiler_params=params(),
         cost_estimate=SMALL,
         name="add",
     )(near, came, *after)
+
+
+def passed_kernel(value_ref, *rest):
+    out_ref, sems = rest[-2:]
+    run_copies([pltpu.make_async_copy(value_ref, out_ref, sems.at[0])])
+
+
+def passed(value, after):
+    return pl.pallas_call(
+        passed_kernel,
+        out_shape=sds(value.shape, value.dtype),
+        in_specs=[HBM] * (1 + len(after)),
+        scratch_shapes=[pltpu.SemaphoreType.DMA((1,))],
+        compiler_params=params(),
+        cost_estimate=SMALL,
+        name="passed",
+    )(value, *after)
+
+
+def gain_kernel(own_ref, came_ref, *rest):
+    rest[-1][...] = own_ref[...] + came_ref[...]
+
+
+def gain_added(own, came, after=()):
+    return pl.pallas_call(
+        gain_kernel,
+        out_shape=sds(own.shape, F32),
+        in_specs=[VMEM] * 2 + [HBM] * len(after),
+        compiler_params=params(),
+        cost_estimate=SMALL,
+        name="gain_added",
+    )(own, came, *after)
 
 
 def swapped(value, axis, j):
@@ -570,8 +619,11 @@
 
 
 def summed(value, axis):
+    n = lax.axis_size(axis)
+    if n <= 4:
+        return sum((rotated(value, axis, k) for k in range(1, n)), value)
     hop = 1
-    while hop < lax.axis_size(axis):
+    while hop < n:
         value, hop = value + swapped(value, axis, hop), 2 * hop
     return value
 
@@ -608,12 +660,13 @@
     halves, token = half_relayed(ins[1], ins[2], after=[att, *moved[1:]])
     ins = ins + halves
     atts = exchanged([att] * n_dp, "dp")
-    cols = stacked(moved, after=halves + atts[1::2])
+    cols = stacked(moved, after=halves + atts[1:2])
     cols = [cols] + [swapped(cols, "seq", j) for j in (1, 2)]
 
-    grads = backward_attention(factor, ins, wo, soft, att, q, k, v, after=[cols[0]])
+    grads = backward_attention(factor, ins, soft, wo, att, q, k, v, after=[cols[0]])
     lower, upper = line_gathered(grads, "dp")
-    dx_near, dx_far = input_grads(grads, wq, wk, wv, after=cols[1:])
+    dx_near, dx_far = input_grads(grads, wq, wk, wv)
+    dx_far = passed(dx_far, after=cols[1:])
     dx_came = swapped(dx_far, "seq", 1)
     cols = cols + [swapped(cols[1], "seq", 2)]
     mix_near, mix_far = forward_terms(
@@ -622,25 +675,25 @@
         factor,
         ins,
         norm_gain,
-        wq,
-        wk,
-        wv,
-        wo,
-        after=[dx_near, *cols[1:3], *lower[:1], *upper[:1]],
+        (wq, wk, wv, wo),
+        after=[dx_far, *lower[:1], *upper[:1]],
     )
     mix_came = swapped(mix_far, "seq", 1)
     dx_sum = added(dx_near, dx_came, after=[mix_near])
     dx_last = swapped(dx_sum, "seq", 2)
-    grad_out = out_weight_grads(cols, atts, after=[dx_sum, *lower[1:2], *upper[1:2]])
-    back_out, gain_part = back(dx_near, dx_came, dx_last, x, ins[0], norm_gain, after=[grad_out])
+    back_out, gain_part = back(dx_near, dx_came, dx_last, x, ins[0], norm_gain, after=[cols[3], *lower[1:2], *upper[1:2]])
     mix_sum = added(mix_near, mix_came, after=[back_out, *lower[2:3], *upper[2:3]])
     mix_last = swapped(mix_sum, "seq", 2)
 
-    gain_part = summed(summed(gain_part, "seq"), "dp")
+    gain_part = gain_added(gain_part, swapped(gain_part, "seq", 1), after=[mix_sum])
+    gain_hop = swapped(gain_part, "seq", 2)
+    grad_q, grad_k, grad_v = weight_grads(cols, grads, lower, upper, after=[gain_part])
+    gain_part = gain_added(gain_part, gain_hop, after=[grad_q, mix_last])
+    grad_out = out_weight_grads(cols, atts, after=[gain_part])
+    gain_part = summed(gain_part, "dp")
     total = mix_near[0].astype(F32) + mix_came[0].astype(F32) + mix_last.astype(F32)
     forward_out = (ins[0][1].astype(F32) + total).astype(BF16)
 
-    grad_q, grad_k, grad_v = weight_grads(cols, grads, lower, upper)
     return (
         forward_out[None, None],
         back_out[None, None],

time: 179 us -> 166 us (0.927)
  waiting for transfers between devices: 47.9 us -> 31.3 us
  starting transfers between devices: 52.4 us -> 59.3 us
  Pallas kernels: 71.2 us -> 68.6 us
    ppermute x6, starting transfers between devices: 14.8 us -> 23.8 us  [shifted(): lax.ppermute(value, axis, [(i, i + by) for i in range(n) if 0 <= i + by <...]
    ppermute x6 -> x9, waiting for transfers between devices: 15.4 us -> 7.1 us  [rotated(): return lax.ppermute(value, axis, [(i, (i + k) % n) for i in range(n)])]
    ppermute x13 -> x11, waiting for transfers between devices: 19 us -> 12 us  [swapped(): lax.ppermute(value, axis, [(i, i ^ j) for i in range(lax.axis_size(axis))])]
    ppermute x13 -> x11, starting transfers between devices: 19 us -> 12.7 us  [swapped(): lax.ppermute(value, axis, [(i, i ^ j) for i in range(lax.axis_size(axis))])]
    ppermute x6 -> x9, starting transfers between devices: 14.2 us -> 18.5 us  [rotated(): return lax.ppermute(value, axis, [(i, (i + k) % n) for i in range(n)])]
    pallas_call x1, Pallas kernels: 11.6 us -> 7.64 us  [backward_attention(): pl.pallas_call(functools.partial(backward_kernel, n), out_shape=sds((toke...]
    pallas_call x4 -> x7, Pallas kernels: 29.7 us -> 31.5 us  [the longest x1 13.3 us: forward_terms(): pl.pallas_call(functools.partial(forward_kernel, n), out_shape=(sds((2, r...]
  transfers between devices with their start and end apart: 28 -> 29, of which waited for: 13 -> 7; matrix products, arithmetic and copies ran while one was open for 2% -> 2% of each run, Pallas kernels for 35% -> 36%
where the time goes in v3:
time: 166 us; the launch traced here: 165 us
  Pallas kernels  68.6 us (41%)
  starting transfers between devices  59.3 us (36%)
  waiting for transfers between devices  31.3 us (19%)
  other arithmetic  5.14 us (3%)
    ppermute x6, starting transfers between devices, shifted(): lax.ppermute(value, axis, [(i, i + by) for i in range(n) if 0 <= i + by <...  23.8 us
    ppermute x9, starting transfers between devices, rotated(): return lax.ppermute(value, axis, [(i, (i + k) % n) for i in range(n)])  18.5 us
    pallas_call x1, Pallas kernels, forward_terms(): pl.pallas_call(functools.partial(forward_kernel, n), out_shape=(sds((2, r...  13.3 us
    pallas_call x2, Pallas kernels, contracted(): pl.pallas_call(functools.partial(kernel, len(parts), samples), out_shape=...  13 us
    ppermute x11, starting transfers between devices, swapped(): lax.ppermute(value, axis, [(i, i ^ j) for i in range(lax.axis_size(axis))])  12.7 us
    ppermute x11, waiting for transfers between devices, swapped(): lax.ppermute(value, axis, [(i, i ^ j) for i in range(lax.axis_size(axis))])  12 us
    ppermute x3, waiting for transfers between devices, crossed(): return lax.ppermute(value, ('pipe', 'seq'), pairs)  11.6 us
    pallas_call x1, Pallas kernels, input_grads(): pl.pallas_call(input_grad_kernel, out_shape=(sds((2, tokens // 4, model),...  9.05 us
  transfers between devices with their start and end apart: 29, of which 7 were waited for; matrix products, arithmetic and copies ran while one was open for 2% of the time, Pallas kernels for 36%

profile of v3, /device:TPU:0, one launch (start us, length us, event | category | flops | bytes accessed | tf_op | source)
XLA Modules:
  0.0 165.2 jit_solution(2027075403175532333)
XLA Ops:
  0.6 2.2 %pick.1 = bf16[2,64,4096]{2,1,0:T(8,128)(2,1)} custom-call(bf16[64,4096]{1,0:T(8,128)(2,1)} %bitcast.51, bf16[64,4096]{1,0:T(8,128)(2,1)} %bitcast.52, bf16[64,4096]{1,0:T(8,128)(2,1)} %bitcast.53, bf16[64,4096]{1,0:T(8,128)(2,1)} %bitcast.54), custom_call_target="tpu_custom_call" | custom-call | flops 1024 | bytes 1024 | tf_op jit(solution)/shard_map/pick/pallas_call | solution.py:105
  2.8 0.5 collective-permute-start
  3.4 2.6 %collective-permute-start.1 = (bf16[2,64,4096]{2,1,0:T(8,128)(2,1)}, bf16[2,64,4096]{2,1,0:T(8,128)(2,1)}, u32[]{:S(2)}, u32[]{:S(2)}) collective-permute-start(bf16[2,64,4096]{2,1,0:T(8,128)(2,1)} %pick.1), channel_id=1, source_target_pairs={{0,20},{4,16},{8,28},{12,24},{16,4},{20,0},{24,12},{28,8},{1,21},{... | collective-permute-start | bytes 3145736 | tf_op jit(solution)/shard_map/ppermute | solution.py:595
  6.0 1.2 collective-permute-start.2
  7.2 0.0 collective-permute-done.ins_ref.rest_0_
  7.2 2.7 %columns.1 = (bf16[2,64,1024]{2,1,0:T(8,128)(2,1)}, bf16[2,64,1024]{2,1,0:T(8,128)(2,1)}, bf16[2,64,1024]{2,1,0:T(8,128)(2,1)}, bf16[2,64,1024]{2,1,0:T(8,128)(2,1)}) custom-call(bf16[64,4096]{1,0:T(8,128)(2,1)} %bitcast.40, bf16[2,64,4096]{2,1,0:T(8,128)(2,1)} %collective-permute-done.ins_ref.rest_0_, f32[1,4096]{1,0:T(1,128)} %gain_ref.3), custom_call_target="tpu_custom_call" | custom-call | flops 1024 | bytes 1024 | tf_op jit(solution)/shard_map/columns/pallas_call | solution.py:131
  9.8 1.8 %collective-permute-start.3 = (bf16[2,64,1024]{2,1,0:T(8,128)(2,1)}, bf16[2,64,1024]{2,1,0:T(8,128)(2,1)}, u32[]{:S(2)}, u32[]{:S(2)}) collective-permute-start(bf16[2,64,1024]{2,1,0:T(8,128)(2,1)} %get-tuple-element.26), channel_id=1, source_target_pairs={{0,1},{1,2},{2,3},{3,0},{4,5},{5,6},{6,7},{7,4},{8,9},{9,10},{10,1... | collective-permute-start | bytes 786440 | tf_op jit(solution)/shard_map/ppermute | solution.py:600
  11.6 2.6 %collective-permute-start.4 = (bf16[2,64,1024]{2,1,0:T(8,128)(2,1)}, bf16[2,64,1024]{2,1,0:T(8,128)(2,1)}, u32[]{:S(2)}, u32[]{:S(2)}) collective-permute-start(bf16[2,64,1024]{2,1,0:T(8,128)(2,1)} %get-tuple-element.27), channel_id=1, source_target_pairs={{0,2},{1,3},{2,0},{3,1},{4,6},{5,7},{6,4},{7,5},{8,10},{9,11},{10,... | collective-permute-start | bytes 786440 | tf_op jit(solution)/shard_map/ppermute | solution.py:600
  14.2 1.3 collective-permute-start.5
  15.5 1.2 broadcast_multiply_fusion.factor_ref
  16.7 3.2 %saved_attention.1 = (f32[4,256,256]{2,1,0:T(8,128)}, bf16[256,512]{1,0:T(8,128)(2,1)}) custom-call(s32[2,2]{1,0:T(2,128)} %bitcast.55, s32[2]{0:T(128)} %bitcast.57, f32[1,4]{1,0:T(1,128)} %broadcast_multiply_fusion.factor_ref, bf16[256,512]{1,0:T(8,128)(2,1)} %bitcast.43, bf16[256,512]{1,0:T(8,128)(2,1)} %bitcast.45, bf16[256,512]{1,0:T(8,128)(2,1)} %bitcast.47, ...), custom_call_target="tpu_custom_call" | custom-call | flops 1024 | bytes 1024 | tf_op jit(solution)/shard_map/saved_attention/pallas_call | solution.py:155
  19.9 9.9 %collective-permute-done.1.first_ref.rest_1_ = bf16[2,64,4096]{2,1,0:T(8,128)(2,1)} collective-permute-done((bf16[2,64,4096]{2,1,0:T(8,128)(2,1)}, bf16[2,64,4096]{2,1,0:T(8,128)(2,1)}, u32[]{:S(2)}, u32[]{:S(2)}) %collective-permute-start.1) | collective-permute-done | bytes 1048608 | tf_op jit(solution)/shard_map/ppermute | solution.py:595
  29.7 1.8 %collective-permute-done.2.second_ref.rest_2_ = bf16[2,64,4096]{2,1,0:T(8,128)(2,1)} collective-permute-done((bf16[2,64,4096]{2,1,0:T(8,128)(2,1)}, bf16[2,64,4096]{2,1,0:T(8,128)(2,1)}, u32[]{:S(2)}, u32[]{:S(2)}) %collective-permute-start.2) | collective-permute-done | bytes 1048608 | tf_op jit(solution)/shard_map/ppermute | solution.py:595
  31.5 0.0 collective-permute-done.3.rest_1_
  31.5 0.5 collective-permute-done.4.rest_2_
  32.0 0.0 collective-permute-done.5.rest_3_
  32.0 2.2 %half_relay.1 = (bf16[2,32,4096]{2,1,0:T(8,128)(2,1)}, bf16[2,32,4096]{2,1,0:T(8,128)(2,1)}) custom-call(bf16[2,64,4096]{2,1,0:T(8,128)(2,1)} %collective-permute-done.1.first_ref.rest_1_, bf16[2,64,4096]{2,1,0:T(8,128)(2,1)} %collective-permute-done.2.second_ref.rest_2_, bf16[256,512]{1,0:T(8,128)(2,1)} %get-tuple-element.25.rest_0_.rest_7_.rest_4_, ...), custom_call_target="tpu_custom_call" | custom-call | flops 1024 | bytes 1024 | tf_op jit(solution)/shard_map/half_relay/pallas_call | solution.py:497
  34.2 1.4 collective-permute-start.6
  35.7 1.5 collective-permute-start.7
  37.2 6.1 %collective-permute-start.8 = (bf16[256,512]{1,0:T(8,128)(2,1)}, bf16[256,512]{1,0:T(8,128)(2,1)}, u32[]{:S(2)}, u32[]{:S(2)}) collective-permute-start(bf16[256,512]{1,0:T(8,128)(2,1)} %get-tuple-element.25.rest_0_.rest_7_.rest_4_), channel_id=1, source_target_pairs={{0,1},{1,2},{2,3},{3,0},{4,5},{5,6},{6,7},{7,4},{8,9},{9,10},{10,1... | collective-permute-start | bytes 786440 | tf_op jit(solution)/shard_map/ppermute | solution.py:600
  43.3 6.6 %collective-permute-done.8.rest_6_.rest_5_ = bf16[256,512]{1,0:T(8,128)(2,1)} collective-permute-done((bf16[256,512]{1,0:T(8,128)(2,1)}, bf16[256,512]{1,0:T(8,128)(2,1)}, u32[]{:S(2)}, u32[]{:S(2)}) %collective-permute-start.8) | collective-permute-done | bytes 262176 | tf_op jit(solution)/shard_map/ppermute | solution.py:600
  49.8 0.0 collective-permute-done.6.rest_4_.rest_3_
  49.8 0.0 collective-permute-done.7.rest_5_.rest_4_
  49.8 2.2 %stack.1.rest_11_.rest_0_ = bf16[2,4,64,1024]{3,2,1,0:T(8,128)(2,1)} custom-call(bf16[2,64,1024]{2,1,0:T(8,128)(2,1)} %get-tuple-element.24.rest_0_, bf16[2,64,1024]{2,1,0:T(8,128)(2,1)} %collective-permute-done.3.rest_1_, bf16[2,64,1024]{2,1,0:T(8,128)(2,1)} %collective-permute-done.4.rest_2_, bf16[2,64,1024]{2,1,0:T(8,128)(2,1)} %collective-permute-done.5.rest_3_, ...), custom_call_target="tpu_custom_call" | custom-call | flops 1024 | bytes 1024 | tf_op jit(solution)/shard_map/stack/pallas_call | solution.py:517
  52.0 0.6 collective-permute-start.9
  52.6 1.2 collective-permute-start.10
  53.8 7.6 %backward_attention.1.g_ref.rest_4_ = bf16[256,1536]{1,0:T(8,128)(2,1)} custom-call(f32[1,4]{1,0:T(1,128)} %broadcast_multiply_fusion.factor_ref, bf16[2,64,4096]{2,1,0:T(8,128)(2,1)} %collective-permute-done.ins_ref.rest_0_, bf16[2,64,4096]{2,1,0:T(8,128)(2,1)} %collective-permute-done.1.first_ref.rest_1_, ...), custom_call_target="tpu_custom_call" | custom-call | flops 1024 | bytes 1024 | tf_op jit(solution)/shard_map/backward_attention/pallas_call | solution.py:246
  61.4 8.9 %collective-permute-start.11 = (bf16[256,1536]{1,0:T(8,128)(2,1)}, bf16[256,1536]{1,0:T(8,128)(2,1)}, u32[]{:S(2)}, u32[]{:S(2)}) collective-permute-start(bf16[256,1536]{1,0:T(8,128)(2,1)} %backward_attention.1.g_ref.rest_4_), channel_id=1, source_target_pairs={{0,1},{1,2},{2,3},{4,5},{5,6},{6,7},{8,9},{9,10},{10,11},{12,13},{... | collective-permute-start | bytes 2359304 | tf_op jit(solution)/shard_map/ppermute | solution.py:605
  70.4 1.3 collective-permute-start.12
  71.7 9.0 %input_grads.1 = (bf16[2,64,4096]{2,1,0:T(8,128)(2,1)}, bf16[2,64,4096]{2,1,0:T(8,128)(2,1)}) custom-call(bf16[256,1536]{1,0:T(8,128)(2,1)} %backward_attention.1.g_ref.rest_4_, bf16[4096,512]{1,0:T(8,128)(2,1)} %bitcast.32, bf16[4096,512]{1,0:T(8,128)(2,1)} %bitcast.34, bf16[4096,512]{1,0:T(8,128)(2,1)} %bitcast.36), custom_call_target="tpu_custom_call" | custom-call | flops 1024 | bytes 1024 | tf_op jit(solution)/shard_map/input_grads/pallas_call | solution.py:288
  80.7 0.0 collective-permute-done.10.rest_1_.rest_2_
  80.7 2.2 %passed.1.rest_10_ = bf16[2,64,4096]{2,1,0:T(8,128)(2,1)} custom-call(bf16[2,64,4096]{2,1,0:T(8,128)(2,1)} %get-tuple-element.32.value_ref, bf16[2,4,64,1024]{3,2,1,0:T(8,128)(2,1)} %collective-permute-done.9.rest_0_.rest_1_, bf16[2,4,64,1024]{3,2,1,0:T(8,128)(2,1)} %collective-permute-done.10.rest_1_.rest_2_), custom_call_target="tpu_custom_call" | custom-call | flops 1024 | bytes 1024 | tf_op jit(solution)/shard_map/passed/pallas_call | solution.py:562
  83.0 1.6 collective-permute-start.14
  84.5 0.6 collective-permute-done.11.rest_11_.rest_5_
  85.1 5.3 %collective-permute-start.17 = (bf16[256,1536]{1,0:T(8,128)(2,1)}, bf16[256,1536]{1,0:T(8,128)(2,1)}, u32[]{:S(2)}, u32[]{:S(2)}) collective-permute-start(bf16[256,1536]{1,0:T(8,128)(2,1)} %collective-permute-done.11.rest_11_.rest_5_), channel_id=1, source_target_pairs={{0,1},{1,2},{2,3},{4,5},{5,6},{6,7},{8,9},{9,10},{10,11},{12,13},{... | collective-permute-start | bytes 2359304 | tf_op jit(solution)/shard_map/ppermute | solution.py:605
  90.4 0.0 collective-permute-done.12.rest_12_.rest_8_
  90.4 1.5 collective-permute-start.18
  91.9 0.6 collective-permute-start.16
  92.5 13.3 %forward_terms.1 = (bf16[2,64,4096]{2,1,0:T(8,128)(2,1)}, bf16[2,64,4096]{2,1,0:T(8,128)(2,1)}) custom-call(s32[2,2]{1,0:T(2,128)} %bitcast.56, s32[2]{0:T(128)} %bitcast.58, f32[1,4]{1,0:T(1,128)} %broadcast_multiply_fusion.factor_ref, bf16[2,64,4096]{2,1,0:T(8,128)(2,1)} %collective-permute-done.ins_ref.rest_0_, ...), custom_call_target="tpu_custom_call" | custom-call | flops 1024 | bytes 1024 | tf_op jit(solution)/shard_map/forward_terms/pallas_call | solution.py:344
  105.8 1.4 collective-permute-start.13
  107.2 5.5 %collective-permute-start.19 = (bf16[256,1536]{1,0:T(8,128)(2,1)}, bf16[256,1536]{1,0:T(8,128)(2,1)}, u32[]{:S(2)}, u32[]{:S(2)}) collective-permute-start(bf16[256,1536]{1,0:T(8,128)(2,1)} %collective-permute-done.17.rest_1_.rest_6_), channel_id=1, source_target_pairs={{0,1},{1,2},{2,3},{4,5},{5,6},{6,7},{8,9},{9,10},{10,11},{12,13},{... | collective-permute-start | bytes 2359304 | tf_op jit(solution)/shard_map/ppermute | solution.py:605
  112.7 1.3 collective-permute-start.20
  114.0 2.1 %add.46 = bf16[64,4096]{1,0:T(8,128)(2,1)} custom-call(bf16[2,64,4096]{2,1,0:T(8,128)(2,1)} %get-tuple-element.35.near_ref, bf16[2,64,4096]{2,1,0:T(8,128)(2,1)} %collective-permute-done.14.came_ref, bf16[2,64,4096]{2,1,0:T(8,128)(2,1)} %get-tuple-element.33.rest_0_.near_ref), custom_call_target="tpu_custom_call" | custom-call | flops 1024 | bytes 1024 | tf_op jit(solution)/shard_map/add/pallas_call | solution.py:541
  116.2 1.6 collective-permute-start.15
  117.8 8.6 %collective-permute-done.15.last_ref = bf16[64,4096]{1,0:T(8,128)(2,1)} collective-permute-done((bf16[64,4096]{1,0:T(8,128)(2,1)}, bf16[64,4096]{1,0:T(8,128)(2,1)}, u32[]{:S(2)}, u32[]{:S(2)}) %collective-permute-start.15) | collective-permute-done | bytes 524320 | tf_op jit(solution)/shard_map/ppermute | solution.py:589
  126.3 4.1 %back.1 = (bf16[64,4096]{1,0:T(8,128)(2,1)}, f32[1,4096]{1,0:T(1,128)}) custom-call(bf16[2,64,4096]{2,1,0:T(8,128)(2,1)} %get-tuple-element.35.near_ref, bf16[2,64,4096]{2,1,0:T(8,128)(2,1)} %collective-permute-done.14.came_ref, bf16[64,4096]{1,0:T(8,128)(2,1)} %collective-permute-done.15.last_ref, bf16[64,4096]{1,0:T(8,128)(2,1)} %bitcast.41, ...), custom_call_target="tpu_custom_call" | custom-call | flops 1024 | bytes 1024 | tf_op jit(solution)/shard_map/back/pallas_call | solution.py:373
  130.4 0.0 collective-permute-done.20.rest_2_.rest_10_
  130.4 2.1 %add.47.rest_0_ = bf16[64,4096]{1,0:T(8,128)(2,1)} custom-call(bf16[2,64,4096]{2,1,0:T(8,128)(2,1)} %get-tuple-element.33.rest_0_.near_ref, bf16[2,64,4096]{2,1,0:T(8,128)(2,1)} %collective-permute-done.13.came_ref, bf16[64,4096]{1,0:T(8,128)(2,1)} %get-tuple-element.36.rest_0_, bf16[256,1536]{1,0:T(8,128)(2,1)} %collective-permute-done.19.rest_1_.rest_7_, ...), custom_call_target="tpu_custom_call" | custom-call | flops 1024 | bytes 1024 | tf_op jit(solution)/shard_map/add/pallas_call | solution.py:541
  132.6 1.6 collective-permute-start.21
  134.2 0.7 collective-permute-start.22
  134.9 3.4 %collective-permute-done.22.came_ref = f32[1,4096]{1,0:T(1,128)} collective-permute-done((f32[1,4096]{1,0:T(1,128)}, f32[1,4096]{1,0:T(1,128)}, u32[]{:S(2)}, u32[]{:S(2)}) %collective-permute-start.22) | collective-permute-done | bytes 16416 | tf_op jit(solution)/shard_map/ppermute | solution.py:589
  138.2 1.3 gain_added.2.rest_11_.own_ref
  139.6 0.5 collective-permute-start.25
  140.1 1.2 collective-permute-start.23
  141.2 3.6 %collective-permute-start.24 = (bf16[256,512]{1,0:T(8,128)(2,1)}, bf16[256,512]{1,0:T(8,128)(2,1)}, u32[]{:S(2)}, u32[]{:S(2)}) collective-permute-start(bf16[256,512]{1,0:T(8,128)(2,1)} %get-tuple-element.25.rest_0_.rest_7_.rest_4_), channel_id=1, source_target_pairs={{0,3},{1,0},{2,1},{3,2},{4,7},{5,4},{6,5},{7,6},{8,11},{9,8},{10,9... | collective-permute-start | bytes 786440 | tf_op jit(solution)/shard_map/ppermute | solution.py:600
  144.8 8.0 %weight_grads.1 = (bf16[1024,512]{1,0:T(8,128)(2,1)}, bf16[1024,512]{1,0:T(8,128)(2,1)}, bf16[1024,512]{1,0:T(8,128)(2,1)}) custom-call(bf16[2,4,64,1024]{3,2,1,0:T(8,128)(2,1)} %stack.1.rest_11_.rest_0_, bf16[2,4,64,1024]{3,2,1,0:T(8,128)(2,1)} %collective-permute-done.9.rest_0_.rest_1_, bf16[2,4,64,1024]{3,2,1,0:T(8,128)(2,1)} %collective-permute-done.10.rest_1_.rest_2_, ...), custom_call_target="tpu_custom_call" | custom-call | flops 1024 | bytes 1024 | tf_op jit(solution)/shard_map/weight_grads/pallas_call | solution.py:457
  152.8 0.0 collective-permute-done.25.came_ref
  152.8 1.3 gain_added.3.rest_8_
  154.1 0.0 collective-permute-start.28
  154.1 0.0 collective-permute-start.27
  154.1 2.0 %collective-permute-start.26 = (f32[1,4096]{1,0:T(1,128)}, f32[1,4096]{1,0:T(1,128)}, u32[]{:S(2)}, u32[]{:S(2)}) collective-permute-start(f32[1,4096]{1,0:T(1,128)} %gain_added.3.rest_8_), channel_id=1, source_target_pairs={{0,1},{1,2},{2,3},{3,0},{4,5},{5,6},{6,7},{7,4},{8,9},{9,10},{10,1... | collective-permute-start | bytes 49160 | tf_op jit(solution)/shard_map/ppermute | solution.py:600
  156.2 2.6 %fusion.1 = bf16[1,1,64,4096]{3,2,1,0:T(8,128)(2,1)} fusion(bf16[64,4096]{1,0:T(8,128)(2,1)} %collective-permute-done.21.rest_1_, bf16[2,64,4096]{2,1,0:T(8,128)(2,1)} %collective-permute-done.13.came_ref, bf16[2,64,4096]{2,1,0:T(8,128)(2,1)} %collective-permute-done.ins_ref.rest_0_, bf16[2,64,4096]{2,1,0:T(8,128)(2,1)} %get-tuple-element.33.rest_0_.near_ref), kind=kLoop, calls=%fused_computation.3 | loop fusion | flops 2097152 | bytes 2621440 | tf_op jit(solution)/shard_map/broadcast_in_dim | solution.py:698
  158.7 5.0 %out_weight_grads.1 = bf16[512,1024]{1,0:T(8,128)(2,1)} custom-call(bf16[2,4,64,1024]{3,2,1,0:T(8,128)(2,1)} %stack.1.rest_11_.rest_0_, bf16[2,4,64,1024]{3,2,1,0:T(8,128)(2,1)} %collective-permute-done.9.rest_0_.rest_1_, bf16[2,4,64,1024]{3,2,1,0:T(8,128)(2,1)} %collective-permute-done.10.rest_1_.rest_2_, ...), custom_call_target="tpu_custom_call" | custom-call | flops 1024 | bytes 1024 | tf_op jit(solution)/shard_map/out_weight_grads/pallas_call | solution.py:457
  163.8 1.4 add_add_fusion
  (13 shorter events, 0.0 us)
Async XLA Ops:
  2.8 4.3 %collective-permute-start = (bf16[2,64,4096]{2,1,0:T(8,128)(2,1)}, bf16[2,64,4096]{2,1,0:T(8,128)(2,1)}, u32[]{:S(2)}, u32[]{:S(2)}) collective-permute-start(bf16[2,64,4096]{2,1,0:T(8,128)(2,1)} %pick.1), channel_id=1, source_target_pairs={{0,16},{4,20},{8,24},{12,28},{16,0},{20,4},{24,8},{28,12},{1,17},{... | collective-permute-start | bytes 3145736 | tf_op jit(solution)/shard_map/ppermute | solution.py:595
  3.4 26.4 %collective-permute-start.1 = (bf16[2,64,4096]{2,1,0:T(8,128)(2,1)}, bf16[2,64,4096]{2,1,0:T(8,128)(2,1)}, u32[]{:S(2)}, u32[]{:S(2)}) collective-permute-start(bf16[2,64,4096]{2,1,0:T(8,128)(2,1)} %pick.1), channel_id=1, source_target_pairs={{0,20},{4,16},{8,28},{12,24},{16,4},{20,0},{24,12},{28,8},{1,21},{... | collective-permute-start | bytes 3145736 | tf_op jit(solution)/shard_map/ppermute | solution.py:595
  6.0 25.5 %collective-permute-start.2 = (bf16[2,64,4096]{2,1,0:T(8,128)(2,1)}, bf16[2,64,4096]{2,1,0:T(8,128)(2,1)}, u32[]{:S(2)}, u32[]{:S(2)}) collective-permute-start(bf16[2,64,4096]{2,1,0:T(8,128)(2,1)} %pick.1), channel_id=1, source_target_pairs={{0,24},{4,28},{8,16},{12,20},{16,8},{20,12},{24,0},{28,4},{1,25},{... | collective-permute-start | bytes 3145736 | tf_op jit(solution)/shard_map/ppermute | solution.py:595
  9.8 21.7 %collective-permute-start.3 = (bf16[2,64,1024]{2,1,0:T(8,128)(2,1)}, bf16[2,64,1024]{2,1,0:T(8,128)(2,1)}, u32[]{:S(2)}, u32[]{:S(2)}) collective-permute-start(bf16[2,64,1024]{2,1,0:T(8,128)(2,1)} %get-tuple-element.26), channel_id=1, source_target_pairs={{0,1},{1,2},{2,3},{3,0},{4,5},{5,6},{6,7},{7,4},{8,9},{9,10},{10,1... | collective-permute-start | bytes 786440 | tf_op jit(solution)/shard_map/ppermute | solution.py:600
  11.6 20.4 %collective-permute-start.4 = (bf16[2,64,1024]{2,1,0:T(8,128)(2,1)}, bf16[2,64,1024]{2,1,0:T(8,128)(2,1)}, u32[]{:S(2)}, u32[]{:S(2)}) collective-permute-start(bf16[2,64,1024]{2,1,0:T(8,128)(2,1)} %get-tuple-element.27), channel_id=1, source_target_pairs={{0,2},{1,3},{2,0},{3,1},{4,6},{5,7},{6,4},{7,5},{8,10},{9,11},{10,... | collective-permute-start | bytes 786440 | tf_op jit(solution)/shard_map/ppermute | solution.py:600
  14.2 17.9 %collective-permute-start.5 = (bf16[2,64,1024]{2,1,0:T(8,128)(2,1)}, bf16[2,64,1024]{2,1,0:T(8,128)(2,1)}, u32[]{:S(2)}, u32[]{:S(2)}) collective-permute-start(bf16[2,64,1024]{2,1,0:T(8,128)(2,1)} %get-tuple-element.28), channel_id=1, source_target_pairs={{0,3},{1,0},{2,1},{3,2},{4,7},{5,4},{6,5},{7,6},{8,11},{9,8},{10,9... | collective-permute-start | bytes 786440 | tf_op jit(solution)/shard_map/ppermute | solution.py:600
  34.2 15.6 %collective-permute-start.6 = (bf16[2,32,4096]{2,1,0:T(8,128)(2,1)}, bf16[2,32,4096]{2,1,0:T(8,128)(2,1)}, u32[]{:S(2)}, u32[]{:S(2)}) collective-permute-start(bf16[2,32,4096]{2,1,0:T(8,128)(2,1)} %get-tuple-element.29), channel_id=1, source_target_pairs={{0,4},{4,0},{8,12},{12,8},{1,5},{5,1},{9,13},{13,9},{2,6},{6,2},{1... | collective-permute-start | bytes 1572872 | tf_op jit(solution)/shard_map/ppermute | solution.py:589
  35.7 14.2 %collective-permute-start.7 = (bf16[2,32,4096]{2,1,0:T(8,128)(2,1)}, bf16[2,32,4096]{2,1,0:T(8,128)(2,1)}, u32[]{:S(2)}, u32[]{:S(2)}) collective-permute-start(bf16[2,32,4096]{2,1,0:T(8,128)(2,1)} %get-tuple-element.30), channel_id=1, source_target_pairs={{0,8},{4,12},{8,0},{12,4},{1,9},{5,13},{9,1},{13,5},{2,10},{6,14},... | collective-permute-start | bytes 1572872 | tf_op jit(solution)/shard_map/ppermute | solution.py:589
  37.2 12.6 %collective-permute-start.8 = (bf16[256,512]{1,0:T(8,128)(2,1)}, bf16[256,512]{1,0:T(8,128)(2,1)}, u32[]{:S(2)}, u32[]{:S(2)}) collective-permute-start(bf16[256,512]{1,0:T(8,128)(2,1)} %get-tuple-element.25.rest_0_.rest_7_.rest_4_), channel_id=1, source_target_pairs={{0,1},{1,2},{2,3},{3,0},{4,5},{5,6},{6,7},{7,4},{8,9},{9,10},{10,1... | collective-permute-start | bytes 786440 | tf_op jit(solution)/shard_map/ppermute | solution.py:600
  52.0 28.7 %collective-permute-start.9 = (bf16[2,4,64,1024]{3,2,1,0:T(8,128)(2,1)}, bf16[2,4,64,1024]{3,2,1,0:T(8,128)(2,1)}, u32[]{:S(2)}, u32[]{:S(2)}) collective-permute-start(bf16[2,4,64,1024]{3,2,1,0:T(8,128)(2,1)} %stack.1.rest_11_.rest_0_), channel_id=1, source_target_pairs={{0,4},{4,0},{8,12},{12,8},{1,5},{5,1},{9,13},{13,9},{2,6},{6,2},{1... | collective-permute-start | bytes 3145736 | tf_op jit(solution)/shard_map/ppermute | solution.py:589
  52.6 28.1 %collective-permute-start.10 = (bf16[2,4,64,1024]{3,2,1,0:T(8,128)(2,1)}, bf16[2,4,64,1024]{3,2,1,0:T(8,128)(2,1)}, u32[]{:S(2)}, u32[]{:S(2)}) collective-permute-start(bf16[2,4,64,1024]{3,2,1,0:T(8,128)(2,1)} %stack.1.rest_11_.rest_0_), channel_id=1, source_target_pairs={{0,8},{4,12},{8,0},{12,4},{1,9},{5,13},{9,1},{13,5},{2,10},{6,14},... | collective-permute-start | bytes 3145736 | tf_op jit(solution)/shard_map/ppermute | solution.py:589
  61.4 23.7 %collective-permute-start.11 = (bf16[256,1536]{1,0:T(8,128)(2,1)}, bf16[256,1536]{1,0:T(8,128)(2,1)}, u32[]{:S(2)}, u32[]{:S(2)}) collective-permute-start(bf16[256,1536]{1,0:T(8,128)(2,1)} %backward_attention.1.g_ref.rest_4_), channel_id=1, source_target_pairs={{0,1},{1,2},{2,3},{4,5},{5,6},{6,7},{8,9},{9,10},{10,11},{12,13},{... | collective-permute-start | bytes 2359304 | tf_op jit(solution)/shard_map/ppermute | solution.py:605
  70.4 20.0 %collective-permute-start.12 = (bf16[256,1536]{1,0:T(8,128)(2,1)}, bf16[256,1536]{1,0:T(8,128)(2,1)}, u32[]{:S(2)}, u32[]{:S(2)}) collective-permute-start(bf16[256,1536]{1,0:T(8,128)(2,1)} %backward_attention.1.g_ref.rest_4_), channel_id=1, source_target_pairs={{1,0},{2,1},{3,2},{5,4},{6,5},{7,6},{9,8},{10,9},{11,10},{13,12},{... | collective-permute-start | bytes 2359304 | tf_op jit(solution)/shard_map/ppermute | solution.py:605
  83.0 31.1 %collective-permute-start.14 = (bf16[2,64,4096]{2,1,0:T(8,128)(2,1)}, bf16[2,64,4096]{2,1,0:T(8,128)(2,1)}, u32[]{:S(2)}, u32[]{:S(2)}) collective-permute-start(bf16[2,64,4096]{2,1,0:T(8,128)(2,1)} %passed.1.rest_10_), channel_id=1, source_target_pairs={{0,4},{4,0},{8,12},{12,8},{1,5},{5,1},{9,13},{13,9},{2,6},{6,2},{1... | collective-permute-start | bytes 3145736 | tf_op jit(solution)/shard_map/ppermute | solution.py:589
  85.1 22.1 %collective-permute-start.17 = (bf16[256,1536]{1,0:T(8,128)(2,1)}, bf16[256,1536]{1,0:T(8,128)(2,1)}, u32[]{:S(2)}, u32[]{:S(2)}) collective-permute-start(bf16[256,1536]{1,0:T(8,128)(2,1)} %collective-permute-done.11.rest_11_.rest_5_), channel_id=1, source_target_pairs={{0,1},{1,2},{2,3},{4,5},{5,6},{6,7},{8,9},{9,10},{10,11},{12,13},{... | collective-permute-start | bytes 2359304 | tf_op jit(solution)/shard_map/ppermute | solution.py:605
  90.4 22.3 %collective-permute-start.18 = (bf16[256,1536]{1,0:T(8,128)(2,1)}, bf16[256,1536]{1,0:T(8,128)(2,1)}, u32[]{:S(2)}, u32[]{:S(2)}) collective-permute-start(bf16[256,1536]{1,0:T(8,128)(2,1)} %collective-permute-done.12.rest_12_.rest_8_), channel_id=1, source_target_pairs={{1,0},{2,1},{3,2},{5,4},{6,5},{7,6},{9,8},{10,9},{11,10},{13,12},{... | collective-permute-start | bytes 2359304 | tf_op jit(solution)/shard_map/ppermute | solution.py:605
  91.9 25.9 %collective-permute-start.16 = (bf16[2,4,64,1024]{3,2,1,0:T(8,128)(2,1)}, bf16[2,4,64,1024]{3,2,1,0:T(8,128)(2,1)}, u32[]{:S(2)}, u32[]{:S(2)}) collective-permute-start(bf16[2,4,64,1024]{3,2,1,0:T(8,128)(2,1)} %collective-permute-done.9.rest_0_.rest_1_), channel_id=1, source_target_pairs={{0,8},{4,12},{8,0},{12,4},{1,9},{5,13},{9,1},{13,5},{2,10},{6,14},... | collective-permute-start | bytes 3145736 | tf_op jit(solution)/shard_map/ppermute | solution.py:589
  105.8 24.7 %collective-permute-start.13 = (bf16[2,64,4096]{2,1,0:T(8,128)(2,1)}, bf16[2,64,4096]{2,1,0:T(8,128)(2,1)}, u32[]{:S(2)}, u32[]{:S(2)}) collective-permute-start(bf16[2,64,4096]{2,1,0:T(8,128)(2,1)} %get-tuple-element.34), channel_id=1, source_target_pairs={{0,4},{4,0},{8,12},{12,8},{1,5},{5,1},{9,13},{13,9},{2,6},{6,2},{1... | collective-permute-start | bytes 3145736 | tf_op jit(solution)/shard_map/ppermute | solution.py:589
  107.2 23.2 %collective-permute-start.19 = (bf16[256,1536]{1,0:T(8,128)(2,1)}, bf16[256,1536]{1,0:T(8,128)(2,1)}, u32[]{:S(2)}, u32[]{:S(2)}) collective-permute-start(bf16[256,1536]{1,0:T(8,128)(2,1)} %collective-permute-done.17.rest_1_.rest_6_), channel_id=1, source_target_pairs={{0,1},{1,2},{2,3},{4,5},{5,6},{6,7},{8,9},{9,10},{10,11},{12,13},{... | collective-permute-start | bytes 2359304 | tf_op jit(solution)/shard_map/ppermute | solution.py:605
  112.7 17.7 %collective-permute-start.20 = (bf16[256,1536]{1,0:T(8,128)(2,1)}, bf16[256,1536]{1,0:T(8,128)(2,1)}, u32[]{:S(2)}, u32[]{:S(2)}) collective-permute-start(bf16[256,1536]{1,0:T(8,128)(2,1)} %collective-permute-done.18.rest_2_.rest_9_), channel_id=1, source_target_pairs={{1,0},{2,1},{3,2},{5,4},{6,5},{7,6},{9,8},{10,9},{11,10},{13,12},{... | collective-permute-start | bytes 2359304 | tf_op jit(solution)/shard_map/ppermute | solution.py:605
  116.2 10.2 %collective-permute-start.15 = (bf16[64,4096]{1,0:T(8,128)(2,1)}, bf16[64,4096]{1,0:T(8,128)(2,1)}, u32[]{:S(2)}, u32[]{:S(2)}) collective-permute-start(bf16[64,4096]{1,0:T(8,128)(2,1)} %add.46), channel_id=1, source_target_pairs={{0,8},{4,12},{8,0},{12,4},{1,9},{5,13},{9,1},{13,5},{2,10},{6,14},... | collective-permute-start | bytes 1572872 | tf_op jit(solution)/shard_map/ppermute | solution.py:589
  132.6 20.2 %collective-permute-start.21 = (bf16[64,4096]{1,0:T(8,128)(2,1)}, bf16[64,4096]{1,0:T(8,128)(2,1)}, u32[]{:S(2)}, u32[]{:S(2)}) collective-permute-start(bf16[64,4096]{1,0:T(8,128)(2,1)} %add.47.rest_0_), channel_id=1, source_target_pairs={{0,8},{4,12},{8,0},{12,4},{1,9},{5,13},{9,1},{13,5},{2,10},{6,14},... | collective-permute-start | bytes 1572872 | tf_op jit(solution)/shard_map/ppermute | solution.py:589
  134.2 4.1 %collective-permute-start.22 = (f32[1,4096]{1,0:T(1,128)}, f32[1,4096]{1,0:T(1,128)}, u32[]{:S(2)}, u32[]{:S(2)}) collective-permute-start(f32[1,4096]{1,0:T(1,128)} %get-tuple-element.37.own_ref), channel_id=1, source_target_pairs={{0,4},{4,0},{8,12},{12,8},{1,5},{5,1},{9,13},{13,9},{2,6},{6,2},{1... | collective-permute-start | bytes 49160 | tf_op jit(solution)/shard_map/ppermute | solution.py:589
  139.6 13.2 %collective-permute-start.25 = (f32[1,4096]{1,0:T(1,128)}, f32[1,4096]{1,0:T(1,128)}, u32[]{:S(2)}, u32[]{:S(2)}) collective-permute-start(f32[1,4096]{1,0:T(1,128)} %gain_added.2.rest_11_.own_ref), channel_id=1, source_target_pairs={{0,8},{4,12},{8,0},{12,4},{1,9},{5,13},{9,1},{13,5},{2,10},{6,14},... | collective-permute-start | bytes 49160 | tf_op jit(solution)/shard_map/ppermute | solution.py:589
  140.1 18.7 %collective-permute-start.23 = (bf16[256,512]{1,0:T(8,128)(2,1)}, bf16[256,512]{1,0:T(8,128)(2,1)}, u32[]{:S(2)}, u32[]{:S(2)}) collective-permute-start(bf16[256,512]{1,0:T(8,128)(2,1)} %get-tuple-element.25.rest_0_.rest_7_.rest_4_), channel_id=1, source_target_pairs={{0,2},{1,3},{2,0},{3,1},{4,6},{5,7},{6,4},{7,5},{8,10},{9,11},{10,... | collective-permute-start | bytes 786440 | tf_op jit(solution)/shard_map/ppermute | solution.py:600
  141.2 17.5 %collective-permute-start.24 = (bf16[256,512]{1,0:T(8,128)(2,1)}, bf16[256,512]{1,0:T(8,128)(2,1)}, u32[]{:S(2)}, u32[]{:S(2)}) collective-permute-start(bf16[256,512]{1,0:T(8,128)(2,1)} %get-tuple-element.25.rest_0_.rest_7_.rest_4_), channel_id=1, source_target_pairs={{0,3},{1,0},{2,1},{3,2},{4,7},{5,4},{6,5},{7,6},{8,11},{9,8},{10,9... | collective-permute-start | bytes 786440 | tf_op jit(solution)/shard_map/ppermute | solution.py:600
  154.1 9.6 %collective-permute-start.28 = (f32[1,4096]{1,0:T(1,128)}, f32[1,4096]{1,0:T(1,128)}, u32[]{:S(2)}, u32[]{:S(2)}) collective-permute-start(f32[1,4096]{1,0:T(1,128)} %gain_added.3.rest_8_), channel_id=1, source_target_pairs={{0,3},{1,0},{2,1},{3,2},{4,7},{5,4},{6,5},{7,6},{8,11},{9,8},{10,9... | collective-permute-start | bytes 49160 | tf_op jit(solution)/shard_map/ppermute | solution.py:600
  154.1 9.6 %collective-permute-start.27 = (f32[1,4096]{1,0:T(1,128)}, f32[1,4096]{1,0:T(1,128)}, u32[]{:S(2)}, u32[]{:S(2)}) collective-permute-start(f32[1,4096]{1,0:T(1,128)} %gain_added.3.rest_8_), channel_id=1, source_target_pairs={{0,2},{1,3},{2,0},{3,1},{4,6},{5,7},{6,4},{7,5},{8,10},{9,11},{10,... | collective-permute-start | bytes 49160 | tf_op jit(solution)/shard_map/ppermute | solution.py:600
  154.1 9.7 %collective-permute-start.26 = (f32[1,4096]{1,0:T(1,128)}, f32[1,4096]{1,0:T(1,128)}, u32[]{:S(2)}, u32[]{:S(2)}) collective-permute-start(f32[1,4096]{1,0:T(1,128)} %gain_added.3.rest_8_), channel_id=1, source_target_pairs={{0,1},{1,2},{2,3},{3,0},{4,5},{5,6},{6,7},{7,4},{8,9},{9,10},{10,1... | collective-permute-start | bytes 49160 | tf_op jit(solution)/shard_map/ppermute | solution.py:600

commit v4 on v3

--- a/solution.py
+++ b/solution.py
@@ -416,7 +416,7 @@
     run_copies(slice_copies(0, parts, cols, sems))
     grad_copies(lambda copy: copy.wait())
     width = out_q.shape[1]
-    tile = min(256, out_q.shape[0])
+    tile = min(512, out_q.shape[0])
     samples, tokens, _ = cols.shape
 
     @pl.loop(0, out_q.shape[0] // tile)
@@ -440,7 +440,7 @@
         copies.append(pltpu.make_async_copy(source, spot, own_sems.at[k]))
     run_copies(copies)
     samples, tokens, slice_width = cols.shape
-    tile = 128
+    tile = 512
 
     @pl.loop(0, out_ref.shape[0] // tile)
     def _(i):
@@ -660,10 +660,10 @@
     halves, token = half_relayed(ins[1], ins[2], after=[att, *moved[1:]])
     ins = ins + halves
     atts = exchanged([att] * n_dp, "dp")
-    cols = stacked(moved, after=halves + atts[1:2])
+    cols = stacked(moved, after=[token])
     cols = [cols] + [swapped(cols, "seq", j) for j in (1, 2)]
 
-    grads = backward_attention(factor, ins, soft, wo, att, q, k, v, after=[cols[0]])
+    grads = backward_attention(factor, ins, soft, wo, att, q, k, v, after=[cols[0], *atts[1:2]])
     lower, upper = line_gathered(grads, "dp")
     dx_near, dx_far = input_grads(grads, wq, wk, wv)
     dx_far = passed(dx_far, after=cols[1:])

time: 166 us -> 162 us (0.976)
  waiting for transfers between devices: 31.3 us -> 28.9 us
    ppermute x9, waiting for transfers between devices: 7.1 us -> 3.68 us  [rotated(): return lax.ppermute(value, axis, [(i, (i + k) % n) for i in range(n)])]
  transfers between devices with their start and end apart: 29 -> 29, of which waited for: 7 -> 8; matrix products, arithmetic and copies ran while one was open for 2% -> 2% of each run, Pallas kernels for 36% -> 38%
where the time goes in v4:
time: 162 us; the launch traced here: 161 us
  Pallas kernels  67.3 us (42%)
  starting transfers between devices  58.5 us (36%)
  waiting for transfers between devices  28.9 us (18%)
  other arithmetic  5.14 us (3%)
    ppermute x6, starting transfers between devices, shifted(): lax.ppermute(value, axis, [(i, i + by) for i in range(n) if 0 <= i + by <...  23.7 us
    ppermute x9, starting transfers between devices, rotated(): return lax.ppermute(value, axis, [(i, (i + k) % n) for i in range(n)])  19.2 us
    pallas_call x1, Pallas kernels, forward_terms(): pl.pallas_call(functools.partial(forward_kernel, n), out_shape=(sds((2, r...  13.3 us
    ppermute x11, waiting for transfers between devices, swapped(): lax.ppermute(value, axis, [(i, i ^ j) for i in range(lax.axis_size(axis))])  12.9 us
    pallas_call x2, Pallas kernels, contracted(): pl.pallas_call(functools.partial(kernel, len(parts), samples), out_shape=...  11.7 us
    ppermute x3, waiting for transfers between devices, crossed(): return lax.ppermute(value, ('pipe', 'seq'), pairs)  11.6 us
    ppermute x11, starting transfers between devices, swapped(): lax.ppermute(value, axis, [(i, i ^ j) for i in range(lax.axis_size(axis))])  11.3 us
    pallas_call x1, Pallas kernels, input_grads(): pl.pallas_call(input_grad_kernel, out_shape=(sds((2, tokens // 4, model),...  9.04 us
  transfers between devices with their start and end apart: 29, of which 8 were waited for; matrix products, arithmetic and copies ran while one was open for 2% of the time, Pallas kernels for 38%

profile of v4, /device:TPU:0, one launch (start us, length us, event | category | flops | bytes accessed | tf_op | source)
XLA Modules:
  0.0 160.7 jit_solution(3042265490391219328)
XLA Ops:
  0.6 2.2 %pick.1 = bf16[2,64,4096]{2,1,0:T(8,128)(2,1)} custom-call(bf16[64,4096]{1,0:T(8,128)(2,1)} %bitcast.51, bf16[64,4096]{1,0:T(8,128)(2,1)} %bitcast.52, bf16[64,4096]{1,0:T(8,128)(2,1)} %bitcast.53, bf16[64,4096]{1,0:T(8,128)(2,1)} %bitcast.54), custom_call_target="tpu_custom_call" | custom-call | flops 1024 | bytes 1024 | tf_op jit(solution)/shard_map/pick/pallas_call | solution.py:105
  2.8 0.5 collective-permute-start
  3.4 2.6 %collective-permute-start.1 = (bf16[2,64,4096]{2,1,0:T(8,128)(2,1)}, bf16[2,64,4096]{2,1,0:T(8,128)(2,1)}, u32[]{:S(2)}, u32[]{:S(2)}) collective-permute-start(bf16[2,64,4096]{2,1,0:T(8,128)(2,1)} %pick.1), channel_id=1, source_target_pairs={{0,20},{4,16},{8,28},{12,24},{16,4},{20,0},{24,12},{28,8},{1,21},{... | collective-permute-start | bytes 3145736 | tf_op jit(solution)/shard_map/ppermute | solution.py:595
  6.0 1.2 collective-permute-start.2
  7.2 0.0 collective-permute-done.ins_ref.rest_0_
  7.2 2.7 %columns.1 = (bf16[2,64,1024]{2,1,0:T(8,128)(2,1)}, bf16[2,64,1024]{2,1,0:T(8,128)(2,1)}, bf16[2,64,1024]{2,1,0:T(8,128)(2,1)}, bf16[2,64,1024]{2,1,0:T(8,128)(2,1)}) custom-call(bf16[64,4096]{1,0:T(8,128)(2,1)} %bitcast.40, bf16[2,64,4096]{2,1,0:T(8,128)(2,1)} %collective-permute-done.ins_ref.rest_0_, f32[1,4096]{1,0:T(1,128)} %gain_ref.3), custom_call_target="tpu_custom_call" | custom-call | flops 1024 | bytes 1024 | tf_op jit(solution)/shard_map/columns/pallas_call | solution.py:131
  9.8 1.8 %collective-permute-start.3 = (bf16[2,64,1024]{2,1,0:T(8,128)(2,1)}, bf16[2,64,1024]{2,1,0:T(8,128)(2,1)}, u32[]{:S(2)}, u32[]{:S(2)}) collective-permute-start(bf16[2,64,1024]{2,1,0:T(8,128)(2,1)} %get-tuple-element.26), channel_id=1, source_target_pairs={{0,1},{1,2},{2,3},{3,0},{4,5},{5,6},{6,7},{7,4},{8,9},{9,10},{10,1... | collective-permute-start | bytes 786440 | tf_op jit(solution)/shard_map/ppermute | solution.py:600
  11.6 2.6 %collective-permute-start.4 = (bf16[2,64,1024]{2,1,0:T(8,128)(2,1)}, bf16[2,64,1024]{2,1,0:T(8,128)(2,1)}, u32[]{:S(2)}, u32[]{:S(2)}) collective-permute-start(bf16[2,64,1024]{2,1,0:T(8,128)(2,1)} %get-tuple-element.27), channel_id=1, source_target_pairs={{0,2},{1,3},{2,0},{3,1},{4,6},{5,7},{6,4},{7,5},{8,10},{9,11},{10,... | collective-permute-start | bytes 786440 | tf_op jit(solution)/shard_map/ppermute | solution.py:600
  14.2 1.3 collective-permute-start.5
  15.5 1.2 broadcast_multiply_fusion.factor_ref
  16.7 3.2 %saved_attention.1 = (f32[4,256,256]{2,1,0:T(8,128)}, bf16[256,512]{1,0:T(8,128)(2,1)}) custom-call(s32[2,2]{1,0:T(2,128)} %bitcast.55, s32[2]{0:T(128)} %bitcast.57, f32[1,4]{1,0:T(1,128)} %broadcast_multiply_fusion.factor_ref, bf16[256,512]{1,0:T(8,128)(2,1)} %bitcast.43, bf16[256,512]{1,0:T(8,128)(2,1)} %bitcast.45, bf16[256,512]{1,0:T(8,128)(2,1)} %bitcast.47, ...), custom_call_target="tpu_custom_call" | custom-call | flops 1024 | bytes 1024 | tf_op jit(solution)/shard_map/saved_attention/pallas_call | solution.py:155
  19.9 9.9 %collective-permute-done.1.first_ref.rest_1_ = bf16[2,64,4096]{2,1,0:T(8,128)(2,1)} collective-permute-done((bf16[2,64,4096]{2,1,0:T(8,128)(2,1)}, bf16[2,64,4096]{2,1,0:T(8,128)(2,1)}, u32[]{:S(2)}, u32[]{:S(2)}) %collective-permute-start.1) | collective-permute-done | bytes 1048608 | tf_op jit(solution)/shard_map/ppermute | solution.py:595
  29.7 1.8 %collective-permute-done.2.second_ref.rest_2_ = bf16[2,64,4096]{2,1,0:T(8,128)(2,1)} collective-permute-done((bf16[2,64,4096]{2,1,0:T(8,128)(2,1)}, bf16[2,64,4096]{2,1,0:T(8,128)(2,1)}, u32[]{:S(2)}, u32[]{:S(2)}) %collective-permute-start.2) | collective-permute-done | bytes 1048608 | tf_op jit(solution)/shard_map/ppermute | solution.py:595
  31.5 0.0 collective-permute-done.3.rest_1_
  31.5 0.5 collective-permute-done.4.rest_2_
  32.0 0.0 collective-permute-done.5.rest_3_
  32.0 2.2 %half_relay.1 = (bf16[2,32,4096]{2,1,0:T(8,128)(2,1)}, bf16[2,32,4096]{2,1,0:T(8,128)(2,1)}) custom-call(bf16[2,64,4096]{2,1,0:T(8,128)(2,1)} %collective-permute-done.1.first_ref.rest_1_, bf16[2,64,4096]{2,1,0:T(8,128)(2,1)} %collective-permute-done.2.second_ref.rest_2_, bf16[256,512]{1,0:T(8,128)(2,1)} %get-tuple-element.25.rest_0_.rest_7_.rest_4_, ...), custom_call_target="tpu_custom_call" | custom-call | flops 1024 | bytes 1024 | tf_op jit(solution)/shard_map/half_relay/pallas_call | solution.py:497
  34.2 1.4 collective-permute-start.6
  35.7 1.5 collective-permute-start.7
  37.2 6.1 %collective-permute-start.8 = (bf16[256,512]{1,0:T(8,128)(2,1)}, bf16[256,512]{1,0:T(8,128)(2,1)}, u32[]{:S(2)}, u32[]{:S(2)}) collective-permute-start(bf16[256,512]{1,0:T(8,128)(2,1)} %get-tuple-element.25.rest_0_.rest_7_.rest_4_), channel_id=1, source_target_pairs={{0,1},{1,2},{2,3},{3,0},{4,5},{5,6},{6,7},{7,4},{8,9},{9,10},{10,1... | collective-permute-start | bytes 786440 | tf_op jit(solution)/shard_map/ppermute | solution.py:600
  43.3 2.2 %stack.1.rest_11_.rest_0_ = bf16[2,4,64,1024]{3,2,1,0:T(8,128)(2,1)} custom-call(bf16[2,64,1024]{2,1,0:T(8,128)(2,1)} %get-tuple-element.24.rest_0_, bf16[2,64,1024]{2,1,0:T(8,128)(2,1)} %collective-permute-done.3.rest_1_, bf16[2,64,1024]{2,1,0:T(8,128)(2,1)} %collective-permute-done.4.rest_2_, bf16[2,64,1024]{2,1,0:T(8,128)(2,1)} %collective-permute-done.5.rest_3_, ...), custom_call_target="tpu_custom_call" | custom-call | flops 1024 | bytes 1024 | tf_op jit(solution)/shard_map/stack/pallas_call | solution.py:517
  45.4 0.6 collective-permute-start.9
  46.0 0.6 collective-permute-start.10
  46.7 3.1 %collective-permute-done.8.rest_12_.rest_5_ = bf16[256,512]{1,0:T(8,128)(2,1)} collective-permute-done((bf16[256,512]{1,0:T(8,128)(2,1)}, bf16[256,512]{1,0:T(8,128)(2,1)}, u32[]{:S(2)}, u32[]{:S(2)}) %collective-permute-start.8) | collective-permute-done | bytes 262176 | tf_op jit(solution)/shard_map/ppermute | solution.py:600
  49.8 1.0 collective-permute-done.7.rest_4_
  50.8 7.6 %backward_attention.1.g_ref.rest_4_ = bf16[256,1536]{1,0:T(8,128)(2,1)} custom-call(f32[1,4]{1,0:T(1,128)} %broadcast_multiply_fusion.factor_ref, bf16[2,64,4096]{2,1,0:T(8,128)(2,1)} %collective-permute-done.ins_ref.rest_0_, bf16[2,64,4096]{2,1,0:T(8,128)(2,1)} %collective-permute-done.1.first_ref.rest_1_, ...), custom_call_target="tpu_custom_call" | custom-call | flops 1024 | bytes 1024 | tf_op jit(solution)/shard_map/backward_attention/pallas_call | solution.py:246
  58.5 8.9 %collective-permute-start.11 = (bf16[256,1536]{1,0:T(8,128)(2,1)}, bf16[256,1536]{1,0:T(8,128)(2,1)}, u32[]{:S(2)}, u32[]{:S(2)}) collective-permute-start(bf16[256,1536]{1,0:T(8,128)(2,1)} %backward_attention.1.g_ref.rest_4_), channel_id=1, source_target_pairs={{0,1},{1,2},{2,3},{4,5},{5,6},{6,7},{8,9},{9,10},{10,11},{12,13},{... | collective-permute-start | bytes 2359304 | tf_op jit(solution)/shard_map/ppermute | solution.py:605
  67.3 1.3 collective-permute-start.12
  68.6 9.0 %input_grads.1 = (bf16[2,64,4096]{2,1,0:T(8,128)(2,1)}, bf16[2,64,4096]{2,1,0:T(8,128)(2,1)}) custom-call(bf16[256,1536]{1,0:T(8,128)(2,1)} %backward_attention.1.g_ref.rest_4_, bf16[4096,512]{1,0:T(8,128)(2,1)} %bitcast.32, bf16[4096,512]{1,0:T(8,128)(2,1)} %bitcast.34, bf16[4096,512]{1,0:T(8,128)(2,1)} %bitcast.36), custom_call_target="tpu_custom_call" | custom-call | flops 1024 | bytes 1024 | tf_op jit(solution)/shard_map/input_grads/pallas_call | solution.py:288
  77.7 0.0 collective-permute-done.9.rest_0_.rest_1_
  77.7 0.0 collective-permute-done.10.rest_1_.rest_2_
  77.7 2.2 %passed.1.rest_10_ = bf16[2,64,4096]{2,1,0:T(8,128)(2,1)} custom-call(bf16[2,64,4096]{2,1,0:T(8,128)(2,1)} %get-tuple-element.32.value_ref, bf16[2,4,64,1024]{3,2,1,0:T(8,128)(2,1)} %collective-permute-done.9.rest_0_.rest_1_, bf16[2,4,64,1024]{3,2,1,0:T(8,128)(2,1)} %collective-permute-done.10.rest_1_.rest_2_), custom_call_target="tpu_custom_call" | custom-call | flops 1024 | bytes 1024 | tf_op jit(solution)/shard_map/passed/pallas_call | solution.py:562
  79.9 0.7 collective-permute-start.14
  80.6 0.7 collective-permute-done.11.rest_11_.rest_5_
  81.3 5.3 %collective-permute-start.17 = (bf16[256,1536]{1,0:T(8,128)(2,1)}, bf16[256,1536]{1,0:T(8,128)(2,1)}, u32[]{:S(2)}, u32[]{:S(2)}) collective-permute-start(bf16[256,1536]{1,0:T(8,128)(2,1)} %collective-permute-done.11.rest_11_.rest_5_), channel_id=1, source_target_pairs={{0,1},{1,2},{2,3},{4,5},{5,6},{6,7},{8,9},{9,10},{10,11},{12,13},{... | collective-permute-start | bytes 2359304 | tf_op jit(solution)/shard_map/ppermute | solution.py:605
  86.6 1.5 collective-permute-start.18
  88.1 1.6 collective-permute-start.16
  89.6 13.3 %forward_terms.1 = (bf16[2,64,4096]{2,1,0:T(8,128)(2,1)}, bf16[2,64,4096]{2,1,0:T(8,128)(2,1)}) custom-call(s32[2,2]{1,0:T(2,128)} %bitcast.56, s32[2]{0:T(128)} %bitcast.58, f32[1,4]{1,0:T(1,128)} %broadcast_multiply_fusion.factor_ref, bf16[2,64,4096]{2,1,0:T(8,128)(2,1)} %collective-permute-done.ins_ref.rest_0_, ...), custom_call_target="tpu_custom_call" | custom-call | flops 1024 | bytes 1024 | tf_op jit(solution)/shard_map/forward_terms/pallas_call | solution.py:344
  102.9 0.9 collective-permute-start.13
  103.8 5.5 %collective-permute-start.19 = (bf16[256,1536]{1,0:T(8,128)(2,1)}, bf16[256,1536]{1,0:T(8,128)(2,1)}, u32[]{:S(2)}, u32[]{:S(2)}) collective-permute-start(bf16[256,1536]{1,0:T(8,128)(2,1)} %collective-permute-done.17.rest_1_.rest_6_), channel_id=1, source_target_pairs={{0,1},{1,2},{2,3},{4,5},{5,6},{6,7},{8,9},{9,10},{10,11},{12,13},{... | collective-permute-start | bytes 2359304 | tf_op jit(solution)/shard_map/ppermute | solution.py:605
  109.4 1.3 collective-permute-start.20
  110.6 0.0 collective-permute-done.14.came_ref
  110.7 2.1 %add.46 = bf16[64,4096]{1,0:T(8,128)(2,1)} custom-call(bf16[2,64,4096]{2,1,0:T(8,128)(2,1)} %get-tuple-element.35.near_ref, bf16[2,64,4096]{2,1,0:T(8,128)(2,1)} %collective-permute-done.14.came_ref, bf16[2,64,4096]{2,1,0:T(8,128)(2,1)} %get-tuple-element.33.rest_0_.near_ref), custom_call_target="tpu_custom_call" | custom-call | flops 1024 | bytes 1024 | tf_op jit(solution)/shard_map/add/pallas_call | solution.py:541
  112.8 0.6 collective-permute-start.15
  113.4 9.0 %collective-permute-done.15.last_ref = bf16[64,4096]{1,0:T(8,128)(2,1)} collective-permute-done((bf16[64,4096]{1,0:T(8,128)(2,1)}, bf16[64,4096]{1,0:T(8,128)(2,1)}, u32[]{:S(2)}, u32[]{:S(2)}) %collective-permute-start.15) | collective-permute-done | bytes 524320 | tf_op jit(solution)/shard_map/ppermute | solution.py:589
  122.4 4.1 %back.1 = (bf16[64,4096]{1,0:T(8,128)(2,1)}, f32[1,4096]{1,0:T(1,128)}) custom-call(bf16[2,64,4096]{2,1,0:T(8,128)(2,1)} %get-tuple-element.35.near_ref, bf16[2,64,4096]{2,1,0:T(8,128)(2,1)} %collective-permute-done.14.came_ref, bf16[64,4096]{1,0:T(8,128)(2,1)} %collective-permute-done.15.last_ref, bf16[64,4096]{1,0:T(8,128)(2,1)} %bitcast.41, ...), custom_call_target="tpu_custom_call" | custom-call | flops 1024 | bytes 1024 | tf_op jit(solution)/shard_map/back/pallas_call | solution.py:373
  126.5 0.0 collective-permute-done.13.came_ref
  126.5 0.0 collective-permute-done.19.rest_1_.rest_7_
  126.5 2.1 %add.47.rest_0_ = bf16[64,4096]{1,0:T(8,128)(2,1)} custom-call(bf16[2,64,4096]{2,1,0:T(8,128)(2,1)} %get-tuple-element.33.rest_0_.near_ref, bf16[2,64,4096]{2,1,0:T(8,128)(2,1)} %collective-permute-done.13.came_ref, bf16[64,4096]{1,0:T(8,128)(2,1)} %get-tuple-element.36.rest_0_, bf16[256,1536]{1,0:T(8,128)(2,1)} %collective-permute-done.19.rest_1_.rest_7_, ...), custom_call_target="tpu_custom_call" | custom-call | flops 1024 | bytes 1024 | tf_op jit(solution)/shard_map/add/pallas_call | solution.py:541
  128.6 0.6 collective-permute-start.21
  129.2 1.1 collective-permute-start.22
  130.3 2.9 %collective-permute-done.22.came_ref = f32[1,4096]{1,0:T(1,128)} collective-permute-done((f32[1,4096]{1,0:T(1,128)}, f32[1,4096]{1,0:T(1,128)}, u32[]{:S(2)}, u32[]{:S(2)}) %collective-permute-start.22) | collective-permute-done | bytes 16416 | tf_op jit(solution)/shard_map/ppermute | solution.py:589
  133.3 1.3 gain_added.2.rest_11_.own_ref
  134.6 1.5 collective-permute-start.25
  136.1 1.2 collective-permute-start.23
  137.3 3.9 %collective-permute-start.24 = (bf16[256,512]{1,0:T(8,128)(2,1)}, bf16[256,512]{1,0:T(8,128)(2,1)}, u32[]{:S(2)}, u32[]{:S(2)}) collective-permute-start(bf16[256,512]{1,0:T(8,128)(2,1)} %get-tuple-element.25.rest_0_.rest_7_.rest_4_), channel_id=1, source_target_pairs={{0,3},{1,0},{2,1},{3,2},{4,7},{5,4},{6,5},{7,6},{8,11},{9,8},{10,9... | collective-permute-start | bytes 786440 | tf_op jit(solution)/shard_map/ppermute | solution.py:600
  141.1 7.4 %weight_grads.1 = (bf16[1024,512]{1,0:T(8,128)(2,1)}, bf16[1024,512]{1,0:T(8,128)(2,1)}, bf16[1024,512]{1,0:T(8,128)(2,1)}) custom-call(bf16[2,4,64,1024]{3,2,1,0:T(8,128)(2,1)} %stack.1.rest_11_.rest_0_, bf16[2,4,64,1024]{3,2,1,0:T(8,128)(2,1)} %collective-permute-done.9.rest_0_.rest_1_, bf16[2,4,64,1024]{3,2,1,0:T(8,128)(2,1)} %collective-permute-done.10.rest_1_.rest_2_, ...), custom_call_target="tpu_custom_call" | custom-call | flops 1024 | bytes 1024 | tf_op jit(solution)/shard_map/weight_grads/pallas_call | solution.py:457
  148.5 0.0 collective-permute-done.21.rest_1_
  148.5 1.3 gain_added.3.rest_8_
  149.9 0.4 collective-permute-start.27
  150.3 2.0 %collective-permute-start.26 = (f32[1,4096]{1,0:T(1,128)}, f32[1,4096]{1,0:T(1,128)}, u32[]{:S(2)}, u32[]{:S(2)}) collective-permute-start(f32[1,4096]{1,0:T(1,128)} %gain_added.3.rest_8_), channel_id=1, source_target_pairs={{0,1},{1,2},{2,3},{3,0},{4,5},{5,6},{6,7},{7,4},{8,9},{9,10},{10,1... | collective-permute-start | bytes 49160 | tf_op jit(solution)/shard_map/ppermute | solution.py:600
  152.3 2.6 %fusion.1 = bf16[1,1,64,4096]{3,2,1,0:T(8,128)(2,1)} fusion(bf16[64,4096]{1,0:T(8,128)(2,1)} %collective-permute-done.21.rest_1_, bf16[2,64,4096]{2,1,0:T(8,128)(2,1)} %collective-permute-done.13.came_ref, bf16[2,64,4096]{2,1,0:T(8,128)(2,1)} %collective-permute-done.ins_ref.rest_0_, bf16[2,64,4096]{2,1,0:T(8,128)(2,1)} %get-tuple-element.33.rest_0_.near_ref), kind=kLoop, calls=%fused_computation.3 | loop fusion | flops 2097152 | bytes 2621440 | tf_op jit(solution)/shard_map/broadcast_in_dim | solution.py:698
  154.9 4.4 %out_weight_grads.1 = bf16[512,1024]{1,0:T(8,128)(2,1)} custom-call(bf16[2,4,64,1024]{3,2,1,0:T(8,128)(2,1)} %stack.1.rest_11_.rest_0_, bf16[2,4,64,1024]{3,2,1,0:T(8,128)(2,1)} %collective-permute-done.9.rest_0_.rest_1_, bf16[2,4,64,1024]{3,2,1,0:T(8,128)(2,1)} %collective-permute-done.10.rest_1_.rest_2_, ...), custom_call_target="tpu_custom_call" | custom-call | flops 1024 | bytes 1024 | tf_op jit(solution)/shard_map/out_weight_grads/pallas_call | solution.py:457
  159.3 1.4 add_add_fusion
  (13 shorter events, 0.0 us)
Async XLA Ops:
  2.8 4.3 %collective-permute-start = (bf16[2,64,4096]{2,1,0:T(8,128)(2,1)}, bf16[2,64,4096]{2,1,0:T(8,128)(2,1)}, u32[]{:S(2)}, u32[]{:S(2)}) collective-permute-start(bf16[2,64,4096]{2,1,0:T(8,128)(2,1)} %pick.1), channel_id=1, source_target_pairs={{0,16},{4,20},{8,24},{12,28},{16,0},{20,4},{24,8},{28,12},{1,17},{... | collective-permute-start | bytes 3145736 | tf_op jit(solution)/shard_map/ppermute | solution.py:595
  3.4 26.4 %collective-permute-start.1 = (bf16[2,64,4096]{2,1,0:T(8,128)(2,1)}, bf16[2,64,4096]{2,1,0:T(8,128)(2,1)}, u32[]{:S(2)}, u32[]{:S(2)}) collective-permute-start(bf16[2,64,4096]{2,1,0:T(8,128)(2,1)} %pick.1), channel_id=1, source_target_pairs={{0,20},{4,16},{8,28},{12,24},{16,4},{20,0},{24,12},{28,8},{1,21},{... | collective-permute-start | bytes 3145736 | tf_op jit(solution)/shard_map/ppermute | solution.py:595
  6.0 25.5 %collective-permute-start.2 = (bf16[2,64,4096]{2,1,0:T(8,128)(2,1)}, bf16[2,64,4096]{2,1,0:T(8,128)(2,1)}, u32[]{:S(2)}, u32[]{:S(2)}) collective-permute-start(bf16[2,64,4096]{2,1,0:T(8,128)(2,1)} %pick.1), channel_id=1, source_target_pairs={{0,24},{4,28},{8,16},{12,20},{16,8},{20,12},{24,0},{28,4},{1,25},{... | collective-permute-start | bytes 3145736 | tf_op jit(solution)/shard_map/ppermute | solution.py:595
  9.8 21.7 %collective-permute-start.3 = (bf16[2,64,1024]{2,1,0:T(8,128)(2,1)}, bf16[2,64,1024]{2,1,0:T(8,128)(2,1)}, u32[]{:S(2)}, u32[]{:S(2)}) collective-permute-start(bf16[2,64,1024]{2,1,0:T(8,128)(2,1)} %get-tuple-element.26), channel_id=1, source_target_pairs={{0,1},{1,2},{2,3},{3,0},{4,5},{5,6},{6,7},{7,4},{8,9},{9,10},{10,1... | collective-permute-start | bytes 786440 | tf_op jit(solution)/shard_map/ppermute | solution.py:600
  11.6 20.4 %collective-permute-start.4 = (bf16[2,64,1024]{2,1,0:T(8,128)(2,1)}, bf16[2,64,1024]{2,1,0:T(8,128)(2,1)}, u32[]{:S(2)}, u32[]{:S(2)}) collective-permute-start(bf16[2,64,1024]{2,1,0:T(8,128)(2,1)} %get-tuple-element.27), channel_id=1, source_target_pairs={{0,2},{1,3},{2,0},{3,1},{4,6},{5,7},{6,4},{7,5},{8,10},{9,11},{10,... | collective-permute-start | bytes 786440 | tf_op jit(solution)/shard_map/ppermute | solution.py:600
  14.2 17.9 %collective-permute-start.5 = (bf16[2,64,1024]{2,1,0:T(8,128)(2,1)}, bf16[2,64,1024]{2,1,0:T(8,128)(2,1)}, u32[]{:S(2)}, u32[]{:S(2)}) collective-permute-start(bf16[2,64,1024]{2,1,0:T(8,128)(2,1)} %get-tuple-element.28), channel_id=1, source_target_pairs={{0,3},{1,0},{2,1},{3,2},{4,7},{5,4},{6,5},{7,6},{8,11},{9,8},{10,9... | collective-permute-start | bytes 786440 | tf_op jit(solution)/shard_map/ppermute | solution.py:600
  34.2 15.6 %collective-permute-start.6 = (bf16[2,32,4096]{2,1,0:T(8,128)(2,1)}, bf16[2,32,4096]{2,1,0:T(8,128)(2,1)}, u32[]{:S(2)}, u32[]{:S(2)}) collective-permute-start(bf16[2,32,4096]{2,1,0:T(8,128)(2,1)} %get-tuple-element.29.rest_4_), channel_id=1, source_target_pairs={{0,4},{4,0},{8,12},{12,8},{1,5},{5,1},{9,13},{13,9},{2,6},{6,2},{1... | collective-permute-start | bytes 1572872 | tf_op jit(solution)/shard_map/ppermute | solution.py:589
  35.7 15.2 %collective-permute-start.7 = (bf16[2,32,4096]{2,1,0:T(8,128)(2,1)}, bf16[2,32,4096]{2,1,0:T(8,128)(2,1)}, u32[]{:S(2)}, u32[]{:S(2)}) collective-permute-start(bf16[2,32,4096]{2,1,0:T(8,128)(2,1)} %get-tuple-element.30), channel_id=1, source_target_pairs={{0,8},{4,12},{8,0},{12,4},{1,9},{5,13},{9,1},{13,5},{2,10},{6,14},... | collective-permute-start | bytes 1572872 | tf_op jit(solution)/shard_map/ppermute | solution.py:589
  37.2 12.6 %collective-permute-start.8 = (bf16[256,512]{1,0:T(8,128)(2,1)}, bf16[256,512]{1,0:T(8,128)(2,1)}, u32[]{:S(2)}, u32[]{:S(2)}) collective-permute-start(bf16[256,512]{1,0:T(8,128)(2,1)} %get-tuple-element.25.rest_0_.rest_7_.rest_4_), channel_id=1, source_target_pairs={{0,1},{1,2},{2,3},{3,0},{4,5},{5,6},{6,7},{7,4},{8,9},{9,10},{10,1... | collective-permute-start | bytes 786440 | tf_op jit(solution)/shard_map/ppermute | solution.py:600
  45.4 32.2 %collective-permute-start.9 = (bf16[2,4,64,1024]{3,2,1,0:T(8,128)(2,1)}, bf16[2,4,64,1024]{3,2,1,0:T(8,128)(2,1)}, u32[]{:S(2)}, u32[]{:S(2)}) collective-permute-start(bf16[2,4,64,1024]{3,2,1,0:T(8,128)(2,1)} %stack.1.rest_11_.rest_0_), channel_id=1, source_target_pairs={{0,4},{4,0},{8,12},{12,8},{1,5},{5,1},{9,13},{13,9},{2,6},{6,2},{1... | collective-permute-start | bytes 3145736 | tf_op jit(solution)/shard_map/ppermute | solution.py:589
  46.0 31.6 %collective-permute-start.10 = (bf16[2,4,64,1024]{3,2,1,0:T(8,128)(2,1)}, bf16[2,4,64,1024]{3,2,1,0:T(8,128)(2,1)}, u32[]{:S(2)}, u32[]{:S(2)}) collective-permute-start(bf16[2,4,64,1024]{3,2,1,0:T(8,128)(2,1)} %stack.1.rest_11_.rest_0_), channel_id=1, source_target_pairs={{0,8},{4,12},{8,0},{12,4},{1,9},{5,13},{9,1},{13,5},{2,10},{6,14},... | collective-permute-start | bytes 3145736 | tf_op jit(solution)/shard_map/ppermute | solution.py:589
  58.5 22.8 %collective-permute-start.11 = (bf16[256,1536]{1,0:T(8,128)(2,1)}, bf16[256,1536]{1,0:T(8,128)(2,1)}, u32[]{:S(2)}, u32[]{:S(2)}) collective-permute-start(bf16[256,1536]{1,0:T(8,128)(2,1)} %backward_attention.1.g_ref.rest_4_), channel_id=1, source_target_pairs={{0,1},{1,2},{2,3},{4,5},{5,6},{6,7},{8,9},{9,10},{10,11},{12,13},{... | collective-permute-start | bytes 2359304 | tf_op jit(solution)/shard_map/ppermute | solution.py:605
  67.3 19.3 %collective-permute-start.12 = (bf16[256,1536]{1,0:T(8,128)(2,1)}, bf16[256,1536]{1,0:T(8,128)(2,1)}, u32[]{:S(2)}, u32[]{:S(2)}) collective-permute-start(bf16[256,1536]{1,0:T(8,128)(2,1)} %backward_attention.1.g_ref.rest_4_), channel_id=1, source_target_pairs={{1,0},{2,1},{3,2},{5,4},{6,5},{7,6},{9,8},{10,9},{11,10},{13,12},{... | collective-permute-start | bytes 2359304 | tf_op jit(solution)/shard_map/ppermute | solution.py:605
  79.9 30.7 %collective-permute-start.14 = (bf16[2,64,4096]{2,1,0:T(8,128)(2,1)}, bf16[2,64,4096]{2,1,0:T(8,128)(2,1)}, u32[]{:S(2)}, u32[]{:S(2)}) collective-permute-start(bf16[2,64,4096]{2,1,0:T(8,128)(2,1)} %passed.1.rest_10_), channel_id=1, source_target_pairs={{0,4},{4,0},{8,12},{12,8},{1,5},{5,1},{9,13},{13,9},{2,6},{6,2},{1... | collective-permute-start | bytes 3145736 | tf_op jit(solution)/shard_map/ppermute | solution.py:589
  81.3 22.6 %collective-permute-start.17 = (bf16[256,1536]{1,0:T(8,128)(2,1)}, bf16[256,1536]{1,0:T(8,128)(2,1)}, u32[]{:S(2)}, u32[]{:S(2)}) collective-permute-start(bf16[256,1536]{1,0:T(8,128)(2,1)} %collective-permute-done.11.rest_11_.rest_5_), channel_id=1, source_target_pairs={{0,1},{1,2},{2,3},{4,5},{5,6},{6,7},{8,9},{9,10},{10,11},{12,13},{... | collective-permute-start | bytes 2359304 | tf_op jit(solution)/shard_map/ppermute | solution.py:605
  86.6 22.8 %collective-permute-start.18 = (bf16[256,1536]{1,0:T(8,128)(2,1)}, bf16[256,1536]{1,0:T(8,128)(2,1)}, u32[]{:S(2)}, u32[]{:S(2)}) collective-permute-start(bf16[256,1536]{1,0:T(8,128)(2,1)} %collective-permute-done.12.rest_12_.rest_8_), channel_id=1, source_target_pairs={{1,0},{2,1},{3,2},{5,4},{6,5},{7,6},{9,8},{10,9},{11,10},{13,12},{... | collective-permute-start | bytes 2359304 | tf_op jit(solution)/shard_map/ppermute | solution.py:605
  88.1 25.3 %collective-permute-start.16 = (bf16[2,4,64,1024]{3,2,1,0:T(8,128)(2,1)}, bf16[2,4,64,1024]{3,2,1,0:T(8,128)(2,1)}, u32[]{:S(2)}, u32[]{:S(2)}) collective-permute-start(bf16[2,4,64,1024]{3,2,1,0:T(8,128)(2,1)} %collective-permute-done.9.rest_0_.rest_1_), channel_id=1, source_target_pairs={{0,8},{4,12},{8,0},{12,4},{1,9},{5,13},{9,1},{13,5},{2,10},{6,14},... | collective-permute-start | bytes 3145736 | tf_op jit(solution)/shard_map/ppermute | solution.py:589
  102.9 23.5 %collective-permute-start.13 = (bf16[2,64,4096]{2,1,0:T(8,128)(2,1)}, bf16[2,64,4096]{2,1,0:T(8,128)(2,1)}, u32[]{:S(2)}, u32[]{:S(2)}) collective-permute-start(bf16[2,64,4096]{2,1,0:T(8,128)(2,1)} %get-tuple-element.34), channel_id=1, source_target_pairs={{0,4},{4,0},{8,12},{12,8},{1,5},{5,1},{9,13},{13,9},{2,6},{6,2},{1... | collective-permute-start | bytes 3145736 | tf_op jit(solution)/shard_map/ppermute | solution.py:589
  103.8 22.6 %collective-permute-start.19 = (bf16[256,1536]{1,0:T(8,128)(2,1)}, bf16[256,1536]{1,0:T(8,128)(2,1)}, u32[]{:S(2)}, u32[]{:S(2)}) collective-permute-start(bf16[256,1536]{1,0:T(8,128)(2,1)} %collective-permute-done.17.rest_1_.rest_6_), channel_id=1, source_target_pairs={{0,1},{1,2},{2,3},{4,5},{5,6},{6,7},{8,9},{9,10},{10,11},{12,13},{... | collective-permute-start | bytes 2359304 | tf_op jit(solution)/shard_map/ppermute | solution.py:605
  109.4 17.1 %collective-permute-start.20 = (bf16[256,1536]{1,0:T(8,128)(2,1)}, bf16[256,1536]{1,0:T(8,128)(2,1)}, u32[]{:S(2)}, u32[]{:S(2)}) collective-permute-start(bf16[256,1536]{1,0:T(8,128)(2,1)} %collective-permute-done.18.rest_2_.rest_9_), channel_id=1, source_target_pairs={{1,0},{2,1},{3,2},{5,4},{6,5},{7,6},{9,8},{10,9},{11,10},{13,12},{... | collective-permute-start | bytes 2359304 | tf_op jit(solution)/shard_map/ppermute | solution.py:605
  112.8 9.6 %collective-permute-start.15 = (bf16[64,4096]{1,0:T(8,128)(2,1)}, bf16[64,4096]{1,0:T(8,128)(2,1)}, u32[]{:S(2)}, u32[]{:S(2)}) collective-permute-start(bf16[64,4096]{1,0:T(8,128)(2,1)} %add.46), channel_id=1, source_target_pairs={{0,8},{4,12},{8,0},{12,4},{1,9},{5,13},{9,1},{13,5},{2,10},{6,14},... | collective-permute-start | bytes 1572872 | tf_op jit(solution)/shard_map/ppermute | solution.py:589
  128.6 19.9 %collective-permute-start.21 = (bf16[64,4096]{1,0:T(8,128)(2,1)}, bf16[64,4096]{1,0:T(8,128)(2,1)}, u32[]{:S(2)}, u32[]{:S(2)}) collective-permute-start(bf16[64,4096]{1,0:T(8,128)(2,1)} %add.47.rest_0_), channel_id=1, source_target_pairs={{0,8},{4,12},{8,0},{12,4},{1,9},{5,13},{9,1},{13,5},{2,10},{6,14},... | collective-permute-start | bytes 1572872 | tf_op jit(solution)/shard_map/ppermute | solution.py:589
  129.2 4.1 %collective-permute-start.22 = (f32[1,4096]{1,0:T(1,128)}, f32[1,4096]{1,0:T(1,128)}, u32[]{:S(2)}, u32[]{:S(2)}) collective-permute-start(f32[1,4096]{1,0:T(1,128)} %get-tuple-element.37.own_ref), channel_id=1, source_target_pairs={{0,4},{4,0},{8,12},{12,8},{1,5},{5,1},{9,13},{13,9},{2,6},{6,2},{1... | collective-permute-start | bytes 49160 | tf_op jit(solution)/shard_map/ppermute | solution.py:589
  134.6 13.9 %collective-permute-start.25 = (f32[1,4096]{1,0:T(1,128)}, f32[1,4096]{1,0:T(1,128)}, u32[]{:S(2)}, u32[]{:S(2)}) collective-permute-start(f32[1,4096]{1,0:T(1,128)} %gain_added.2.rest_11_.own_ref), channel_id=1, source_target_pairs={{0,8},{4,12},{8,0},{12,4},{1,9},{5,13},{9,1},{13,5},{2,10},{6,14},... | collective-permute-start | bytes 49160 | tf_op jit(solution)/shard_map/ppermute | solution.py:589
  136.1 18.8 %collective-permute-start.23 = (bf16[256,512]{1,0:T(8,128)(2,1)}, bf16[256,512]{1,0:T(8,128)(2,1)}, u32[]{:S(2)}, u32[]{:S(2)}) collective-permute-start(bf16[256,512]{1,0:T(8,128)(2,1)} %get-tuple-element.25.rest_0_.rest_7_.rest_4_), channel_id=1, source_target_pairs={{0,2},{1,3},{2,0},{3,1},{4,6},{5,7},{6,4},{7,5},{8,10},{9,11},{10,... | collective-permute-start | bytes 786440 | tf_op jit(solution)/shard_map/ppermute | solution.py:600
  137.3 17.6 %collective-permute-start.24 = (bf16[256,512]{1,0:T(8,128)(2,1)}, bf16[256,512]{1,0:T(8,128)(2,1)}, u32[]{:S(2)}, u32[]{:S(2)}) collective-permute-start(bf16[256,512]{1,0:T(8,128)(2,1)} %get-tuple-element.25.rest_0_.rest_7_.rest_4_), channel_id=1, source_target_pairs={{0,3},{1,0},{2,1},{3,2},{4,7},{5,4},{6,5},{7,6},{8,11},{9,8},{10,9... | collective-permute-start | bytes 786440 | tf_op jit(solution)/shard_map/ppermute | solution.py:600
  149.9 9.4 %collective-permute-start.28 = (f32[1,4096]{1,0:T(1,128)}, f32[1,4096]{1,0:T(1,128)}, u32[]{:S(2)}, u32[]{:S(2)}) collective-permute-start(f32[1,4096]{1,0:T(1,128)} %gain_added.3.rest_8_), channel_id=1, source_target_pairs={{0,3},{1,0},{2,1},{3,2},{4,7},{5,4},{6,5},{7,6},{8,11},{9,8},{10,9... | collective-permute-start | bytes 49160 | tf_op jit(solution)/shard_map/ppermute | solution.py:600
  149.9 9.4 %collective-permute-start.27 = (f32[1,4096]{1,0:T(1,128)}, f32[1,4096]{1,0:T(1,128)}, u32[]{:S(2)}, u32[]{:S(2)}) collective-permute-start(f32[1,4096]{1,0:T(1,128)} %gain_added.3.rest_8_), channel_id=1, source_target_pairs={{0,2},{1,3},{2,0},{3,1},{4,6},{5,7},{6,4},{7,5},{8,10},{9,11},{10,... | collective-permute-start | bytes 49160 | tf_op jit(solution)/shard_map/ppermute | solution.py:600
  150.3 9.0 %collective-permute-start.26 = (f32[1,4096]{1,0:T(1,128)}, f32[1,4096]{1,0:T(1,128)}, u32[]{:S(2)}, u32[]{:S(2)}) collective-permute-start(f32[1,4096]{1,0:T(1,128)} %gain_added.3.rest_8_), channel_id=1, source_target_pairs={{0,1},{1,2},{2,3},{3,0},{4,5},{5,6},{6,7},{7,4},{8,9},{9,10},{10,1... | collective-permute-start | bytes 49160 | tf_op jit(solution)/shard_map/ppermute | solution.py:600

commit v5 on v4

--- a/solution.py
+++ b/solution.py
@@ -50,6 +50,28 @@
         copy.start()
     for copy in copies:
         copy.wait()
+
+
+def carry(pairs, held, sems):
+    loads = [pltpu.make_async_copy(a, held.at[i], sems.at[0, i]) for i, (a, _) in enumerate(pairs)]
+    stores = [pltpu.make_async_copy(held.at[i], b, sems.at[1, i]) for i, (_, b) in enumerate(pairs)]
+    for load in loads:
+        load.start()
+    for load, store in zip(loads, stores):
+        load.wait()
+        store.start()
+    for store in stores:
+        store.wait()
+
+
+def carry_scratch(count, rows, width):
+    return [pltpu.VMEM((count, rows, width), BF16), pltpu.SemaphoreType.DMA((2, count))]
+
+
+def row_pieces(source, target):
+    return [
+        (source.at[pl.ds(at, 16)], target.at[pl.ds(at, 16)]) for at in range(0, source.shape[0], 16)
+    ]
 
 
 def normalized(rows, gain):
@@ -81,16 +103,11 @@
     return lifted / jnp.sum(lifted, axis=-1, keepdims=True)
 
 
-def pick_kernel(forward_ref, encoded_ref, grad_ref, head_ref, out_ref, sems):
+def pick_kernel(forward_ref, encoded_ref, grad_ref, head_ref, out_ref, held, sems):
     section = lax.axis_index("pipe")
 
     def both(first, second):
-        run_copies(
-            [
-                pltpu.make_async_copy(first, out_ref.at[0], sems.at[0]),
-                pltpu.make_async_copy(second, out_ref.at[1], sems.at[1]),
-            ]
-        )
+        carry(row_pieces(first, out_ref.at[0]) + row_pieces(second, out_ref.at[1]), held, sems)
 
     @pl.when(section == 0)
     def _():
@@ -102,11 +119,13 @@
 
 
 def pick(sent_forward, encoded, grad_sent, head):
+    rows, model = encoded.shape
     return pl.pallas_call(
         pick_kernel,
-        out_shape=sds((2,) + encoded.shape, BF16),
+        out_shape=sds((2, rows, model), BF16),
         in_specs=[HBM] * 4,
-        scratch_shapes=[pltpu.SemaphoreType.DMA((2,))],
+        out_specs=HBM,
+        scratch_shapes=carry_scratch(rows // 8, 16, model),
         compiler_params=params(),
         cost_estimate=SMALL,
         name="pick",
@@ -380,6 +399,10 @@
     )(near, came, last, x, ins, gain, *after)
 
 
+def ring_device(place, n):
+    return 2 * place if place < (n + 1) // 2 else 2 * (n - 1 - place) + 1
+
+
 def slice_copies(which, parts, cols, sems):
     seq, dp = lax.axis_index("seq"), lax.axis_index("dp")
     copies = []
@@ -394,27 +417,17 @@
 
 
 def weight_kernel(n_seq, n_dp, *rest):
-    parts, own, rest = rest[:n_seq], rest[n_seq], rest[n_seq + 1 :]
-    lower, upper = rest[: n_dp - 1], rest[n_dp - 1 : 2 * n_dp - 2]
+    parts, factors_in = rest[:n_seq], rest[n_seq : n_seq + n_dp]
     out_q, out_k, out_v, cols, grads, sems, own_sems = rest[-7:]
     me = lax.axis_index("dp")
-
-    def grad_copies(act):
-        act(pltpu.make_async_copy(own, grads.at[me], own_sems.at[0]))
-        for k in range(1, n_dp):
-            spot = grads.at[lax.rem(me + n_dp - k, n_dp)]
-
-            @pl.when(me >= k)
-            def _():
-                act(pltpu.make_async_copy(lower[k - 1], spot, own_sems.at[k]))
-
-            @pl.when(me < k)
-            def _():
-                act(pltpu.make_async_copy(upper[n_dp - k - 1], spot, own_sems.at[k]))
-
-    grad_copies(lambda copy: copy.start())
-    run_copies(slice_copies(0, parts, cols, sems))
-    grad_copies(lambda copy: copy.wait())
+    half = me // 2
+    place = jnp.where(me % 2 == 0, half, n_dp - 1 - half)
+    copies = slice_copies(0, parts, cols, sems)
+    for t, source in enumerate(factors_in):
+        before = lax.rem(place + n_dp - t, n_dp)
+        sample = jnp.where(before < (n_dp + 1) // 2, 2 * before, 2 * (n_dp - 1 - before) + 1)
+        copies.append(pltpu.make_async_copy(source, grads.at[sample], own_sems.at[t]))
+    run_copies(copies)
     width = out_q.shape[1]
     tile = min(512, out_q.shape[0])
     samples, tokens, _ = cols.shape
@@ -470,10 +483,9 @@
     )(*parts, *factors, *after)
 
 
-def weight_grads(parts, own, lower, upper, after=()):
-    shape = sds((parts[0].shape[3], own.shape[1] // 3), BF16)
-    factors = [own, *lower, *upper]
-    return contracted(weight_kernel, "weight_grads", parts, factors, (shape,) * 3, after)
+def weight_grads(parts, grads, after=()):
+    shape = sds((parts[0].shape[3], grads[0].shape[1] // 3), BF16)
+    return contracted(weight_kernel, "weight_grads", parts, grads, (shape,) * 3, after)
 
 
 def out_weight_grads(parts, atts, after=()):
@@ -482,14 +494,13 @@
 
 
 def half_relay_kernel(first_ref, second_ref, *rest):
-    for_x, for_y, sems = rest[-3:]
-    half = for_x.shape[1]
-    run_copies(
-        [
-            pltpu.make_async_copy(second_ref.at[:, pl.ds(0, half)], for_x, sems.at[0]),
-            pltpu.make_async_copy(first_ref.at[:, pl.ds(half, half)], for_y, sems.at[1]),
-        ]
-    )
+    for_x, for_y, held, sems = rest[-4:]
+    pair, half, _ = for_x.shape
+    pairs = []
+    for i in range(pair):
+        pairs += row_pieces(second_ref.at[i, pl.ds(0, half)], for_x.at[i])
+        pairs += row_pieces(first_ref.at[i, pl.ds(half, half)], for_y.at[i])
+    carry(pairs, held, sems)
 
 
 def half_relayed(first, second, after=()):
@@ -498,7 +509,8 @@
         half_relay_kernel,
         out_shape=(sds((pair, rows // 2, model), BF16),) * 2,
         in_specs=[HBM] * (2 + len(after)),
-        scratch_shapes=[pltpu.SemaphoreType.DMA((2,))],
+        out_specs=(HBM, HBM),
+        scratch_shapes=carry_scratch(pair * rows // 16, 16, model),
         compiler_params=params(),
         cost_estimate=SMALL,
         name="half_relay",
@@ -507,8 +519,8 @@
 
 
 def stack_kernel(n, *rest):
-    out_ref, sems = rest[-2:]
-    run_copies([pltpu.make_async_copy(rest[k], out_ref.at[:, k], sems.at[k]) for k in range(n)])
+    out_ref, held, sems = rest[-3:]
+    carry([(rest[k].at[i], out_ref.at[i, k]) for i in range(2) for k in range(n)], held, sems)
 
 
 def stacked(parts, after=()):
@@ -518,7 +530,8 @@
         functools.partial(stack_kernel, n),
         out_shape=sds((pair, n, rows, width), BF16),
         in_specs=[HBM] * (n + len(after)),
-        scratch_shapes=[pltpu.SemaphoreType.DMA((n,))],
+        out_specs=HBM,
+        scratch_shapes=carry_scratch(pair * n, rows, width),
         compiler_params=params(),
         cost_estimate=SMALL,
         name="stack",
@@ -554,16 +567,18 @@
 
 
 def passed_kernel(value_ref, *rest):
-    out_ref, sems = rest[-2:]
-    run_copies([pltpu.make_async_copy(value_ref, out_ref, sems.at[0])])
+    out_ref, held, sems = rest[-3:]
+    carry(row_pieces(value_ref.at[0], out_ref.at[0]) + row_pieces(value_ref.at[1], out_ref.at[1]), held, sems)
 
 
 def passed(value, after):
+    pair, rows, model = value.shape
     return pl.pallas_call(
         passed_kernel,
         out_shape=sds(value.shape, value.dtype),
         in_specs=[HBM] * (1 + len(after)),
-        scratch_shapes=[pltpu.SemaphoreType.DMA((1,))],
+        out_specs=HBM,
+        scratch_shapes=carry_scratch(pair * rows // 16, 16, model),
         compiler_params=params(),
         cost_estimate=SMALL,
         name="passed",
@@ -600,18 +615,13 @@
     return lax.ppermute(value, axis, [(i, (i + k) % n) for i in range(n)])
 
 
-def shifted(value, axis, by):
+def ring_gathered(value, axis):
     n = lax.axis_size(axis)
-    return lax.ppermute(value, axis, [(i, i + by) for i in range(n) if 0 <= i + by < n])
-
-
-def line_gathered(value, axis):
-    lower, upper, up, down = [], [], value, value
-    for _ in range(lax.axis_size(axis) - 1):
-        up, down = shifted(up, axis, 1), shifted(down, axis, -1)
-        lower.append(up)
-        upper.append(down)
-    return lower, upper
+    pairs = [(ring_device(p, n), ring_device((p + 1) % n, n)) for p in range(n)]
+    values = [value]
+    for _ in range(n - 1):
+        values.append(lax.ppermute(values[-1], axis, pairs))
+    return values
 
 
 def exchanged(parts, axis):
@@ -664,7 +674,7 @@
     cols = [cols] + [swapped(cols, "seq", j) for j in (1, 2)]
 
     grads = backward_attention(factor, ins, soft, wo, att, q, k, v, after=[cols[0], *atts[1:2]])
-    lower, upper = line_gathered(grads, "dp")
+    ring = ring_gathered(grads, "dp")
     dx_near, dx_far = input_grads(grads, wq, wk, wv)
     dx_far = passed(dx_far, after=cols[1:])
     dx_came = swapped(dx_far, "seq", 1)
@@ -676,18 +686,18 @@
         ins,
         norm_gain,
         (wq, wk, wv, wo),
-        after=[dx_far, *lower[:1], *upper[:1]],
+        after=[dx_far, *ring[1:2]],
     )
     mix_came = swapped(mix_far, "seq", 1)
     dx_sum = added(dx_near, dx_came, after=[mix_near])
     dx_last = swapped(dx_sum, "seq", 2)
-    back_out, gain_part = back(dx_near, dx_came, dx_last, x, ins[0], norm_gain, after=[cols[3], *lower[1:2], *upper[1:2]])
-    mix_sum = added(mix_near, mix_came, after=[back_out, *lower[2:3], *upper[2:3]])
+    back_out, gain_part = back(dx_near, dx_came, dx_last, x, ins[0], norm_gain, after=[cols[3], *ring[2:3], *atts[3:]])
+    mix_sum = added(mix_near, mix_came, after=[back_out, *ring[3:4]])
     mix_last = swapped(mix_sum, "seq", 2)
 
     gain_part = gain_added(gain_part, swapped(gain_part, "seq", 1), after=[mix_sum])
     gain_hop = swapped(gain_part, "seq", 2)
-    grad_q, grad_k, grad_v = weight_grads(cols, grads, lower, upper, after=[gain_part])
+    grad_q, grad_k, grad_v = weight_grads(cols, ring, after=[gain_part])
     gain_part = gain_added(gain_part, gain_hop, after=[grad_q, mix_last])
     grad_out = out_weight_grads(cols, atts, after=[gain_part])
     gain_part = summed(gain_part, "dp")

time: 162 us -> 157 us (0.969)
  starting transfers between devices: 58.5 us -> 46.9 us
  waiting for transfers between devices: 28.9 us -> 36.6 us
    ppermute x6 -> x3, starting transfers between devices: 23.7 us -> 6.33 us  [ring_gathered(): values.append(lax.ppermute(values[-1], axis, pairs))]
    ppermute x9, waiting for transfers between devices: 3.68 us -> 16 us  [rotated(): return lax.ppermute(value, axis, [(i, (i + k) % n) for i in range(n)])]
    ppermute x11, waiting for transfers between devices: 12.9 us -> 3.63 us  [swapped(): lax.ppermute(value, axis, [(i, i ^ j) for i in range(lax.axis_size(axis))])]
    ppermute x6 -> x3, waiting for transfers between devices: 0.67 us -> 5.34 us  [ring_gathered(): values.append(lax.ppermute(values[-1], axis, pairs))]
    ppermute x9, starting transfers between devices: 19.2 us -> 23.3 us  [rotated(): return lax.ppermute(value, axis, [(i, (i + k) % n) for i in range(n)])]
    ppermute x11, starting transfers between devices: 11.3 us -> 13 us  [swapped(): lax.ppermute(value, axis, [(i, i ^ j) for i in range(lax.axis_size(axis))])]
  transfers between devices with their start and end apart: 29 -> 26, of which waited for: 8 -> 9; matrix products, arithmetic and copies ran while one was open for 2% -> 2% of each run, Pallas kernels for 38% -> 39%
where the time goes in v5:
time: 157 us; the launch traced here: 156 us
  Pallas kernels  67 us (43%)
  starting transfers between devices  46.9 us (30%)
  waiting for transfers between devices  36.6 us (23%)
  other arithmetic  5.14 us (3%)
    ppermute x9, starting transfers between devices, rotated(): return lax.ppermute(value, axis, [(i, (i + k) % n) for i in range(n)])  23.3 us
    ppermute x9, waiting for transfers between devices, rotated(): return lax.ppermute(value, axis, [(i, (i + k) % n) for i in range(n)])  16 us
    pallas_call x1, Pallas kernels, forward_terms(): pl.pallas_call(functools.partial(forward_kernel, n), out_shape=(sds((2, r...  13.3 us
    ppermute x11, starting transfers between devices, swapped(): lax.ppermute(value, axis, [(i, i ^ j) for i in range(lax.axis_size(axis))])  13 us
    pallas_call x2, Pallas kernels, contracted(): pl.pallas_call(functools.partial(kernel, len(parts), samples), out_shape=...  11.7 us
    ppermute x3, waiting for transfers between devices, crossed(): return lax.ppermute(value, ('pipe', 'seq'), pairs)  11.6 us
    pallas_call x1, Pallas kernels, input_grads(): pl.pallas_call(input_grad_kernel, out_shape=(sds((2, tokens // 4, model),...  9.08 us
    pallas_call x1, Pallas kernels, backward_attention(): pl.pallas_call(functools.partial(backward_kernel, n), out_shape=sds((toke...  7.66 us
  transfers between devices with their start and end apart: 26, of which 9 were waited for; matrix products, arithmetic and copies ran while one was open for 2% of the time, Pallas kernels for 39%

profile of v5, /device:TPU:0, one launch (start us, length us, event | category | flops | bytes accessed | tf_op | source)
XLA Modules:
  0.0 156.4 jit_solution(1834930501075130581)
XLA Ops:
  0.6 2.1 %pick.1 = bf16[2,64,4096]{2,1,0:T(8,128)(2,1)} custom-call(bf16[64,4096]{1,0:T(8,128)(2,1)} %bitcast.51, bf16[64,4096]{1,0:T(8,128)(2,1)} %bitcast.52, bf16[64,4096]{1,0:T(8,128)(2,1)} %bitcast.53, bf16[64,4096]{1,0:T(8,128)(2,1)} %bitcast.54), custom_call_target="tpu_custom_call" | custom-call | flops 1024 | bytes 1024 | tf_op jit(solution)/shard_map/pick/pallas_call | solution.py:123
  2.7 0.5 collective-permute-start
  3.3 2.6 %collective-permute-start.1 = (bf16[2,64,4096]{2,1,0:T(8,128)(2,1)}, bf16[2,64,4096]{2,1,0:T(8,128)(2,1)}, u32[]{:S(2)}, u32[]{:S(2)}) collective-permute-start(bf16[2,64,4096]{2,1,0:T(8,128)(2,1)} %pick.1), channel_id=1, source_target_pairs={{0,20},{4,16},{8,28},{12,24},{16,4},{20,0},{24,12},{28,8},{1,21},{... | collective-permute-start | bytes 3145736 | tf_op jit(solution)/shard_map/ppermute | solution.py:610
  5.9 1.2 collective-permute-start.2
  7.1 0.0 collective-permute-done.ins_ref.rest_0_
  7.1 2.7 %columns.1 = (bf16[2,64,1024]{2,1,0:T(8,128)(2,1)}, bf16[2,64,1024]{2,1,0:T(8,128)(2,1)}, bf16[2,64,1024]{2,1,0:T(8,128)(2,1)}, bf16[2,64,1024]{2,1,0:T(8,128)(2,1)}) custom-call(bf16[64,4096]{1,0:T(8,128)(2,1)} %bitcast.40, bf16[2,64,4096]{2,1,0:T(8,128)(2,1)} %collective-permute-done.ins_ref.rest_0_, f32[1,4096]{1,0:T(1,128)} %gain_ref.3), custom_call_target="tpu_custom_call" | custom-call | flops 1024 | bytes 1024 | tf_op jit(solution)/shard_map/columns/pallas_call | solution.py:150
  9.7 1.8 %collective-permute-start.3 = (bf16[2,64,1024]{2,1,0:T(8,128)(2,1)}, bf16[2,64,1024]{2,1,0:T(8,128)(2,1)}, u32[]{:S(2)}, u32[]{:S(2)}) collective-permute-start(bf16[2,64,1024]{2,1,0:T(8,128)(2,1)} %get-tuple-element.26), channel_id=1, source_target_pairs={{0,1},{1,2},{2,3},{3,0},{4,5},{5,6},{6,7},{7,4},{8,9},{9,10},{10,1... | collective-permute-start | bytes 786440 | tf_op jit(solution)/shard_map/ppermute | solution.py:615
  11.5 2.6 %collective-permute-start.4 = (bf16[2,64,1024]{2,1,0:T(8,128)(2,1)}, bf16[2,64,1024]{2,1,0:T(8,128)(2,1)}, u32[]{:S(2)}, u32[]{:S(2)}) collective-permute-start(bf16[2,64,1024]{2,1,0:T(8,128)(2,1)} %get-tuple-element.27), channel_id=1, source_target_pairs={{0,2},{1,3},{2,0},{3,1},{4,6},{5,7},{6,4},{7,5},{8,10},{9,11},{10,... | collective-permute-start | bytes 786440 | tf_op jit(solution)/shard_map/ppermute | solution.py:615
  14.1 1.3 collective-permute-start.5
  15.4 1.2 broadcast_multiply_fusion.factor_ref
  16.6 3.2 %saved_attention.1 = (f32[4,256,256]{2,1,0:T(8,128)}, bf16[256,512]{1,0:T(8,128)(2,1)}) custom-call(s32[2,2]{1,0:T(2,128)} %bitcast.55, s32[2]{0:T(128)} %bitcast.57, f32[1,4]{1,0:T(1,128)} %broadcast_multiply_fusion.factor_ref, bf16[256,512]{1,0:T(8,128)(2,1)} %bitcast.43, bf16[256,512]{1,0:T(8,128)(2,1)} %bitcast.45, bf16[256,512]{1,0:T(8,128)(2,1)} %bitcast.47, ...), custom_call_target="tpu_custom_call" | custom-call | flops 1024 | bytes 1024 | tf_op jit(solution)/shard_map/saved_attention/pallas_call | solution.py:174
  19.8 9.8 %collective-permute-done.1.first_ref.rest_1_ = bf16[2,64,4096]{2,1,0:T(8,128)(2,1)} collective-permute-done((bf16[2,64,4096]{2,1,0:T(8,128)(2,1)}, bf16[2,64,4096]{2,1,0:T(8,128)(2,1)}, u32[]{:S(2)}, u32[]{:S(2)}) %collective-permute-start.1) | collective-permute-done | bytes 1048608 | tf_op jit(solution)/shard_map/ppermute | solution.py:610
  29.6 1.8 %collective-permute-done.2.second_ref.rest_2_ = bf16[2,64,4096]{2,1,0:T(8,128)(2,1)} collective-permute-done((bf16[2,64,4096]{2,1,0:T(8,128)(2,1)}, bf16[2,64,4096]{2,1,0:T(8,128)(2,1)}, u32[]{:S(2)}, u32[]{:S(2)}) %collective-permute-start.2) | collective-permute-done | bytes 1048608 | tf_op jit(solution)/shard_map/ppermute | solution.py:610
  31.4 0.0 collective-permute-done.3.rest_1_
  31.4 0.5 collective-permute-done.4.rest_2_
  31.9 2.1 %half_relay.1 = (bf16[2,32,4096]{2,1,0:T(8,128)(2,1)}, bf16[2,32,4096]{2,1,0:T(8,128)(2,1)}) custom-call(bf16[2,64,4096]{2,1,0:T(8,128)(2,1)} %collective-permute-done.1.first_ref.rest_1_, bf16[2,64,4096]{2,1,0:T(8,128)(2,1)} %collective-permute-done.2.second_ref.rest_2_, bf16[256,512]{1,0:T(8,128)(2,1)} %get-tuple-element.25.rest_0_.rest_7_.rest_4_, ...), custom_call_target="tpu_custom_call" | custom-call | flops 1024 | bytes 1024 | tf_op jit(solution)/shard_map/half_relay/pallas_call | solution.py:508
  34.0 1.4 collective-permute-start.6
  35.5 1.5 collective-permute-start.7
  37.0 2.1 %stack.1.rest_11_.rest_0_ = bf16[2,4,64,1024]{3,2,1,0:T(8,128)(2,1)} custom-call(bf16[2,64,1024]{2,1,0:T(8,128)(2,1)} %get-tuple-element.24.rest_0_, bf16[2,64,1024]{2,1,0:T(8,128)(2,1)} %collective-permute-done.3.rest_1_, bf16[2,64,1024]{2,1,0:T(8,128)(2,1)} %collective-permute-done.4.rest_2_, bf16[2,64,1024]{2,1,0:T(8,128)(2,1)} %collective-permute-done.5.rest_3_, ...), custom_call_target="tpu_custom_call" | custom-call | flops 1024 | bytes 1024 | tf_op jit(solution)/shard_map/stack/pallas_call | solution.py:529
  39.1 0.6 collective-permute-start.9
  39.7 0.6 collective-permute-start.10
  40.3 6.1 %collective-permute-start.8 = (bf16[256,512]{1,0:T(8,128)(2,1)}, bf16[256,512]{1,0:T(8,128)(2,1)}, u32[]{:S(2)}, u32[]{:S(2)}) collective-permute-start(bf16[256,512]{1,0:T(8,128)(2,1)} %get-tuple-element.25.rest_0_.rest_7_.rest_4_), channel_id=1, source_target_pairs={{0,1},{1,2},{2,3},{3,0},{4,5},{5,6},{6,7},{7,4},{8,9},{9,10},{10,1... | collective-permute-start | bytes 786440 | tf_op jit(solution)/shard_map/ppermute | solution.py:615
  46.4 6.1 %collective-permute-done.8.rest_12_.rest_5_ = bf16[256,512]{1,0:T(8,128)(2,1)} collective-permute-done((bf16[256,512]{1,0:T(8,128)(2,1)}, bf16[256,512]{1,0:T(8,128)(2,1)}, u32[]{:S(2)}, u32[]{:S(2)}) %collective-permute-start.8) | collective-permute-done | bytes 262176 | tf_op jit(solution)/shard_map/ppermute | solution.py:615
  52.5 7.7 %backward_attention.1.g_ref.rest_4_ = bf16[256,1536]{1,0:T(8,128)(2,1)} custom-call(f32[1,4]{1,0:T(1,128)} %broadcast_multiply_fusion.factor_ref, bf16[2,64,4096]{2,1,0:T(8,128)(2,1)} %collective-permute-done.ins_ref.rest_0_, bf16[2,64,4096]{2,1,0:T(8,128)(2,1)} %collective-permute-done.1.first_ref.rest_1_, ...), custom_call_target="tpu_custom_call" | custom-call | flops 1024 | bytes 1024 | tf_op jit(solution)/shard_map/backward_attention/pallas_call | solution.py:265
  60.2 3.2 %collective-permute-start.11 = (bf16[256,1536]{1,0:T(8,128)(2,1)}, bf16[256,1536]{1,0:T(8,128)(2,1)}, u32[]{:S(2)}, u32[]{:S(2)}) collective-permute-start(bf16[256,1536]{1,0:T(8,128)(2,1)} %backward_attention.1.g_ref.rest_4_), channel_id=1, source_target_pairs={{0,2},{2,3},{3,1},{1,0},{4,6},{6,7},{7,5},{5,4},{8,10},{10,11},{11... | collective-permute-start | bytes 2359304 | tf_op jit(solution)/shard_map/ppermute | solution.py:623
  63.4 9.1 %input_grads.1 = (bf16[2,64,4096]{2,1,0:T(8,128)(2,1)}, bf16[2,64,4096]{2,1,0:T(8,128)(2,1)}) custom-call(bf16[256,1536]{1,0:T(8,128)(2,1)} %backward_attention.1.g_ref.rest_4_, bf16[4096,512]{1,0:T(8,128)(2,1)} %bitcast.32, bf16[4096,512]{1,0:T(8,128)(2,1)} %bitcast.34, bf16[4096,512]{1,0:T(8,128)(2,1)} %bitcast.36), custom_call_target="tpu_custom_call" | custom-call | flops 1024 | bytes 1024 | tf_op jit(solution)/shard_map/input_grads/pallas_call | solution.py:307
  72.5 0.0 collective-permute-done.10.rest_1_.rest_2_
  72.5 2.1 %passed.1.rest_10_ = bf16[2,64,4096]{2,1,0:T(8,128)(2,1)} custom-call(bf16[2,64,4096]{2,1,0:T(8,128)(2,1)} %get-tuple-element.32.value_ref, bf16[2,4,64,1024]{3,2,1,0:T(8,128)(2,1)} %collective-permute-done.9.rest_0_.rest_1_, bf16[2,4,64,1024]{3,2,1,0:T(8,128)(2,1)} %collective-permute-done.10.rest_1_.rest_2_), custom_call_target="tpu_custom_call" | custom-call | flops 1024 | bytes 1024 | tf_op jit(solution)/shard_map/passed/pallas_call | solution.py:576
  74.6 0.7 collective-permute-start.13
  75.3 4.7 %collective-permute-done.11.rest_11_.rest_5_ = bf16[256,1536]{1,0:T(8,128)(2,1)} collective-permute-done((bf16[256,1536]{1,0:T(8,128)(2,1)}, bf16[256,1536]{1,0:T(8,128)(2,1)}, u32[]{:S(2)}, u32[]{:S(2)}) %collective-permute-start.11) | collective-permute-done | bytes 786464 | tf_op jit(solution)/shard_map/ppermute | solution.py:623
  80.0 1.6 %collective-permute-start.16 = (bf16[256,1536]{1,0:T(8,128)(2,1)}, bf16[256,1536]{1,0:T(8,128)(2,1)}, u32[]{:S(2)}, u32[]{:S(2)}) collective-permute-start(bf16[256,1536]{1,0:T(8,128)(2,1)} %collective-permute-done.11.rest_11_.rest_5_), channel_id=1, source_target_pairs={{0,2},{2,3},{3,1},{1,0},{4,6},{6,7},{7,5},{5,4},{8,10},{10,11},{11... | collective-permute-start | bytes 2359304 | tf_op jit(solution)/shard_map/ppermute | solution.py:623
  81.6 1.5 collective-permute-start.15
  83.1 13.3 %forward_terms.1 = (bf16[2,64,4096]{2,1,0:T(8,128)(2,1)}, bf16[2,64,4096]{2,1,0:T(8,128)(2,1)}) custom-call(s32[2,2]{1,0:T(2,128)} %bitcast.56, s32[2]{0:T(128)} %bitcast.58, f32[1,4]{1,0:T(1,128)} %broadcast_multiply_fusion.factor_ref, bf16[2,64,4096]{2,1,0:T(8,128)(2,1)} %collective-permute-done.ins_ref.rest_0_, ...), custom_call_target="tpu_custom_call" | custom-call | flops 1024 | bytes 1024 | tf_op jit(solution)/shard_map/forward_terms/pallas_call | solution.py:363
  96.4 0.6 collective-permute-start.12
  97.1 0.6 collective-permute-done.16.rest_1_.rest_6_
  97.7 1.5 collective-permute-start.18
  99.2 1.2 collective-permute-done.13.came_ref
  100.4 2.1 %add.46 = bf16[64,4096]{1,0:T(8,128)(2,1)} custom-call(bf16[2,64,4096]{2,1,0:T(8,128)(2,1)} %get-tuple-element.35.near_ref, bf16[2,64,4096]{2,1,0:T(8,128)(2,1)} %collective-permute-done.13.came_ref, bf16[2,64,4096]{2,1,0:T(8,128)(2,1)} %get-tuple-element.33.rest_0_.near_ref), custom_call_target="tpu_custom_call" | custom-call | flops 1024 | bytes 1024 | tf_op jit(solution)/shard_map/add/pallas_call | solution.py:554
  102.5 2.2 %collective-permute-start.14 = (bf16[64,4096]{1,0:T(8,128)(2,1)}, bf16[64,4096]{1,0:T(8,128)(2,1)}, u32[]{:S(2)}, u32[]{:S(2)}) collective-permute-start(bf16[64,4096]{1,0:T(8,128)(2,1)} %add.46), channel_id=1, source_target_pairs={{0,8},{4,12},{8,0},{12,4},{1,9},{5,13},{9,1},{13,5},{2,10},{6,14},... | collective-permute-start | bytes 1572872 | tf_op jit(solution)/shard_map/ppermute | solution.py:604
  104.8 5.7 %collective-permute-start.17 = (bf16[256,512]{1,0:T(8,128)(2,1)}, bf16[256,512]{1,0:T(8,128)(2,1)}, u32[]{:S(2)}, u32[]{:S(2)}) collective-permute-start(bf16[256,512]{1,0:T(8,128)(2,1)} %get-tuple-element.25.rest_0_.rest_7_.rest_4_), channel_id=1, source_target_pairs={{0,3},{1,0},{2,1},{3,2},{4,7},{5,4},{6,5},{7,6},{8,11},{9,8},{10,9... | collective-permute-start | bytes 786440 | tf_op jit(solution)/shard_map/ppermute | solution.py:615
  110.5 9.3 %collective-permute-done.17.rest_2_.rest_7_ = bf16[256,512]{1,0:T(8,128)(2,1)} collective-permute-done((bf16[256,512]{1,0:T(8,128)(2,1)}, bf16[256,512]{1,0:T(8,128)(2,1)}, u32[]{:S(2)}, u32[]{:S(2)}) %collective-permute-start.17) | collective-permute-done | bytes 262176 | tf_op jit(solution)/shard_map/ppermute | solution.py:615
  119.8 0.0 collective-permute-done.15.rest_0_.rest_3_
  119.8 0.0 collective-permute-done.14.last_ref
  119.8 4.1 %back.1 = (bf16[64,4096]{1,0:T(8,128)(2,1)}, f32[1,4096]{1,0:T(1,128)}) custom-call(bf16[2,64,4096]{2,1,0:T(8,128)(2,1)} %get-tuple-element.35.near_ref, bf16[2,64,4096]{2,1,0:T(8,128)(2,1)} %collective-permute-done.13.came_ref, bf16[64,4096]{1,0:T(8,128)(2,1)} %collective-permute-done.14.last_ref, bf16[64,4096]{1,0:T(8,128)(2,1)} %bitcast.41, ...), custom_call_target="tpu_custom_call" | custom-call | flops 1024 | bytes 1024 | tf_op jit(solution)/shard_map/back/pallas_call | solution.py:392
  123.9 0.0 collective-permute-done.12.came_ref
  123.9 0.0 collective-permute-done.18.rest_1_.rest_7_
  123.9 2.1 %add.47.rest_0_ = bf16[64,4096]{1,0:T(8,128)(2,1)} custom-call(bf16[2,64,4096]{2,1,0:T(8,128)(2,1)} %get-tuple-element.33.rest_0_.near_ref, bf16[2,64,4096]{2,1,0:T(8,128)(2,1)} %collective-permute-done.12.came_ref, bf16[64,4096]{1,0:T(8,128)(2,1)} %get-tuple-element.36.rest_0_, bf16[256,1536]{1,0:T(8,128)(2,1)} %collective-permute-done.18.rest_1_.rest_7_), custom_call_target="tpu_custom_call" | custom-call | flops 1024 | bytes 1024 | tf_op jit(solution)/shard_map/add/pallas_call | solution.py:554
  126.1 1.6 %collective-permute-start.19 = (bf16[64,4096]{1,0:T(8,128)(2,1)}, bf16[64,4096]{1,0:T(8,128)(2,1)}, u32[]{:S(2)}, u32[]{:S(2)}) collective-permute-start(bf16[64,4096]{1,0:T(8,128)(2,1)} %add.47.rest_0_), channel_id=1, source_target_pairs={{0,8},{4,12},{8,0},{12,4},{1,9},{5,13},{9,1},{13,5},{2,10},{6,14},... | collective-permute-start | bytes 1572872 | tf_op jit(solution)/shard_map/ppermute | solution.py:604
  127.6 1.6 %collective-permute-start.20 = (f32[1,4096]{1,0:T(1,128)}, f32[1,4096]{1,0:T(1,128)}, u32[]{:S(2)}, u32[]{:S(2)}) collective-permute-start(f32[1,4096]{1,0:T(1,128)} %get-tuple-element.37.own_ref), channel_id=1, source_target_pairs={{0,4},{4,0},{8,12},{12,8},{1,5},{5,1},{9,13},{13,9},{2,6},{6,2},{1... | collective-permute-start | bytes 49160 | tf_op jit(solution)/shard_map/ppermute | solution.py:604
  129.3 2.4 %collective-permute-done.20.came_ref = f32[1,4096]{1,0:T(1,128)} collective-permute-done((f32[1,4096]{1,0:T(1,128)}, f32[1,4096]{1,0:T(1,128)}, u32[]{:S(2)}, u32[]{:S(2)}) %collective-permute-start.20) | collective-permute-done | bytes 16416 | tf_op jit(solution)/shard_map/ppermute | solution.py:604
  131.7 1.3 gain_added.2.rest_8_.own_ref
  133.0 0.5 collective-permute-start.22
  133.5 2.7 %collective-permute-start.21 = (bf16[256,512]{1,0:T(8,128)(2,1)}, bf16[256,512]{1,0:T(8,128)(2,1)}, u32[]{:S(2)}, u32[]{:S(2)}) collective-permute-start(bf16[256,512]{1,0:T(8,128)(2,1)} %get-tuple-element.25.rest_0_.rest_7_.rest_4_), channel_id=1, source_target_pairs={{0,2},{1,3},{2,0},{3,1},{4,6},{5,7},{6,4},{7,5},{8,10},{9,11},{10,... | collective-permute-start | bytes 786440 | tf_op jit(solution)/shard_map/ppermute | solution.py:615
  136.2 7.4 %weight_grads.1 = (bf16[1024,512]{1,0:T(8,128)(2,1)}, bf16[1024,512]{1,0:T(8,128)(2,1)}, bf16[1024,512]{1,0:T(8,128)(2,1)}) custom-call(bf16[2,4,64,1024]{3,2,1,0:T(8,128)(2,1)} %stack.1.rest_11_.rest_0_, bf16[2,4,64,1024]{3,2,1,0:T(8,128)(2,1)} %collective-permute-done.9.rest_0_.rest_1_, bf16[2,4,64,1024]{3,2,1,0:T(8,128)(2,1)} %collective-permute-done.10.rest_1_.rest_2_, ...), custom_call_target="tpu_custom_call" | custom-call | flops 1024 | bytes 1024 | tf_op jit(solution)/shard_map/weight_grads/pallas_call | solution.py:470
  143.6 1.3 gain_added.3.rest_8_
  145.0 2.5 %collective-permute-start.25 = (f32[1,4096]{1,0:T(1,128)}, f32[1,4096]{1,0:T(1,128)}, u32[]{:S(2)}, u32[]{:S(2)}) collective-permute-start(f32[1,4096]{1,0:T(1,128)} %gain_added.3.rest_8_), channel_id=1, source_target_pairs={{0,3},{1,0},{2,1},{3,2},{4,7},{5,4},{6,5},{7,6},{8,11},{9,8},{10,9... | collective-permute-start | bytes 49160 | tf_op jit(solution)/shard_map/ppermute | solution.py:615
  147.5 0.0 collective-permute-start.24
  147.5 0.6 collective-permute-start.23
  148.1 2.6 %fusion.1 = bf16[1,1,64,4096]{3,2,1,0:T(8,128)(2,1)} fusion(bf16[64,4096]{1,0:T(8,128)(2,1)} %collective-permute-done.19.rest_1_, bf16[2,64,4096]{2,1,0:T(8,128)(2,1)} %collective-permute-done.12.came_ref, bf16[2,64,4096]{2,1,0:T(8,128)(2,1)} %collective-permute-done.ins_ref.rest_0_, bf16[2,64,4096]{2,1,0:T(8,128)(2,1)} %get-tuple-element.33.rest_0_.near_ref), kind=kLoop, calls=%fused_computation.3 | loop fusion | flops 2097152 | bytes 2621440 | tf_op jit(solution)/shard_map/broadcast_in_dim | solution.py:708
  150.6 0.0 collective-permute-done.21.rest_6_
  150.6 4.3 %out_weight_grads.1 = bf16[512,1024]{1,0:T(8,128)(2,1)} custom-call(bf16[2,4,64,1024]{3,2,1,0:T(8,128)(2,1)} %stack.1.rest_11_.rest_0_, bf16[2,4,64,1024]{3,2,1,0:T(8,128)(2,1)} %collective-permute-done.9.rest_0_.rest_1_, bf16[2,4,64,1024]{3,2,1,0:T(8,128)(2,1)} %collective-permute-done.10.rest_1_.rest_2_, ...), custom_call_target="tpu_custom_call" | custom-call | flops 1024 | bytes 1024 | tf_op jit(solution)/shard_map/out_weight_grads/pallas_call | solution.py:470
  155.0 0.0 collective-permute-done.25
  155.0 0.0 collective-permute-done.23
  155.0 1.4 add_add_fusion
  (7 shorter events, 0.0 us)
Async XLA Ops:
  2.7 4.3 %collective-permute-start = (bf16[2,64,4096]{2,1,0:T(8,128)(2,1)}, bf16[2,64,4096]{2,1,0:T(8,128)(2,1)}, u32[]{:S(2)}, u32[]{:S(2)}) collective-permute-start(bf16[2,64,4096]{2,1,0:T(8,128)(2,1)} %pick.1), channel_id=1, source_target_pairs={{0,16},{4,20},{8,24},{12,28},{16,0},{20,4},{24,8},{28,12},{1,17},{... | collective-permute-start | bytes 3145736 | tf_op jit(solution)/shard_map/ppermute | solution.py:610
  3.3 26.3 %collective-permute-start.1 = (bf16[2,64,4096]{2,1,0:T(8,128)(2,1)}, bf16[2,64,4096]{2,1,0:T(8,128)(2,1)}, u32[]{:S(2)}, u32[]{:S(2)}) collective-permute-start(bf16[2,64,4096]{2,1,0:T(8,128)(2,1)} %pick.1), channel_id=1, source_target_pairs={{0,20},{4,16},{8,28},{12,24},{16,4},{20,0},{24,12},{28,8},{1,21},{... | collective-permute-start | bytes 3145736 | tf_op jit(solution)/shard_map/ppermute | solution.py:610
  5.9 25.5 %collective-permute-start.2 = (bf16[2,64,4096]{2,1,0:T(8,128)(2,1)}, bf16[2,64,4096]{2,1,0:T(8,128)(2,1)}, u32[]{:S(2)}, u32[]{:S(2)}) collective-permute-start(bf16[2,64,4096]{2,1,0:T(8,128)(2,1)} %pick.1), channel_id=1, source_target_pairs={{0,24},{4,28},{8,16},{12,20},{16,8},{20,12},{24,0},{28,4},{1,25},{... | collective-permute-start | bytes 3145736 | tf_op jit(solution)/shard_map/ppermute | solution.py:610
  9.7 21.7 %collective-permute-start.3 = (bf16[2,64,1024]{2,1,0:T(8,128)(2,1)}, bf16[2,64,1024]{2,1,0:T(8,128)(2,1)}, u32[]{:S(2)}, u32[]{:S(2)}) collective-permute-start(bf16[2,64,1024]{2,1,0:T(8,128)(2,1)} %get-tuple-element.26), channel_id=1, source_target_pairs={{0,1},{1,2},{2,3},{3,0},{4,5},{5,6},{6,7},{7,4},{8,9},{9,10},{10,1... | collective-permute-start | bytes 786440 | tf_op jit(solution)/shard_map/ppermute | solution.py:615
  11.5 20.4 %collective-permute-start.4 = (bf16[2,64,1024]{2,1,0:T(8,128)(2,1)}, bf16[2,64,1024]{2,1,0:T(8,128)(2,1)}, u32[]{:S(2)}, u32[]{:S(2)}) collective-permute-start(bf16[2,64,1024]{2,1,0:T(8,128)(2,1)} %get-tuple-element.27), channel_id=1, source_target_pairs={{0,2},{1,3},{2,0},{3,1},{4,6},{5,7},{6,4},{7,5},{8,10},{9,11},{10,... | collective-permute-start | bytes 786440 | tf_op jit(solution)/shard_map/ppermute | solution.py:615
  14.1 17.9 %collective-permute-start.5 = (bf16[2,64,1024]{2,1,0:T(8,128)(2,1)}, bf16[2,64,1024]{2,1,0:T(8,128)(2,1)}, u32[]{:S(2)}, u32[]{:S(2)}) collective-permute-start(bf16[2,64,1024]{2,1,0:T(8,128)(2,1)} %get-tuple-element.28), channel_id=1, source_target_pairs={{0,3},{1,0},{2,1},{3,2},{4,7},{5,4},{6,5},{7,6},{8,11},{9,8},{10,9... | collective-permute-start | bytes 786440 | tf_op jit(solution)/shard_map/ppermute | solution.py:615
  34.0 18.5 %collective-permute-start.6 = (bf16[2,32,4096]{2,1,0:T(8,128)(2,1)}, bf16[2,32,4096]{2,1,0:T(8,128)(2,1)}, u32[]{:S(2)}, u32[]{:S(2)}) collective-permute-start(bf16[2,32,4096]{2,1,0:T(8,128)(2,1)} %get-tuple-element.29.rest_4_), channel_id=1, source_target_pairs={{0,4},{4,0},{8,12},{12,8},{1,5},{5,1},{9,13},{13,9},{2,6},{6,2},{1... | collective-permute-start | bytes 1572872 | tf_op jit(solution)/shard_map/ppermute | solution.py:604
  35.5 17.1 %collective-permute-start.7 = (bf16[2,32,4096]{2,1,0:T(8,128)(2,1)}, bf16[2,32,4096]{2,1,0:T(8,128)(2,1)}, u32[]{:S(2)}, u32[]{:S(2)}) collective-permute-start(bf16[2,32,4096]{2,1,0:T(8,128)(2,1)} %get-tuple-element.30), channel_id=1, source_target_pairs={{0,8},{4,12},{8,0},{12,4},{1,9},{5,13},{9,1},{13,5},{2,10},{6,14},... | collective-permute-start | bytes 1572872 | tf_op jit(solution)/shard_map/ppermute | solution.py:604
  39.1 33.4 %collective-permute-start.9 = (bf16[2,4,64,1024]{3,2,1,0:T(8,128)(2,1)}, bf16[2,4,64,1024]{3,2,1,0:T(8,128)(2,1)}, u32[]{:S(2)}, u32[]{:S(2)}) collective-permute-start(bf16[2,4,64,1024]{3,2,1,0:T(8,128)(2,1)} %stack.1.rest_11_.rest_0_), channel_id=1, source_target_pairs={{0,4},{4,0},{8,12},{12,8},{1,5},{5,1},{9,13},{13,9},{2,6},{6,2},{1... | collective-permute-start | bytes 3145736 | tf_op jit(solution)/shard_map/ppermute | solution.py:604
  39.7 32.8 %collective-permute-start.10 = (bf16[2,4,64,1024]{3,2,1,0:T(8,128)(2,1)}, bf16[2,4,64,1024]{3,2,1,0:T(8,128)(2,1)}, u32[]{:S(2)}, u32[]{:S(2)}) collective-permute-start(bf16[2,4,64,1024]{3,2,1,0:T(8,128)(2,1)} %stack.1.rest_11_.rest_0_), channel_id=1, source_target_pairs={{0,8},{4,12},{8,0},{12,4},{1,9},{5,13},{9,1},{13,5},{2,10},{6,14},... | collective-permute-start | bytes 3145736 | tf_op jit(solution)/shard_map/ppermute | solution.py:604
  40.3 12.2 %collective-permute-start.8 = (bf16[256,512]{1,0:T(8,128)(2,1)}, bf16[256,512]{1,0:T(8,128)(2,1)}, u32[]{:S(2)}, u32[]{:S(2)}) collective-permute-start(bf16[256,512]{1,0:T(8,128)(2,1)} %get-tuple-element.25.rest_0_.rest_7_.rest_4_), channel_id=1, source_target_pairs={{0,1},{1,2},{2,3},{3,0},{4,5},{5,6},{6,7},{7,4},{8,9},{9,10},{10,1... | collective-permute-start | bytes 786440 | tf_op jit(solution)/shard_map/ppermute | solution.py:615
  60.2 19.8 %collective-permute-start.11 = (bf16[256,1536]{1,0:T(8,128)(2,1)}, bf16[256,1536]{1,0:T(8,128)(2,1)}, u32[]{:S(2)}, u32[]{:S(2)}) collective-permute-start(bf16[256,1536]{1,0:T(8,128)(2,1)} %backward_attention.1.g_ref.rest_4_), channel_id=1, source_target_pairs={{0,2},{2,3},{3,1},{1,0},{4,6},{6,7},{7,5},{5,4},{8,10},{10,11},{11... | collective-permute-start | bytes 2359304 | tf_op jit(solution)/shard_map/ppermute | solution.py:623
  74.6 25.8 %collective-permute-start.13 = (bf16[2,64,4096]{2,1,0:T(8,128)(2,1)}, bf16[2,64,4096]{2,1,0:T(8,128)(2,1)}, u32[]{:S(2)}, u32[]{:S(2)}) collective-permute-start(bf16[2,64,4096]{2,1,0:T(8,128)(2,1)} %passed.1.rest_10_), channel_id=1, source_target_pairs={{0,4},{4,0},{8,12},{12,8},{1,5},{5,1},{9,13},{13,9},{2,6},{6,2},{1... | collective-permute-start | bytes 3145736 | tf_op jit(solution)/shard_map/ppermute | solution.py:604
  80.0 17.7 %collective-permute-start.16 = (bf16[256,1536]{1,0:T(8,128)(2,1)}, bf16[256,1536]{1,0:T(8,128)(2,1)}, u32[]{:S(2)}, u32[]{:S(2)}) collective-permute-start(bf16[256,1536]{1,0:T(8,128)(2,1)} %collective-permute-done.11.rest_11_.rest_5_), channel_id=1, source_target_pairs={{0,2},{2,3},{3,1},{1,0},{4,6},{6,7},{7,5},{5,4},{8,10},{10,11},{11... | collective-permute-start | bytes 2359304 | tf_op jit(solution)/shard_map/ppermute | solution.py:623
  81.6 38.2 %collective-permute-start.15 = (bf16[2,4,64,1024]{3,2,1,0:T(8,128)(2,1)}, bf16[2,4,64,1024]{3,2,1,0:T(8,128)(2,1)}, u32[]{:S(2)}, u32[]{:S(2)}) collective-permute-start(bf16[2,4,64,1024]{3,2,1,0:T(8,128)(2,1)} %collective-permute-done.9.rest_0_.rest_1_), channel_id=1, source_target_pairs={{0,8},{4,12},{8,0},{12,4},{1,9},{5,13},{9,1},{13,5},{2,10},{6,14},... | collective-permute-start | bytes 3145736 | tf_op jit(solution)/shard_map/ppermute | solution.py:604
  96.4 27.5 %collective-permute-start.12 = (bf16[2,64,4096]{2,1,0:T(8,128)(2,1)}, bf16[2,64,4096]{2,1,0:T(8,128)(2,1)}, u32[]{:S(2)}, u32[]{:S(2)}) collective-permute-start(bf16[2,64,4096]{2,1,0:T(8,128)(2,1)} %get-tuple-element.34), channel_id=1, source_target_pairs={{0,4},{4,0},{8,12},{12,8},{1,5},{5,1},{9,13},{13,9},{2,6},{6,2},{1... | collective-permute-start | bytes 3145736 | tf_op jit(solution)/shard_map/ppermute | solution.py:604
  97.7 26.2 %collective-permute-start.18 = (bf16[256,1536]{1,0:T(8,128)(2,1)}, bf16[256,1536]{1,0:T(8,128)(2,1)}, u32[]{:S(2)}, u32[]{:S(2)}) collective-permute-start(bf16[256,1536]{1,0:T(8,128)(2,1)} %collective-permute-done.16.rest_1_.rest_6_), channel_id=1, source_target_pairs={{0,2},{2,3},{3,1},{1,0},{4,6},{6,7},{7,5},{5,4},{8,10},{10,11},{11... | collective-permute-start | bytes 2359304 | tf_op jit(solution)/shard_map/ppermute | solution.py:623
  102.5 17.3 %collective-permute-start.14 = (bf16[64,4096]{1,0:T(8,128)(2,1)}, bf16[64,4096]{1,0:T(8,128)(2,1)}, u32[]{:S(2)}, u32[]{:S(2)}) collective-permute-start(bf16[64,4096]{1,0:T(8,128)(2,1)} %add.46), channel_id=1, source_target_pairs={{0,8},{4,12},{8,0},{12,4},{1,9},{5,13},{9,1},{13,5},{2,10},{6,14},... | collective-permute-start | bytes 1572872 | tf_op jit(solution)/shard_map/ppermute | solution.py:604
  104.8 15.0 %collective-permute-start.17 = (bf16[256,512]{1,0:T(8,128)(2,1)}, bf16[256,512]{1,0:T(8,128)(2,1)}, u32[]{:S(2)}, u32[]{:S(2)}) collective-permute-start(bf16[256,512]{1,0:T(8,128)(2,1)} %get-tuple-element.25.rest_0_.rest_7_.rest_4_), channel_id=1, source_target_pairs={{0,3},{1,0},{2,1},{3,2},{4,7},{5,4},{6,5},{7,6},{8,11},{9,8},{10,9... | collective-permute-start | bytes 786440 | tf_op jit(solution)/shard_map/ppermute | solution.py:615
  126.1 17.6 %collective-permute-start.19 = (bf16[64,4096]{1,0:T(8,128)(2,1)}, bf16[64,4096]{1,0:T(8,128)(2,1)}, u32[]{:S(2)}, u32[]{:S(2)}) collective-permute-start(bf16[64,4096]{1,0:T(8,128)(2,1)} %add.47.rest_0_), channel_id=1, source_target_pairs={{0,8},{4,12},{8,0},{12,4},{1,9},{5,13},{9,1},{13,5},{2,10},{6,14},... | collective-permute-start | bytes 1572872 | tf_op jit(solution)/shard_map/ppermute | solution.py:604
  127.6 4.1 %collective-permute-start.20 = (f32[1,4096]{1,0:T(1,128)}, f32[1,4096]{1,0:T(1,128)}, u32[]{:S(2)}, u32[]{:S(2)}) collective-permute-start(f32[1,4096]{1,0:T(1,128)} %get-tuple-element.37.own_ref), channel_id=1, source_target_pairs={{0,4},{4,0},{8,12},{12,8},{1,5},{5,1},{9,13},{13,9},{2,6},{6,2},{1... | collective-permute-start | bytes 49160 | tf_op jit(solution)/shard_map/ppermute | solution.py:604
  133.0 10.6 %collective-permute-start.22 = (f32[1,4096]{1,0:T(1,128)}, f32[1,4096]{1,0:T(1,128)}, u32[]{:S(2)}, u32[]{:S(2)}) collective-permute-start(f32[1,4096]{1,0:T(1,128)} %gain_added.2.rest_8_.own_ref), channel_id=1, source_target_pairs={{0,8},{4,12},{8,0},{12,4},{1,9},{5,13},{9,1},{13,5},{2,10},{6,14},... | collective-permute-start | bytes 49160 | tf_op jit(solution)/shard_map/ppermute | solution.py:604
  133.5 17.1 %collective-permute-start.21 = (bf16[256,512]{1,0:T(8,128)(2,1)}, bf16[256,512]{1,0:T(8,128)(2,1)}, u32[]{:S(2)}, u32[]{:S(2)}) collective-permute-start(bf16[256,512]{1,0:T(8,128)(2,1)} %get-tuple-element.25.rest_0_.rest_7_.rest_4_), channel_id=1, source_target_pairs={{0,2},{1,3},{2,0},{3,1},{4,6},{5,7},{6,4},{7,5},{8,10},{9,11},{10,... | collective-permute-start | bytes 786440 | tf_op jit(solution)/shard_map/ppermute | solution.py:615
  145.0 10.0 %collective-permute-start.25 = (f32[1,4096]{1,0:T(1,128)}, f32[1,4096]{1,0:T(1,128)}, u32[]{:S(2)}, u32[]{:S(2)}) collective-permute-start(f32[1,4096]{1,0:T(1,128)} %gain_added.3.rest_8_), channel_id=1, source_target_pairs={{0,3},{1,0},{2,1},{3,2},{4,7},{5,4},{6,5},{7,6},{8,11},{9,8},{10,9... | collective-permute-start | bytes 49160 | tf_op jit(solution)/shard_map/ppermute | solution.py:615
  147.5 7.5 %collective-permute-start.24 = (f32[1,4096]{1,0:T(1,128)}, f32[1,4096]{1,0:T(1,128)}, u32[]{:S(2)}, u32[]{:S(2)}) collective-permute-start(f32[1,4096]{1,0:T(1,128)} %gain_added.3.rest_8_), channel_id=1, source_target_pairs={{0,2},{1,3},{2,0},{3,1},{4,6},{5,7},{6,4},{7,5},{8,10},{9,11},{10,... | collective-permute-start | bytes 49160 | tf_op jit(solution)/shard_map/ppermute | solution.py:615
  147.5 7.5 %collective-permute-start.23 = (f32[1,4096]{1,0:T(1,128)}, f32[1,4096]{1,0:T(1,128)}, u32[]{:S(2)}, u32[]{:S(2)}) collective-permute-start(f32[1,4096]{1,0:T(1,128)} %gain_added.3.rest_8_), channel_id=1, source_target_pairs={{0,1},{1,2},{2,3},{3,0},{4,5},{5,6},{6,7},{7,4},{8,9},{9,10},{10,1... | collective-permute-start | bytes 49160 | tf_op jit(solution)/shard_map/ppermute | solution.py:615

commit v6 on v5

--- a/solution.py
+++ b/solution.py
@@ -691,8 +691,8 @@
     mix_came = swapped(mix_far, "seq", 1)
     dx_sum = added(dx_near, dx_came, after=[mix_near])
     dx_last = swapped(dx_sum, "seq", 2)
-    back_out, gain_part = back(dx_near, dx_came, dx_last, x, ins[0], norm_gain, after=[cols[3], *ring[2:3], *atts[3:]])
-    mix_sum = added(mix_near, mix_came, after=[back_out, *ring[3:4]])
+    back_out, gain_part = back(dx_near, dx_came, dx_last, x, ins[0], norm_gain, after=[cols[3], *ring[2:3]])
+    mix_sum = added(mix_near, mix_came, after=[back_out, *ring[3:4], *atts[3:]])
     mix_last = swapped(mix_sum, "seq", 2)
 
     gain_part = gain_added(gain_part, swapped(gain_part, "seq", 1), after=[mix_sum])

time: 157 us -> 157 us (level)
  starting transfers between devices: 46.9 us -> 49.7 us
  waiting for transfers between devices: 36.6 us -> 33.8 us
    ppermute x9, waiting for transfers between devices: 16 us -> 7.75 us  [rotated(): return lax.ppermute(value, axis, [(i, (i + k) % n) for i in range(n)])]
    ppermute x11, waiting for transfers between devices: 3.63 us -> 9.08 us  [swapped(): lax.ppermute(value, axis, [(i, i ^ j) for i in range(lax.axis_size(axis))])]
    ppermute x9, starting transfers between devices: 23.3 us -> 26.7 us  [rotated(): return lax.ppermute(value, axis, [(i, (i + k) % n) for i in range(n)])]
  transfers between devices with their start and end apart: 26 -> 26, of which waited for: 9 -> 11; matrix products, arithmetic and copies ran while one was open for 2% -> 2% of each run, Pallas kernels for 39% -> 39%
where the time goes in v6:
time: 157 us; the launch traced here: 156 us
  Pallas kernels  67 us (43%)
  starting transfers between devices  49.7 us (32%)
  waiting for transfers between devices  33.8 us (22%)
  other arithmetic  5.14 us (3%)
    ppermute x9, starting transfers between devices, rotated(): return lax.ppermute(value, axis, [(i, (i + k) % n) for i in range(n)])  26.7 us
    pallas_call x1, Pallas kernels, forward_terms(): pl.pallas_call(functools.partial(forward_kernel, n), out_shape=(sds((2, r...  13.3 us
    ppermute x11, starting transfers between devices, swapped(): lax.ppermute(value, axis, [(i, i ^ j) for i in range(lax.axis_size(axis))])  12.3 us
    pallas_call x2, Pallas kernels, contracted(): pl.pallas_call(functools.partial(kernel, len(parts), samples), out_shape=...  11.7 us
    ppermute x3, waiting for transfers between devices, crossed(): return lax.ppermute(value, ('pipe', 'seq'), pairs)  11.6 us
    ppermute x11, waiting for transfers between devices, swapped(): lax.ppermute(value, axis, [(i, i ^ j) for i in range(lax.axis_size(axis))])  9.08 us
    pallas_call x1, Pallas kernels, input_grads(): pl.pallas_call(input_grad_kernel, out_shape=(sds((2, tokens // 4, model),...  9.08 us
    ppermute x9, waiting for transfers between devices, rotated(): return lax.ppermute(value, axis, [(i, (i + k) % n) for i in range(n)])  7.75 us
  transfers between devices with their start and end apart: 26, of which 11 were waited for; matrix products, arithmetic and copies ran while one was open for 2% of the time, Pallas kernels for 39%

profile of v6, /device:TPU:0, one launch (start us, length us, event | category | flops | bytes accessed | tf_op | source)
XLA Modules:
  0.0 156.4 jit_solution(4117870339793487303)
XLA Ops:
  0.6 2.1 %pick.1 = bf16[2,64,4096]{2,1,0:T(8,128)(2,1)} custom-call(bf16[64,4096]{1,0:T(8,128)(2,1)} %bitcast.50, bf16[64,4096]{1,0:T(8,128)(2,1)} %bitcast.51, bf16[64,4096]{1,0:T(8,128)(2,1)} %bitcast.52, bf16[64,4096]{1,0:T(8,128)(2,1)} %bitcast.53), custom_call_target="tpu_custom_call" | custom-call | flops 1024 | bytes 1024 | tf_op jit(solution)/shard_map/pick/pallas_call | solution.py:123
  2.7 0.5 collective-permute-start
  3.3 2.6 %collective-permute-start.1 = (bf16[2,64,4096]{2,1,0:T(8,128)(2,1)}, bf16[2,64,4096]{2,1,0:T(8,128)(2,1)}, u32[]{:S(2)}, u32[]{:S(2)}) collective-permute-start(bf16[2,64,4096]{2,1,0:T(8,128)(2,1)} %pick.1), channel_id=1, source_target_pairs={{0,20},{4,16},{8,28},{12,24},{16,4},{20,0},{24,12},{28,8},{1,21},{... | collective-permute-start | bytes 3145736 | tf_op jit(solution)/shard_map/ppermute | solution.py:610
  5.9 1.2 collective-permute-start.2
  7.1 0.0 collective-permute-done.ins_ref.rest_0_
  7.1 2.7 %columns.1 = (bf16[2,64,1024]{2,1,0:T(8,128)(2,1)}, bf16[2,64,1024]{2,1,0:T(8,128)(2,1)}, bf16[2,64,1024]{2,1,0:T(8,128)(2,1)}, bf16[2,64,1024]{2,1,0:T(8,128)(2,1)}) custom-call(bf16[64,4096]{1,0:T(8,128)(2,1)} %bitcast.40, bf16[2,64,4096]{2,1,0:T(8,128)(2,1)} %collective-permute-done.ins_ref.rest_0_, f32[1,4096]{1,0:T(1,128)} %gain_ref.3), custom_call_target="tpu_custom_call" | custom-call | flops 1024 | bytes 1024 | tf_op jit(solution)/shard_map/columns/pallas_call | solution.py:150
  9.7 1.8 %collective-permute-start.3 = (bf16[2,64,1024]{2,1,0:T(8,128)(2,1)}, bf16[2,64,1024]{2,1,0:T(8,128)(2,1)}, u32[]{:S(2)}, u32[]{:S(2)}) collective-permute-start(bf16[2,64,1024]{2,1,0:T(8,128)(2,1)} %get-tuple-element.26), channel_id=1, source_target_pairs={{0,1},{1,2},{2,3},{3,0},{4,5},{5,6},{6,7},{7,4},{8,9},{9,10},{10,1... | collective-permute-start | bytes 786440 | tf_op jit(solution)/shard_map/ppermute | solution.py:615
  11.5 2.6 %collective-permute-start.4 = (bf16[2,64,1024]{2,1,0:T(8,128)(2,1)}, bf16[2,64,1024]{2,1,0:T(8,128)(2,1)}, u32[]{:S(2)}, u32[]{:S(2)}) collective-permute-start(bf16[2,64,1024]{2,1,0:T(8,128)(2,1)} %get-tuple-element.27), channel_id=1, source_target_pairs={{0,2},{1,3},{2,0},{3,1},{4,6},{5,7},{6,4},{7,5},{8,10},{9,11},{10,... | collective-permute-start | bytes 786440 | tf_op jit(solution)/shard_map/ppermute | solution.py:615
  14.1 1.3 collective-permute-start.5
  15.4 1.2 broadcast_multiply_fusion.factor_ref
  16.6 3.2 %saved_attention.1 = (f32[4,256,256]{2,1,0:T(8,128)}, bf16[256,512]{1,0:T(8,128)(2,1)}) custom-call(s32[2,2]{1,0:T(2,128)} %bitcast.55, s32[2]{0:T(128)} %bitcast.57, f32[1,4]{1,0:T(1,128)} %broadcast_multiply_fusion.factor_ref, bf16[256,512]{1,0:T(8,128)(2,1)} %bitcast.43, bf16[256,512]{1,0:T(8,128)(2,1)} %bitcast.45, bf16[256,512]{1,0:T(8,128)(2,1)} %bitcast.47, ...), custom_call_target="tpu_custom_call" | custom-call | flops 1024 | bytes 1024 | tf_op jit(solution)/shard_map/saved_attention/pallas_call | solution.py:174
  19.8 9.8 %collective-permute-done.1.first_ref.rest_1_ = bf16[2,64,4096]{2,1,0:T(8,128)(2,1)} collective-permute-done((bf16[2,64,4096]{2,1,0:T(8,128)(2,1)}, bf16[2,64,4096]{2,1,0:T(8,128)(2,1)}, u32[]{:S(2)}, u32[]{:S(2)}) %collective-permute-start.1) | collective-permute-done | bytes 1048608 | tf_op jit(solution)/shard_map/ppermute | solution.py:610
  29.6 1.8 %collective-permute-done.2.second_ref.rest_2_ = bf16[2,64,4096]{2,1,0:T(8,128)(2,1)} collective-permute-done((bf16[2,64,4096]{2,1,0:T(8,128)(2,1)}, bf16[2,64,4096]{2,1,0:T(8,128)(2,1)}, u32[]{:S(2)}, u32[]{:S(2)}) %collective-permute-start.2) | collective-permute-done | bytes 1048608 | tf_op jit(solution)/shard_map/ppermute | solution.py:610
  31.4 0.0 collective-permute-done.3.rest_1_
  31.4 0.5 collective-permute-done.4.rest_2_
  31.9 0.0 collective-permute-done.5.rest_3_
  31.9 2.1 %half_relay.1 = (bf16[2,32,4096]{2,1,0:T(8,128)(2,1)}, bf16[2,32,4096]{2,1,0:T(8,128)(2,1)}) custom-call(bf16[2,64,4096]{2,1,0:T(8,128)(2,1)} %collective-permute-done.1.first_ref.rest_1_, bf16[2,64,4096]{2,1,0:T(8,128)(2,1)} %collective-permute-done.2.second_ref.rest_2_, bf16[256,512]{1,0:T(8,128)(2,1)} %get-tuple-element.25.rest_0_.rest_7_.rest_4_, ...), custom_call_target="tpu_custom_call" | custom-call | flops 1024 | bytes 1024 | tf_op jit(solution)/shard_map/half_relay/pallas_call | solution.py:508
  34.0 1.4 collective-permute-start.6
  35.5 1.5 collective-permute-start.7
  37.0 2.1 %stack.1.rest_11_.rest_0_ = bf16[2,4,64,1024]{3,2,1,0:T(8,128)(2,1)} custom-call(bf16[2,64,1024]{2,1,0:T(8,128)(2,1)} %get-tuple-element.24.rest_0_, bf16[2,64,1024]{2,1,0:T(8,128)(2,1)} %collective-permute-done.3.rest_1_, bf16[2,64,1024]{2,1,0:T(8,128)(2,1)} %collective-permute-done.4.rest_2_, bf16[2,64,1024]{2,1,0:T(8,128)(2,1)} %collective-permute-done.5.rest_3_, ...), custom_call_target="tpu_custom_call" | custom-call | flops 1024 | bytes 1024 | tf_op jit(solution)/shard_map/stack/pallas_call | solution.py:529
  39.1 0.6 collective-permute-start.9
  39.7 0.6 collective-permute-start.10
  40.3 6.1 %collective-permute-start.8 = (bf16[256,512]{1,0:T(8,128)(2,1)}, bf16[256,512]{1,0:T(8,128)(2,1)}, u32[]{:S(2)}, u32[]{:S(2)}) collective-permute-start(bf16[256,512]{1,0:T(8,128)(2,1)} %get-tuple-element.25.rest_0_.rest_7_.rest_4_), channel_id=1, source_target_pairs={{0,1},{1,2},{2,3},{3,0},{4,5},{5,6},{6,7},{7,4},{8,9},{9,10},{10,1... | collective-permute-start | bytes 786440 | tf_op jit(solution)/shard_map/ppermute | solution.py:615
  46.4 6.1 %collective-permute-done.8.rest_12_.rest_5_ = bf16[256,512]{1,0:T(8,128)(2,1)} collective-permute-done((bf16[256,512]{1,0:T(8,128)(2,1)}, bf16[256,512]{1,0:T(8,128)(2,1)}, u32[]{:S(2)}, u32[]{:S(2)}) %collective-permute-start.8) | collective-permute-done | bytes 262176 | tf_op jit(solution)/shard_map/ppermute | solution.py:615
  52.5 0.0 collective-permute-done.6.rest_3_
  52.5 0.0 collective-permute-done.7.rest_4_
  52.5 7.7 %backward_attention.1.g_ref.rest_4_ = bf16[256,1536]{1,0:T(8,128)(2,1)} custom-call(f32[1,4]{1,0:T(1,128)} %broadcast_multiply_fusion.factor_ref, bf16[2,64,4096]{2,1,0:T(8,128)(2,1)} %collective-permute-done.ins_ref.rest_0_, bf16[2,64,4096]{2,1,0:T(8,128)(2,1)} %collective-permute-done.1.first_ref.rest_1_, ...), custom_call_target="tpu_custom_call" | custom-call | flops 1024 | bytes 1024 | tf_op jit(solution)/shard_map/backward_attention/pallas_call | solution.py:265
  60.2 3.2 %collective-permute-start.11 = (bf16[256,1536]{1,0:T(8,128)(2,1)}, bf16[256,1536]{1,0:T(8,128)(2,1)}, u32[]{:S(2)}, u32[]{:S(2)}) collective-permute-start(bf16[256,1536]{1,0:T(8,128)(2,1)} %backward_attention.1.g_ref.rest_4_), channel_id=1, source_target_pairs={{0,2},{2,3},{3,1},{1,0},{4,6},{6,7},{7,5},{5,4},{8,10},{10,11},{11... | collective-permute-start | bytes 2359304 | tf_op jit(solution)/shard_map/ppermute | solution.py:623
  63.4 9.1 %input_grads.1 = (bf16[2,64,4096]{2,1,0:T(8,128)(2,1)}, bf16[2,64,4096]{2,1,0:T(8,128)(2,1)}) custom-call(bf16[256,1536]{1,0:T(8,128)(2,1)} %backward_attention.1.g_ref.rest_4_, bf16[4096,512]{1,0:T(8,128)(2,1)} %bitcast.32, bf16[4096,512]{1,0:T(8,128)(2,1)} %bitcast.34, bf16[4096,512]{1,0:T(8,128)(2,1)} %bitcast.36), custom_call_target="tpu_custom_call" | custom-call | flops 1024 | bytes 1024 | tf_op jit(solution)/shard_map/input_grads/pallas_call | solution.py:307
  72.5 0.0 collective-permute-done.9.rest_0_.rest_1_
  72.5 2.1 %passed.1.rest_10_ = bf16[2,64,4096]{2,1,0:T(8,128)(2,1)} custom-call(bf16[2,64,4096]{2,1,0:T(8,128)(2,1)} %get-tuple-element.32.value_ref, bf16[2,4,64,1024]{3,2,1,0:T(8,128)(2,1)} %collective-permute-done.9.rest_0_.rest_1_, bf16[2,4,64,1024]{3,2,1,0:T(8,128)(2,1)} %collective-permute-done.10.rest_1_.rest_2_), custom_call_target="tpu_custom_call" | custom-call | flops 1024 | bytes 1024 | tf_op jit(solution)/shard_map/passed/pallas_call | solution.py:576
  74.6 0.7 collective-permute-start.13
  75.3 4.7 %collective-permute-done.11.rest_11_.rest_5_ = bf16[256,1536]{1,0:T(8,128)(2,1)} collective-permute-done((bf16[256,1536]{1,0:T(8,128)(2,1)}, bf16[256,1536]{1,0:T(8,128)(2,1)}, u32[]{:S(2)}, u32[]{:S(2)}) %collective-permute-start.11) | collective-permute-done | bytes 786464 | tf_op jit(solution)/shard_map/ppermute | solution.py:623
  80.0 1.6 %collective-permute-start.16 = (bf16[256,1536]{1,0:T(8,128)(2,1)}, bf16[256,1536]{1,0:T(8,128)(2,1)}, u32[]{:S(2)}, u32[]{:S(2)}) collective-permute-start(bf16[256,1536]{1,0:T(8,128)(2,1)} %collective-permute-done.11.rest_11_.rest_5_), channel_id=1, source_target_pairs={{0,2},{2,3},{3,1},{1,0},{4,6},{6,7},{7,5},{5,4},{8,10},{10,11},{11... | collective-permute-start | bytes 2359304 | tf_op jit(solution)/shard_map/ppermute | solution.py:623
  81.6 1.5 collective-permute-start.15
  83.1 13.3 %forward_terms.1 = (bf16[2,64,4096]{2,1,0:T(8,128)(2,1)}, bf16[2,64,4096]{2,1,0:T(8,128)(2,1)}) custom-call(s32[2,2]{1,0:T(2,128)} %bitcast.56, s32[2]{0:T(128)} %bitcast.58, f32[1,4]{1,0:T(1,128)} %broadcast_multiply_fusion.factor_ref, bf16[2,64,4096]{2,1,0:T(8,128)(2,1)} %collective-permute-done.ins_ref.rest_0_, ...), custom_call_target="tpu_custom_call" | custom-call | flops 1024 | bytes 1024 | tf_op jit(solution)/shard_map/forward_terms/pallas_call | solution.py:363
  96.4 0.6 collective-permute-start.12
  97.1 0.6 collective-permute-done.16.rest_1_.rest_6_
  97.7 1.5 collective-permute-start.17
  99.2 1.2 collective-permute-done.13.came_ref
  100.4 2.1 %add.46 = bf16[64,4096]{1,0:T(8,128)(2,1)} custom-call(bf16[2,64,4096]{2,1,0:T(8,128)(2,1)} %get-tuple-element.35.near_ref, bf16[2,64,4096]{2,1,0:T(8,128)(2,1)} %collective-permute-done.13.came_ref, bf16[2,64,4096]{2,1,0:T(8,128)(2,1)} %get-tuple-element.33.rest_0_.near_ref), custom_call_target="tpu_custom_call" | custom-call | flops 1024 | bytes 1024 | tf_op jit(solution)/shard_map/add/pallas_call | solution.py:554
  102.5 2.2 %collective-permute-start.14 = (bf16[64,4096]{1,0:T(8,128)(2,1)}, bf16[64,4096]{1,0:T(8,128)(2,1)}, u32[]{:S(2)}, u32[]{:S(2)}) collective-permute-start(bf16[64,4096]{1,0:T(8,128)(2,1)} %add.46), channel_id=1, source_target_pairs={{0,8},{4,12},{8,0},{12,4},{1,9},{5,13},{9,1},{13,5},{2,10},{6,14},... | collective-permute-start | bytes 1572872 | tf_op jit(solution)/shard_map/ppermute | solution.py:604
  104.8 5.7 %collective-permute-start.18 = (bf16[256,512]{1,0:T(8,128)(2,1)}, bf16[256,512]{1,0:T(8,128)(2,1)}, u32[]{:S(2)}, u32[]{:S(2)}) collective-permute-start(bf16[256,512]{1,0:T(8,128)(2,1)} %get-tuple-element.25.rest_0_.rest_7_.rest_4_), channel_id=1, source_target_pairs={{0,3},{1,0},{2,1},{3,2},{4,7},{5,4},{6,5},{7,6},{8,11},{9,8},{10,9... | collective-permute-start | bytes 786440 | tf_op jit(solution)/shard_map/ppermute | solution.py:615
  110.5 0.0 collective-permute-done.15.rest_0_.rest_3_
  110.5 4.1 %collective-permute-done.14.last_ref = bf16[64,4096]{1,0:T(8,128)(2,1)} collective-permute-done((bf16[64,4096]{1,0:T(8,128)(2,1)}, bf16[64,4096]{1,0:T(8,128)(2,1)}, u32[]{:S(2)}, u32[]{:S(2)}) %collective-permute-start.14) | collective-permute-done | bytes 524320 | tf_op jit(solution)/shard_map/ppermute | solution.py:604
  114.6 4.1 %back.1 = (bf16[64,4096]{1,0:T(8,128)(2,1)}, f32[1,4096]{1,0:T(1,128)}) custom-call(bf16[2,64,4096]{2,1,0:T(8,128)(2,1)} %get-tuple-element.35.near_ref, bf16[2,64,4096]{2,1,0:T(8,128)(2,1)} %collective-permute-done.13.came_ref, bf16[64,4096]{1,0:T(8,128)(2,1)} %collective-permute-done.14.last_ref, bf16[64,4096]{1,0:T(8,128)(2,1)} %bitcast.41, ...), custom_call_target="tpu_custom_call" | custom-call | flops 1024 | bytes 1024 | tf_op jit(solution)/shard_map/back/pallas_call | solution.py:392
  118.7 1.1 collective-permute-done.18.rest_2_.rest_7_
  119.8 0.7 collective-permute-done.12.came_ref
  120.5 0.0 collective-permute-done.17.rest_1_.rest_7_
  120.5 2.1 %add.47.rest_0_ = bf16[64,4096]{1,0:T(8,128)(2,1)} custom-call(bf16[2,64,4096]{2,1,0:T(8,128)(2,1)} %get-tuple-element.33.rest_0_.near_ref, bf16[2,64,4096]{2,1,0:T(8,128)(2,1)} %collective-permute-done.12.came_ref, bf16[64,4096]{1,0:T(8,128)(2,1)} %get-tuple-element.36.rest_0_, bf16[256,1536]{1,0:T(8,128)(2,1)} %collective-permute-done.17.rest_1_.rest_7_, ...), custom_call_target="tpu_custom_call" | custom-call | flops 1024 | bytes 1024 | tf_op jit(solution)/shard_map/add/pallas_call | solution.py:554
  122.6 1.6 %collective-permute-start.19 = (bf16[64,4096]{1,0:T(8,128)(2,1)}, bf16[64,4096]{1,0:T(8,128)(2,1)}, u32[]{:S(2)}, u32[]{:S(2)}) collective-permute-start(bf16[64,4096]{1,0:T(8,128)(2,1)} %add.47.rest_0_), channel_id=1, source_target_pairs={{0,8},{4,12},{8,0},{12,4},{1,9},{5,13},{9,1},{13,5},{2,10},{6,14},... | collective-permute-start | bytes 1572872 | tf_op jit(solution)/shard_map/ppermute | solution.py:604
  124.2 1.0 collective-permute-start.20
  125.1 3.1 %collective-permute-done.20.came_ref = f32[1,4096]{1,0:T(1,128)} collective-permute-done((f32[1,4096]{1,0:T(1,128)}, f32[1,4096]{1,0:T(1,128)}, u32[]{:S(2)}, u32[]{:S(2)}) %collective-permute-start.20) | collective-permute-done | bytes 16416 | tf_op jit(solution)/shard_map/ppermute | solution.py:604
  128.2 1.3 gain_added.2.rest_8_.own_ref
  129.6 0.5 collective-permute-start.22
  130.1 5.3 %collective-permute-start.21 = (bf16[256,512]{1,0:T(8,128)(2,1)}, bf16[256,512]{1,0:T(8,128)(2,1)}, u32[]{:S(2)}, u32[]{:S(2)}) collective-permute-start(bf16[256,512]{1,0:T(8,128)(2,1)} %get-tuple-element.25.rest_0_.rest_7_.rest_4_), channel_id=1, source_target_pairs={{0,2},{1,3},{2,0},{3,1},{4,6},{5,7},{6,4},{7,5},{8,10},{9,11},{10,... | collective-permute-start | bytes 786440 | tf_op jit(solution)/shard_map/ppermute | solution.py:615
  135.4 7.4 %weight_grads.1 = (bf16[1024,512]{1,0:T(8,128)(2,1)}, bf16[1024,512]{1,0:T(8,128)(2,1)}, bf16[1024,512]{1,0:T(8,128)(2,1)}) custom-call(bf16[2,4,64,1024]{3,2,1,0:T(8,128)(2,1)} %stack.1.rest_11_.rest_0_, bf16[2,4,64,1024]{3,2,1,0:T(8,128)(2,1)} %collective-permute-done.9.rest_0_.rest_1_, bf16[2,4,64,1024]{3,2,1,0:T(8,128)(2,1)} %collective-permute-done.10.rest_1_.rest_2_, ...), custom_call_target="tpu_custom_call" | custom-call | flops 1024 | bytes 1024 | tf_op jit(solution)/shard_map/weight_grads/pallas_call | solution.py:470
  142.8 0.0 collective-permute-done.22.came_ref
  142.8 1.3 gain_added.3.rest_8_
  144.1 3.4 %collective-permute-start.25 = (f32[1,4096]{1,0:T(1,128)}, f32[1,4096]{1,0:T(1,128)}, u32[]{:S(2)}, u32[]{:S(2)}) collective-permute-start(f32[1,4096]{1,0:T(1,128)} %gain_added.3.rest_8_), channel_id=1, source_target_pairs={{0,3},{1,0},{2,1},{3,2},{4,7},{5,4},{6,5},{7,6},{8,11},{9,8},{10,9... | collective-permute-start | bytes 49160 | tf_op jit(solution)/shard_map/ppermute | solution.py:615
  147.5 0.6 collective-permute-start.23
  148.1 2.6 %fusion.1 = bf16[1,1,64,4096]{3,2,1,0:T(8,128)(2,1)} fusion(bf16[64,4096]{1,0:T(8,128)(2,1)} %collective-permute-done.19.rest_1_, bf16[2,64,4096]{2,1,0:T(8,128)(2,1)} %collective-permute-done.12.came_ref, bf16[2,64,4096]{2,1,0:T(8,128)(2,1)} %collective-permute-done.ins_ref.rest_0_, bf16[2,64,4096]{2,1,0:T(8,128)(2,1)} %get-tuple-element.33.rest_0_.near_ref), kind=kLoop, calls=%fused_computation.3 | loop fusion | flops 2097152 | bytes 2621440 | tf_op jit(solution)/shard_map/broadcast_in_dim | solution.py:708
  150.6 4.3 %out_weight_grads.1 = bf16[512,1024]{1,0:T(8,128)(2,1)} custom-call(bf16[2,4,64,1024]{3,2,1,0:T(8,128)(2,1)} %stack.1.rest_11_.rest_0_, bf16[2,4,64,1024]{3,2,1,0:T(8,128)(2,1)} %collective-permute-done.9.rest_0_.rest_1_, bf16[2,4,64,1024]{3,2,1,0:T(8,128)(2,1)} %collective-permute-done.10.rest_1_.rest_2_, ...), custom_call_target="tpu_custom_call" | custom-call | flops 1024 | bytes 1024 | tf_op jit(solution)/shard_map/out_weight_grads/pallas_call | solution.py:470
  155.0 1.4 add_add_fusion
  (7 shorter events, 0.0 us)
Async XLA Ops:
  2.7 4.3 %collective-permute-start = (bf16[2,64,4096]{2,1,0:T(8,128)(2,1)}, bf16[2,64,4096]{2,1,0:T(8,128)(2,1)}, u32[]{:S(2)}, u32[]{:S(2)}) collective-permute-start(bf16[2,64,4096]{2,1,0:T(8,128)(2,1)} %pick.1), channel_id=1, source_target_pairs={{0,16},{4,20},{8,24},{12,28},{16,0},{20,4},{24,8},{28,12},{1,17},{... | collective-permute-start | bytes 3145736 | tf_op jit(solution)/shard_map/ppermute | solution.py:610
  3.3 26.3 %collective-permute-start.1 = (bf16[2,64,4096]{2,1,0:T(8,128)(2,1)}, bf16[2,64,4096]{2,1,0:T(8,128)(2,1)}, u32[]{:S(2)}, u32[]{:S(2)}) collective-permute-start(bf16[2,64,4096]{2,1,0:T(8,128)(2,1)} %pick.1), channel_id=1, source_target_pairs={{0,20},{4,16},{8,28},{12,24},{16,4},{20,0},{24,12},{28,8},{1,21},{... | collective-permute-start | bytes 3145736 | tf_op jit(solution)/shard_map/ppermute | solution.py:610
  5.9 25.5 %collective-permute-start.2 = (bf16[2,64,4096]{2,1,0:T(8,128)(2,1)}, bf16[2,64,4096]{2,1,0:T(8,128)(2,1)}, u32[]{:S(2)}, u32[]{:S(2)}) collective-permute-start(bf16[2,64,4096]{2,1,0:T(8,128)(2,1)} %pick.1), channel_id=1, source_target_pairs={{0,24},{4,28},{8,16},{12,20},{16,8},{20,12},{24,0},{28,4},{1,25},{... | collective-permute-start | bytes 3145736 | tf_op jit(solution)/shard_map/ppermute | solution.py:610
  9.7 21.7 %collective-permute-start.3 = (bf16[2,64,1024]{2,1,0:T(8,128)(2,1)}, bf16[2,64,1024]{2,1,0:T(8,128)(2,1)}, u32[]{:S(2)}, u32[]{:S(2)}) collective-permute-start(bf16[2,64,1024]{2,1,0:T(8,128)(2,1)} %get-tuple-element.26), channel_id=1, source_target_pairs={{0,1},{1,2},{2,3},{3,0},{4,5},{5,6},{6,7},{7,4},{8,9},{9,10},{10,1... | collective-permute-start | bytes 786440 | tf_op jit(solution)/shard_map/ppermute | solution.py:615
  11.5 20.4 %collective-permute-start.4 = (bf16[2,64,1024]{2,1,0:T(8,128)(2,1)}, bf16[2,64,1024]{2,1,0:T(8,128)(2,1)}, u32[]{:S(2)}, u32[]{:S(2)}) collective-permute-start(bf16[2,64,1024]{2,1,0:T(8,128)(2,1)} %get-tuple-element.27), channel_id=1, source_target_pairs={{0,2},{1,3},{2,0},{3,1},{4,6},{5,7},{6,4},{7,5},{8,10},{9,11},{10,... | collective-permute-start | bytes 786440 | tf_op jit(solution)/shard_map/ppermute | solution.py:615
  14.1 17.9 %collective-permute-start.5 = (bf16[2,64,1024]{2,1,0:T(8,128)(2,1)}, bf16[2,64,1024]{2,1,0:T(8,128)(2,1)}, u32[]{:S(2)}, u32[]{:S(2)}) collective-permute-start(bf16[2,64,1024]{2,1,0:T(8,128)(2,1)} %get-tuple-element.28), channel_id=1, source_target_pairs={{0,3},{1,0},{2,1},{3,2},{4,7},{5,4},{6,5},{7,6},{8,11},{9,8},{10,9... | collective-permute-start | bytes 786440 | tf_op jit(solution)/shard_map/ppermute | solution.py:615
  34.0 18.5 %collective-permute-start.6 = (bf16[2,32,4096]{2,1,0:T(8,128)(2,1)}, bf16[2,32,4096]{2,1,0:T(8,128)(2,1)}, u32[]{:S(2)}, u32[]{:S(2)}) collective-permute-start(bf16[2,32,4096]{2,1,0:T(8,128)(2,1)} %get-tuple-element.29.rest_4_), channel_id=1, source_target_pairs={{0,4},{4,0},{8,12},{12,8},{1,5},{5,1},{9,13},{13,9},{2,6},{6,2},{1... | collective-permute-start | bytes 1572872 | tf_op jit(solution)/shard_map/ppermute | solution.py:604
  35.5 17.1 %collective-permute-start.7 = (bf16[2,32,4096]{2,1,0:T(8,128)(2,1)}, bf16[2,32,4096]{2,1,0:T(8,128)(2,1)}, u32[]{:S(2)}, u32[]{:S(2)}) collective-permute-start(bf16[2,32,4096]{2,1,0:T(8,128)(2,1)} %get-tuple-element.30), channel_id=1, source_target_pairs={{0,8},{4,12},{8,0},{12,4},{1,9},{5,13},{9,1},{13,5},{2,10},{6,14},... | collective-permute-start | bytes 1572872 | tf_op jit(solution)/shard_map/ppermute | solution.py:604
  39.1 33.4 %collective-permute-start.9 = (bf16[2,4,64,1024]{3,2,1,0:T(8,128)(2,1)}, bf16[2,4,64,1024]{3,2,1,0:T(8,128)(2,1)}, u32[]{:S(2)}, u32[]{:S(2)}) collective-permute-start(bf16[2,4,64,1024]{3,2,1,0:T(8,128)(2,1)} %stack.1.rest_11_.rest_0_), channel_id=1, source_target_pairs={{0,4},{4,0},{8,12},{12,8},{1,5},{5,1},{9,13},{13,9},{2,6},{6,2},{1... | collective-permute-start | bytes 3145736 | tf_op jit(solution)/shard_map/ppermute | solution.py:604
  39.7 32.8 %collective-permute-start.10 = (bf16[2,4,64,1024]{3,2,1,0:T(8,128)(2,1)}, bf16[2,4,64,1024]{3,2,1,0:T(8,128)(2,1)}, u32[]{:S(2)}, u32[]{:S(2)}) collective-permute-start(bf16[2,4,64,1024]{3,2,1,0:T(8,128)(2,1)} %stack.1.rest_11_.rest_0_), channel_id=1, source_target_pairs={{0,8},{4,12},{8,0},{12,4},{1,9},{5,13},{9,1},{13,5},{2,10},{6,14},... | collective-permute-start | bytes 3145736 | tf_op jit(solution)/shard_map/ppermute | solution.py:604
  40.3 12.2 %collective-permute-start.8 = (bf16[256,512]{1,0:T(8,128)(2,1)}, bf16[256,512]{1,0:T(8,128)(2,1)}, u32[]{:S(2)}, u32[]{:S(2)}) collective-permute-start(bf16[256,512]{1,0:T(8,128)(2,1)} %get-tuple-element.25.rest_0_.rest_7_.rest_4_), channel_id=1, source_target_pairs={{0,1},{1,2},{2,3},{3,0},{4,5},{5,6},{6,7},{7,4},{8,9},{9,10},{10,1... | collective-permute-start | bytes 786440 | tf_op jit(solution)/shard_map/ppermute | solution.py:615
  60.2 19.8 %collective-permute-start.11 = (bf16[256,1536]{1,0:T(8,128)(2,1)}, bf16[256,1536]{1,0:T(8,128)(2,1)}, u32[]{:S(2)}, u32[]{:S(2)}) collective-permute-start(bf16[256,1536]{1,0:T(8,128)(2,1)} %backward_attention.1.g_ref.rest_4_), channel_id=1, source_target_pairs={{0,2},{2,3},{3,1},{1,0},{4,6},{6,7},{7,5},{5,4},{8,10},{10,11},{11... | collective-permute-start | bytes 2359304 | tf_op jit(solution)/shard_map/ppermute | solution.py:623
  74.6 25.8 %collective-permute-start.13 = (bf16[2,64,4096]{2,1,0:T(8,128)(2,1)}, bf16[2,64,4096]{2,1,0:T(8,128)(2,1)}, u32[]{:S(2)}, u32[]{:S(2)}) collective-permute-start(bf16[2,64,4096]{2,1,0:T(8,128)(2,1)} %passed.1.rest_10_), channel_id=1, source_target_pairs={{0,4},{4,0},{8,12},{12,8},{1,5},{5,1},{9,13},{13,9},{2,6},{6,2},{1... | collective-permute-start | bytes 3145736 | tf_op jit(solution)/shard_map/ppermute | solution.py:604
  80.0 17.7 %collective-permute-start.16 = (bf16[256,1536]{1,0:T(8,128)(2,1)}, bf16[256,1536]{1,0:T(8,128)(2,1)}, u32[]{:S(2)}, u32[]{:S(2)}) collective-permute-start(bf16[256,1536]{1,0:T(8,128)(2,1)} %collective-permute-done.11.rest_11_.rest_5_), channel_id=1, source_target_pairs={{0,2},{2,3},{3,1},{1,0},{4,6},{6,7},{7,5},{5,4},{8,10},{10,11},{11... | collective-permute-start | bytes 2359304 | tf_op jit(solution)/shard_map/ppermute | solution.py:623
  81.6 28.9 %collective-permute-start.15 = (bf16[2,4,64,1024]{3,2,1,0:T(8,128)(2,1)}, bf16[2,4,64,1024]{3,2,1,0:T(8,128)(2,1)}, u32[]{:S(2)}, u32[]{:S(2)}) collective-permute-start(bf16[2,4,64,1024]{3,2,1,0:T(8,128)(2,1)} %collective-permute-done.9.rest_0_.rest_1_), channel_id=1, source_target_pairs={{0,8},{4,12},{8,0},{12,4},{1,9},{5,13},{9,1},{13,5},{2,10},{6,14},... | collective-permute-start | bytes 3145736 | tf_op jit(solution)/shard_map/ppermute | solution.py:604
  96.4 24.0 %collective-permute-start.12 = (bf16[2,64,4096]{2,1,0:T(8,128)(2,1)}, bf16[2,64,4096]{2,1,0:T(8,128)(2,1)}, u32[]{:S(2)}, u32[]{:S(2)}) collective-permute-start(bf16[2,64,4096]{2,1,0:T(8,128)(2,1)} %get-tuple-element.34), channel_id=1, source_target_pairs={{0,4},{4,0},{8,12},{12,8},{1,5},{5,1},{9,13},{13,9},{2,6},{6,2},{1... | collective-permute-start | bytes 3145736 | tf_op jit(solution)/shard_map/ppermute | solution.py:604
  97.7 22.8 %collective-permute-start.17 = (bf16[256,1536]{1,0:T(8,128)(2,1)}, bf16[256,1536]{1,0:T(8,128)(2,1)}, u32[]{:S(2)}, u32[]{:S(2)}) collective-permute-start(bf16[256,1536]{1,0:T(8,128)(2,1)} %collective-permute-done.16.rest_1_.rest_6_), channel_id=1, source_target_pairs={{0,2},{2,3},{3,1},{1,0},{4,6},{6,7},{7,5},{5,4},{8,10},{10,11},{11... | collective-permute-start | bytes 2359304 | tf_op jit(solution)/shard_map/ppermute | solution.py:623
  102.5 12.1 %collective-permute-start.14 = (bf16[64,4096]{1,0:T(8,128)(2,1)}, bf16[64,4096]{1,0:T(8,128)(2,1)}, u32[]{:S(2)}, u32[]{:S(2)}) collective-permute-start(bf16[64,4096]{1,0:T(8,128)(2,1)} %add.46), channel_id=1, source_target_pairs={{0,8},{4,12},{8,0},{12,4},{1,9},{5,13},{9,1},{13,5},{2,10},{6,14},... | collective-permute-start | bytes 1572872 | tf_op jit(solution)/shard_map/ppermute | solution.py:604
  104.8 15.0 %collective-permute-start.18 = (bf16[256,512]{1,0:T(8,128)(2,1)}, bf16[256,512]{1,0:T(8,128)(2,1)}, u32[]{:S(2)}, u32[]{:S(2)}) collective-permute-start(bf16[256,512]{1,0:T(8,128)(2,1)} %get-tuple-element.25.rest_0_.rest_7_.rest_4_), channel_id=1, source_target_pairs={{0,3},{1,0},{2,1},{3,2},{4,7},{5,4},{6,5},{7,6},{8,11},{9,8},{10,9... | collective-permute-start | bytes 786440 | tf_op jit(solution)/shard_map/ppermute | solution.py:615
  122.6 20.2 %collective-permute-start.19 = (bf16[64,4096]{1,0:T(8,128)(2,1)}, bf16[64,4096]{1,0:T(8,128)(2,1)}, u32[]{:S(2)}, u32[]{:S(2)}) collective-permute-start(bf16[64,4096]{1,0:T(8,128)(2,1)} %add.47.rest_0_), channel_id=1, source_target_pairs={{0,8},{4,12},{8,0},{12,4},{1,9},{5,13},{9,1},{13,5},{2,10},{6,14},... | collective-permute-start | bytes 1572872 | tf_op jit(solution)/shard_map/ppermute | solution.py:604
  124.2 4.1 %collective-permute-start.20 = (f32[1,4096]{1,0:T(1,128)}, f32[1,4096]{1,0:T(1,128)}, u32[]{:S(2)}, u32[]{:S(2)}) collective-permute-start(f32[1,4096]{1,0:T(1,128)} %get-tuple-element.37.own_ref), channel_id=1, source_target_pairs={{0,4},{4,0},{8,12},{12,8},{1,5},{5,1},{9,13},{13,9},{2,6},{6,2},{1... | collective-permute-start | bytes 49160 | tf_op jit(solution)/shard_map/ppermute | solution.py:604
  129.6 13.2 %collective-permute-start.22 = (f32[1,4096]{1,0:T(1,128)}, f32[1,4096]{1,0:T(1,128)}, u32[]{:S(2)}, u32[]{:S(2)}) collective-permute-start(f32[1,4096]{1,0:T(1,128)} %gain_added.2.rest_8_.own_ref), channel_id=1, source_target_pairs={{0,8},{4,12},{8,0},{12,4},{1,9},{5,13},{9,1},{13,5},{2,10},{6,14},... | collective-permute-start | bytes 49160 | tf_op jit(solution)/shard_map/ppermute | solution.py:604
  130.1 20.5 %collective-permute-start.21 = (bf16[256,512]{1,0:T(8,128)(2,1)}, bf16[256,512]{1,0:T(8,128)(2,1)}, u32[]{:S(2)}, u32[]{:S(2)}) collective-permute-start(bf16[256,512]{1,0:T(8,128)(2,1)} %get-tuple-element.25.rest_0_.rest_7_.rest_4_), channel_id=1, source_target_pairs={{0,2},{1,3},{2,0},{3,1},{4,6},{5,7},{6,4},{7,5},{8,10},{9,11},{10,... | collective-permute-start | bytes 786440 | tf_op jit(solution)/shard_map/ppermute | solution.py:615
  144.1 10.9 %collective-permute-start.25 = (f32[1,4096]{1,0:T(1,128)}, f32[1,4096]{1,0:T(1,128)}, u32[]{:S(2)}, u32[]{:S(2)}) collective-permute-start(f32[1,4096]{1,0:T(1,128)} %gain_added.3.rest_8_), channel_id=1, source_target_pairs={{0,3},{1,0},{2,1},{3,2},{4,7},{5,4},{6,5},{7,6},{8,11},{9,8},{10,9... | collective-permute-start | bytes 49160 | tf_op jit(solution)/shard_map/ppermute | solution.py:615
  147.5 7.5 %collective-permute-start.24 = (f32[1,4096]{1,0:T(1,128)}, f32[1,4096]{1,0:T(1,128)}, u32[]{:S(2)}, u32[]{:S(2)}) collective-permute-start(f32[1,4096]{1,0:T(1,128)} %gain_added.3.rest_8_), channel_id=1, source_target_pairs={{0,2},{1,3},{2,0},{3,1},{4,6},{5,7},{6,4},{7,5},{8,10},{9,11},{10,... | collective-permute-start | bytes 49160 | tf_op jit(solution)/shard_map/ppermute | solution.py:615
  147.5 7.5 %collective-permute-start.23 = (f32[1,4096]{1,0:T(1,128)}, f32[1,4096]{1,0:T(1,128)}, u32[]{:S(2)}, u32[]{:S(2)}) collective-permute-start(f32[1,4096]{1,0:T(1,128)} %gain_added.3.rest_8_), channel_id=1, source_target_pairs={{0,1},{1,2},{2,3},{3,0},{4,5},{5,6},{6,7},{7,4},{8,9},{9,10},{10,1... | collective-permute-start | bytes 49160 | tf_op jit(solution)/shard_map/ppermute | solution.py:615
